TPU v7x, 128 devices: a whole 4x4x4 slice. The times are simulated.
128 devices in a mesh: row: 8 (over y, core), col: 16 (over z, x).
Axes of the slice: x: 4, y: 4, z: 4, core: 2. Of those that a mesh axis runs over, the one named last changes fastest.
Arguments:
- inverse: float32 [16384, 16384], P('row', 'col'), may hold values from -6 to 6
- front_blocks: int32 [2, 32], replicated, may hold values from 0 to 63, as said below
- panels: float32 [2, 8192, 256], P(None, 'row'), may hold values from -0.0625 to 0.0625
- diag_terms: float32 [2, 256, 256], replicated, may hold values from -6 to 6
- bounds: int32 [2, 4], replicated, may hold values from 1 to 128, 256 in all within a row
Outputs:
- border: float32 [2, 8192, 256], P(None, ('row', 'col'))
- diag_block: float32 [2, 256, 256], replicated
Inputs may be any that keep to these rules, and one draw needn't show every extreme that they name: `front_blocks`: each row names 32 distinct blocks. Positions 4 r to 4 r + 3 name blocks of four different groups of 8 consecutive blocks, and every such group is named at exactly four positions, of four different r. Positions 2 o and 2 o + 1 name blocks of two different groups of 4 consecutive blocks, and every such group is named at exactly two positions, of two different o.
All inputs are finite; a program needn't handle non-finite values.
Results may differ from a plain program's by a relative error of at most 0.0001.
Values sent between devices are 32-bit elements; how exact they have to be, the bound alone decides.
No kernel may reach another device: no remote copies, remote signals or barrier semaphores. Data moves between devices by JAX's collectives and lax.ppermute only.
A program may use at most 128 MiB of HBM per device.

v0:
```python
import jax
import jax.numpy as jnp
from jax import lax
from jax.sharding import PartitionSpec as P

BS = 256


def body(inverse, front_blocks, panels, diag_terms, bounds):
    n_row = lax.axis_size("row")
    n_col = lax.axis_size("col")
    row_index = lax.axis_index("row")
    col_index = lax.axis_index("col")
    rows_loc, cols_loc = inverse.shape
    row_group = rows_loc // BS
    col_group = cols_loc // BS
    list_length = front_blocks.shape[1]
    per_owner = list_length // n_row
    sig_blocks = inverse.reshape(row_group, BS, cols_loc)
    highest = lax.Precision.HIGHEST
    borders = []
    diagonals = []
    for front_index in range(2):
        front_list = front_blocks[front_index]
        own_blocks = lax.dynamic_slice_in_dim(front_list, row_index * per_owner, per_owner)
        w_loc = panels[front_index]
        panel_width = w_loc.shape[1]
        w_pieces = w_loc.reshape(per_owner, BS, panel_width)
        targets = col_index * col_group + jnp.arange(col_group, dtype=jnp.int32)
        picker = (own_blocks[None, :] == targets[:, None]).astype(jnp.float32)
        own_piece = jnp.einsum("ki,iab->ab", picker, w_pieces, precision=highest)
        slot_rows = lax.all_gather(own_piece, "row", axis=0, tiled=True).reshape(
            n_row, BS, panel_width
        )
        owners = front_list.reshape(n_row, per_owner)
        placer = jnp.sum((owners[None, :, :] == targets[:, None, None]).astype(jnp.float32), axis=2)
        w_tilde = jnp.einsum("ks,sab->kab", placer, slot_rows, precision=highest).reshape(
            cols_loc, panel_width
        )
        dest_lists = front_list.reshape(n_row, per_owner)
        local_ids = row_index * row_group + jnp.arange(row_group, dtype=jnp.int32)
        send_pick = jnp.sum(
            (dest_lists[:, :, None] == local_ids[None, None, :]).astype(jnp.float32), axis=1
        )
        source_rows = own_blocks // row_group
        source_pick = (source_rows[:, None] == jnp.arange(n_row, dtype=jnp.int32)[None, :]).astype(
            jnp.float32
        )
        share_rows = per_owner * BS // n_col
        outgoing = jnp.einsum("dk,kab->dab", send_pick, sig_blocks, precision=highest)
        incoming = lax.all_to_all(outgoing, "row", split_axis=0, concat_axis=0, tiled=True)
        front_rows = jnp.einsum("is,sab->iab", source_pick, incoming, precision=highest).reshape(
            per_owner * BS, cols_loc
        )
        product = lax.psum_scatter(
            jnp.dot(front_rows, w_tilde, precision=highest), "col", scatter_dimension=0, tiled=True
        )
        w_mine = lax.dynamic_slice_in_dim(w_loc, col_index * share_rows, share_rows, 0)
        own_term = jnp.dot(w_mine.T, product, precision=highest)
        summed_total = lax.psum(own_term, ("row", "col"))
        node_ends = jnp.cumsum(bounds[front_index])
        columns = jnp.arange(panel_width, dtype=jnp.int32)
        node_ids = jnp.sum((columns[:, None] >= node_ends[None, :]).astype(jnp.int32), axis=1)
        same_node = (node_ids[:, None] == node_ids[None, :]).astype(jnp.float32)
        borders.append(-product)
        diagonals.append(same_node * (diag_terms[front_index] + summed_total))
    return (jnp.stack(borders), jnp.stack(diagonals))


def solution(mesh):
    placed = (P("row", "col"), P(), P(None, "row", None), P(), P())
    return jax.shard_map(
        body,
        mesh=mesh,
        in_specs=placed,
        out_specs=(P(None, ("row", "col"), None), P()),
        check_vma=False,
    )
```

profile of v0, /device:TPU:1, one launch (start us, length us, event | category | flops | bytes accessed | tf_op | source)
XLA Modules:
  0.0 502.0 jit_solution(1659487593830317478)
XLA Ops:
  7.2 0.8 slice_reduce_fusion.1
  8.0 0.1 eq.61
  8.0 0.1 copy.25
  8.1 0.1 eq.144
  8.2 0.1 copy.33
  8.3 0.1 convert_reduce_fusion.1
  8.4 16.9 %fusion.4 = f32[8,256,1024]{2,0,1:T(8,128)S(1)} fusion(f32[8,256,1024]{2,1,0:T(8,128)} %bitcast.83, f32[8,8]{1,0:T(8,128)S(1)} %get-tuple-element.9), kind=kOutput, calls=%fused_computation.4 | convolution fusion | flops 201326592 | bytes 16777472 | tf_op jit(solution)/shard_map/dk,kab->dab/dot_general | solution.py:50
  25.3 8.1 %copy.35 = f32[8,256,1024]{2,1,0:T(8,128)} copy(f32[8,256,1024]{2,0,1:T(8,128)S(1)} %fusion.4) | data formatting | bytes 16777216 | tf_op jit(solution)/shard_map/dk,kab->dab/dot_general | solution.py:50
  33.4 6.3 %all-to-all-start.1 = ((f32[8,256,1024]{2,1,0:T(8,128)}), f32[8,256,1024]{2,1,0:T(8,128)}, u32[]{:S(2)}, u32[]{:S(2)}) async-start(f32[8,256,1024]{2,1,0:T(8,128)} %copy.35), calls=%async_computation.2 | async-start | bytes 16777216 | tf_op jit(solution)/shard_map/all_to_all | solution.py:51
  39.6 0.0 all-gather.5.cloned.1.call-start
  39.7 0.1 and_select_fusion
  39.7 0.1 and_select_fusion.1
  39.8 0.1 convert_reduce_fusion.7
  39.9 1.7 fusion.44
  41.6 2.3 fusion.12
  43.9 0.7 copy.63
  44.7 0.0 all-gather.5.cloned.1.call-update
  44.7 17.4 %fusion.6 = f32[8,256,1024]{2,0,1:T(8,128)S(1)} fusion(f32[8,256,1024]{2,1,0:T(8,128)} %bitcast.84, f32[8,8]{1,0:T(8,128)S(1)} %get-tuple-element.8), kind=kOutput, calls=%fused_computation.6 | convolution fusion | flops 201326592 | bytes 16777472 | tf_op jit(solution)/shard_map/dk,kab->dab/dot_general | solution.py:50
  62.0 8.1 %copy.27 = f32[8,256,1024]{2,1,0:T(8,128)} copy(f32[8,256,1024]{2,0,1:T(8,128)S(1)} %fusion.6) | data formatting | bytes 16777216 | tf_op jit(solution)/shard_map/dk,kab->dab/dot_general | solution.py:50
  70.1 71.8 %all-to-all-done.1 = f32[8,256,1024]{2,1,0:T(8,128)} async-done(((f32[8,256,1024]{2,1,0:T(8,128)}), f32[8,256,1024]{2,1,0:T(8,128)}, u32[]{:S(2)}, u32[]{:S(2)}) %all-to-all-start.1) | async-done | bytes 8388640 | tf_op jit(solution)/shard_map/all_to_all | solution.py:51
  141.9 5.8 %all-to-all-start = ((f32[8,256,1024]{2,1,0:T(8,128)}), f32[8,256,1024]{2,1,0:T(8,128)}, u32[]{:S(2)}, u32[]{:S(2)}) async-start(f32[8,256,1024]{2,1,0:T(8,128)} %copy.27), calls=%async_computation | async-start | bytes 16777216 | tf_op jit(solution)/shard_map/all_to_all | solution.py:51
  147.7 0.0 all-gather.3.cloned.1.call-start
  147.7 2.3 fusion.14
  150.1 0.7 copy.64
  150.8 0.0 all-gather.3.cloned.1.call-update
  150.8 0.4 reduce-scatter.5.cloned.1.call-start
  151.3 0.1 convert_reduce_fusion.3
  151.4 0.0 all-gather.5.cloned.1.call-done
  151.4 4.4 fusion.8
  155.8 0.2 copy.40
  156.1 12.1 %fusion = f32[4,256,1024]{2,0,1:T(4,128)S(1)} fusion(f32[8,256,1024]{2,1,0:T(8,128)} %all-to-all-done.1, s32[4]{0:T(128)S(1)} %get-tuple-element.14), kind=kOutput, calls=%fused_computation | convolution fusion | flops 100663328 | bytes 12582928 | tf_op jit(solution)/shard_map/is,sab->iab/dot_general | solution.py:52
  168.1 2.4 copy.37
  170.6 4.4 fusion.46
  175.0 0.0 reduce-scatter.5.cloned.1.call-update
  175.0 0.0 reduce-scatter.3.cloned.1.call-start
  175.0 14.1 %all-gather.3.cloned.1.call-done = f32[2048,256]{1,0:T(8,128)} async-done(((f32[256,256]{1,0:T(8,128)}), f32[2048,256]{1,0:T(8,128)}) %all-gather.3.cloned.1.call-update) | async-done | bytes 2097168 | tf_op jit(solution)/shard_map/all_gather | solution.py:32
  189.1 4.4 fusion.10
  193.6 0.2 copy.32
  193.8 56.2 %all-to-all-done = f32[8,256,1024]{2,1,0:T(8,128)} async-done(((f32[8,256,1024]{2,1,0:T(8,128)}), f32[8,256,1024]{2,1,0:T(8,128)}, u32[]{:S(2)}, u32[]{:S(2)}) %all-to-all-start) | async-done | bytes 8388640 | tf_op jit(solution)/shard_map/all_to_all | solution.py:51
  250.0 12.2 %fusion.2 = f32[4,256,1024]{2,0,1:T(4,128)S(1)} fusion(f32[8,256,1024]{2,1,0:T(8,128)} %all-to-all-done, s32[4]{0:T(128)S(1)} %get-tuple-element.12), kind=kOutput, calls=%fused_computation.2 | convolution fusion | flops 100663328 | bytes 12582928 | tf_op jit(solution)/shard_map/is,sab->iab/dot_general | solution.py:52
  262.2 0.0 copy-start
  262.2 2.4 copy.29
  264.6 4.4 fusion.45
  269.0 0.0 reduce-scatter.3.cloned.1.call-update
  269.1 0.0 all-reduce.3.cloned.1.call-start
  269.1 0.0 copy-done
  269.1 0.2 reduce-window.17
  269.3 0.2 reduce-window.16
  269.5 0.1 convert_reduce_fusion.4
  269.6 0.0 reduce-scatter.5.cloned.1.call-done
  269.6 2.0 fusion.20
  271.6 69.7 %reduce-scatter.3.cloned.1.call-done = f32[64,256]{1,0:T(8,128)} async-done(((f32[1024,256]{1,0:T(8,128)}), f32[64,256]{1,0:T(8,128)}) %reduce-scatter.3.cloned.1.call-update) | async-done | bytes 65552 | tf_op jit(solution)/shard_map/reduce_scatter | solution.py:55
  341.3 2.0 fusion.22
  343.3 0.0 all-reduce.3.cloned.1.call-update
  343.3 0.8 negate_bitcast_fusion
  344.2 0.8 negate_bitcast_fusion.1
  345.0 0.7 pad_maximum_fusion.1
  345.7 147.4 %all-reduce.3.cloned.1.call-done = (f32[256,256]{1,0:T(8,128)}, f32[256,256]{1,0:T(8,128)}) async-done(((f32[256,256]{1,0:T(8,128)}, f32[256,256]{1,0:T(8,128)}), (f32[256,256]{1,0:T(8,128)}, f32[256,256]{1,0:T(8,128)})) %all-reduce.3.cloned.1.call-update) | async-done | bytes 524304 | tf_op jit(solution)/shard_map/psum | solution.py:60
  493.1 1.3 fusion.19
  494.4 0.8 pad_maximum_fusion
  (3 shorter events, 0.0 us)
Async XLA Ops:
  33.4 108.6 %all-to-all-start.1 = ((f32[8,256,1024]{2,1,0:T(8,128)}), f32[8,256,1024]{2,1,0:T(8,128)}, u32[]{:S(2)}, u32[]{:S(2)}) async-start(f32[8,256,1024]{2,1,0:T(8,128)} %copy.35), calls=%async_computation.2 | async-start | bytes 16777216 | tf_op jit(solution)/shard_map/all_to_all | solution.py:51
  39.6 111.8 %all-gather.5.cloned.1.call-start = ((), (), s32[]{:S(2)}) async-start(), calls=%async_computation.6 | async-start | bytes 2359296 | tf_op jit(solution)/shard_map/all_gather | solution.py:32
  141.9 108.1 %all-to-all-start = ((f32[8,256,1024]{2,1,0:T(8,128)}), f32[8,256,1024]{2,1,0:T(8,128)}, u32[]{:S(2)}, u32[]{:S(2)}) async-start(f32[8,256,1024]{2,1,0:T(8,128)} %copy.27), calls=%async_computation | async-start | bytes 16777216 | tf_op jit(solution)/shard_map/all_to_all | solution.py:51
  147.7 41.4 %all-gather.3.cloned.1.call-start = ((), (), s32[]{:S(2)}) async-start(), calls=%async_computation.4 | async-start | bytes 2359296 | tf_op jit(solution)/shard_map/all_gather | solution.py:32
  150.8 118.8 %reduce-scatter.5.cloned.1.call-start = ((), (), s32[]{:S(2)}) async-start(), calls=%async_computation.7 | async-start | bytes 1114112 | tf_op jit(solution)/shard_map/reduce_scatter | solution.py:55
  175.0 166.3 %reduce-scatter.3.cloned.1.call-start = ((), (), s32[]{:S(2)}) async-start(), calls=%async_computation.5 | async-start | bytes 1114112 | tf_op jit(solution)/shard_map/reduce_scatter | solution.py:55
  262.2 6.9 %copy-start = (s32[2,4]{1,0:T(2,128)S(1)}, s32[2,4]{1,0:T(2,128)}, u32[]{:S(2)}) copy-start(s32[2,4]{1,0:T(2,128)} %param.9) | copy-start | bytes 100
  269.1 224.0 %all-reduce.3.cloned.1.call-start = ((), (), s32[]{:S(2)}) async-start(), calls=%async_computation.8 | async-start | bytes 1048576 | tf_op jit(solution)/shard_map/psum | solution.py:60
Sparse Core Ops, SparseCore 0:
  44.8 37.1 all-gather.4
  151.0 38.1 all-gather.2
  192.4 70.4 reduce-scatter.4
  269.2 72.0 reduce-scatter.2
  346.7 146.3 all-reduce.2
where the time goes:
time: 508 us; the launch traced here: 502 us
  waiting for transfers between devices  359 us (71%)
  matrix products  84.8 us (17%)
  local copies, waits for them, and re-layouts  25.6 us (5%)
  between operations  14.2 us (3%)
  starting transfers between devices  12.6 us (2%)
  other arithmetic  5.37 us (1%)
    psum x1, waiting for transfers between devices, body(): summed_total = lax.psum(own_term, ('row', 'col'))  147 us
    all_to_all x2, waiting for transfers between devices, body(): lax.all_to_all(outgoing, 'row', split_axis=0, concat_axis=0, tiled=True)  128 us
    reduce_scatter x2, waiting for transfers between devices, body(): lax.psum_scatter(jnp.dot(front_rows, w_tilde, precision=highest), 'col',...  69.8 us
    dot_general x2, matrix products, body(): jnp.einsum('dk,kab->dab', send_pick, sig_blocks, precision=highest)  34.3 us
    dot_general x2, matrix products, body(): jnp.einsum('is,sab->iab', source_pick, incoming, precision=highest)  24.2 us
    dot_general x2, local copies, waits for them, and re-layouts, body(): jnp.einsum('dk,kab->dab', send_pick, sig_blocks, precision=highest)  16.1 us
    all_gather x2, waiting for transfers between devices, body(): lax.all_gather(own_piece, 'row', axis=0, tiled=True)  14.1 us
    all_to_all x2, starting transfers between devices, body(): lax.all_to_all(outgoing, 'row', split_axis=0, concat_axis=0, tiled=True)  12 us
  transfers between devices with their start and end apart: 7, of which 5 were waited for; matrix products, arithmetic and copies ran while one was open for 17% of the time, Pallas kernels for 0%

commit v1 on v0

v1 whole, which is shorter than its diff:
```python
import jax
import jax.numpy as jnp
from jax import lax
from jax.experimental import pallas as pl
from jax.experimental.pallas import tpu as pltpu
from jax.sharding import Mesh, PartitionSpec as P

F32 = jnp.float32
BF16 = jnp.bfloat16
ROW = ("y", "core")
COL = ("z", "x")
ALL = ("y", "core", "z", "x")
VMEM = pl.BlockSpec(memory_space=pltpu.VMEM)
SMEM = pl.BlockSpec(memory_space=pltpu.SMEM)
ANY = pl.BlockSpec(memory_space=pl.ANY)
PARAMS = pltpu.CompilerParams(vmem_limit_bytes=40 * 1024 * 1024)


def sds(shape, dtype=F32):
    return jax.ShapeDtypeStruct(shape, dtype)


def split(v):
    hi = v.astype(BF16)
    lo = (v - hi.astype(F32)).astype(BF16)
    return hi, lo


def dot3(a, b, dims):
    (ah, al), (bh, bl) = a, b
    mm = lambda p, q: lax.dot_general(p, q, (dims, ((), ())), preferred_element_type=F32)
    return mm(ah, bh) + (mm(ah, bl) + mm(al, bh))


def pack_kernel(fb, w, out, tab):
    r = lax.axis_index("y") * 2 + lax.axis_index("core")
    z, x = lax.axis_index("z"), lax.axis_index("x")
    c = z * 4 + x
    share = x * 64 + z * 16
    for f in range(2):
        own = [fb[f, 4 * r + i] for i in range(4)]
        piece = jnp.int32(0)
        for i in range(1, 4):
            piece = jnp.where((own[i] >> 2) == c, i, piece)
        for d in range(8):
            at = pl.multiple_of(piece * 256 + d * 32, 32)
            out[d, 32 * f : 32 * f + 32] = w[f, pl.ds(at, 32), :]
            named = jnp.int32(0)
            for i in range(1, 4):
                named = jnp.where((own[i] >> 3) == d, i, named)
            at = pl.multiple_of(named * 256 + share, 16)
            out[d, 64 + 16 * f : 80 + 16 * f] = w[f, pl.ds(at, 16), :]
    for k in range(32):
        tab[k] = 0
    for f in range(2):
        rows = jnp.int32(0)
        cols = jnp.int32(0)
        for p in range(32):
            b = fb[f, p]
            tab[16 * f + rows] = p
            rows = rows + ((b >> 3) == r).astype(jnp.int32)
            tab[16 * f + 8 + cols] = p
            cols = cols + ((b >> 2) == c).astype(jnp.int32)


def pick_kernel(tab, inc, slices, mine):
    for f in range(2):
        for t in range(2):
            p = tab[16 * f + 8 + t]
            slices[2 * f + t] = inc[p >> 2, 32 * f : 32 * f + 32, :]
        for s in range(4):
            p = tab[16 * f + s]
            mine[4 * f + s] = inc[p >> 2, 64 + 16 * f : 80 + 16 * f, :]


def product_kernel(fb, tab, inverse, w, out, tiles, sems):
    copies = []
    for f in range(2):
        for s in range(4):
            for t in range(2):
                k = (4 * f + s) * 2 + t
                rb = fb[f, tab[16 * f + s]] & 7
                cb = fb[f, tab[16 * f + 8 + t]] & 3
                src = inverse.at[
                    pl.ds(pl.multiple_of(rb * 256, 256), 256),
                    pl.ds(pl.multiple_of(cb * 256, 256), 256),
                ]
                copy = pltpu.make_async_copy(src, tiles.at[k], sems.at[k])
                copy.start()
                copies.append(copy)
    for f in range(2):
        ws = [split(w[:, 2 * f + t].reshape(256, 256)) for t in range(2)]
        for s in range(4):
            total = None
            for t in range(2):
                k = (4 * f + s) * 2 + t
                copies[k].wait()
                part = dot3(split(tiles[k]), ws[t], ((1,), (0,)))
                total = part if total is None else total + part
            for d in range(16):
                at = 64 * (d % 4) + 16 * (d // 4)
                out[d, 4 * f + s] = total[at : at + 16, :]


def same_node(bounds, f):
    a = lax.broadcasted_iota(jnp.int32, (256, 256), 0)
    b = lax.broadcasted_iota(jnp.int32, (256, 256), 1)
    ia = jnp.zeros((256, 256), jnp.int32)
    ib = jnp.zeros((256, 256), jnp.int32)
    end = jnp.int32(0)
    for k in range(4):
        end = end + bounds[f, k]
        ia = ia + (a >= end).astype(jnp.int32)
        ib = ib + (b >= end).astype(jnp.int32)
    return ia == ib


def reduce_kernel(tab, bounds, parts, mine, route, share):
    route[...] = jnp.zeros(route.shape, F32)
    for f in range(2):
        rows = []
        for s in range(4):
            v = parts[0, 4 * f + s]
            for d in range(1, 16):
                v = v + parts[d, 4 * f + s]
            rows.append(v)
            route[tab[16 * f + s] >> 2, f] = -v
        left = mine[4 * f : 4 * f + 4].reshape(64, 256)
        right = jnp.concatenate(rows, axis=0)
        full = dot3(split(left), split(right), ((0,), (0,)))
        full = jnp.where(same_node(bounds, f), full, 0.0)
        packed = full[:, :128] + full[:, 128:]
        share[64 * f : 64 * f + 64] = packed.reshape(64, 4, 128)


def place_kernel(fb, inc, out):
    r = lax.axis_index("y") * 2 + lax.axis_index("core")
    for f in range(2):
        for i in range(4):
            out[i, f] = inc[fb[f, 4 * r + i] >> 3, f]


def spread_kernel(inc, out):
    total = jnp.sum(inc[...], axis=0)
    out[...] = jnp.broadcast_to(total[None], out.shape)


def finish_kernel(bounds, packed, terms, out):
    for f in range(2):
        v = packed[64 * f : 64 * f + 64].reshape(256, 128)
        full = terms[f] + jnp.concatenate([v, v], axis=1)
        out[f] = jnp.where(same_node(bounds, f), full, 0.0)


def call(kernel, ins, out_shape, out_specs=None, scratch=()):
    if out_specs is None:
        out_specs = jax.tree.map(lambda _: VMEM, out_shape)
    return pl.pallas_call(
        kernel,
        in_specs=ins,
        out_shape=out_shape,
        out_specs=out_specs,
        scratch_shapes=scratch,
        compiler_params=PARAMS,
    )


def body(inverse, fb, panels, terms, bounds):
    a2a = lambda v, axes: lax.all_to_all(v, axes, 0, 0, tiled=True)
    outgoing, tab = call(
        pack_kernel, [SMEM, VMEM], (sds((8, 96, 256)), sds((32,), jnp.int32)), (VMEM, SMEM)
    )(fb, panels)
    incoming = a2a(outgoing, ROW)
    slices, mine = call(
        pick_kernel, [SMEM, VMEM], (sds((4, 32, 256)), sds((8, 16, 256)))
    )(tab, incoming)
    w = lax.all_gather(slices, ROW, axis=0, tiled=False)
    parts = call(
        product_kernel,
        [SMEM, SMEM, ANY, VMEM],
        sds((16, 8, 16, 256)),
        scratch=[pltpu.VMEM((16, 256, 256), F32), pltpu.SemaphoreType.DMA((16,))],
    )(fb, tab, inverse, w.reshape(8, 4, 32, 256))
    parts = a2a(parts, COL)
    route, share = call(
        reduce_kernel,
        [SMEM, SMEM, VMEM, VMEM],
        (sds((8, 2, 16, 256)), sds((128, 4, 128))),
    )(tab, bounds, parts, mine)
    share = a2a(share, ALL)
    route = a2a(route, ROW)
    route = call(place_kernel, [SMEM, VMEM], sds((4, 2, 16, 256)))(fb, route)
    border = a2a(route, "z").transpose(1, 0, 2, 3).reshape(2, 64, 256)
    share = call(spread_kernel, [VMEM], sds((128, 4, 128)))(share)
    packed = a2a(share, ALL)
    diag = call(finish_kernel, [SMEM, VMEM, VMEM], sds((2, 256, 256)))(bounds, packed, terms)
    return border, diag


def solution(mesh):
    grid = Mesh(mesh.devices.reshape(4, 2, 4, 4), ALL)
    placed = (P(ROW, COL), P(), P(None, ROW, None), P(), P())
    return jax.shard_map(
        body,
        mesh=grid,
        in_specs=placed,
        out_specs=(P(None, ALL, None), P()),
        check_vma=False,
    )
```

time: 508 us -> 162 us (0.32); the launches traced: 502 us -> 161 us
  waiting for transfers between devices: 359 us -> 49.9 us
  matrix products: 84.8 us -> 0 us
  blocking collectives: 0 us -> 62.9 us
  local copies, waits for them, and re-layouts: 25.6 us -> 7.55 us
  Pallas kernels: 0 us -> 14.1 us
  other arithmetic: 5.37 us -> 0 us
    psum x1 -> x0, waiting for transfers between devices: 147 us -> none  [body(): summed_total = lax.psum(own_term, ('row', 'col'))]
    all_to_all x2 -> x3, waiting for transfers between devices: 128 us -> 25.2 us  [body(): a2a = lambda v, axes: lax.all_to_all(v, axes, 0, 0, tiled=True)]
    dot_general x12 -> x0, matrix products: 84.8 us -> none  [the longest x2 34.3 us: body(): jnp.einsum('dk,kab->dab', send_pick, sig_blocks, precision=highest)]
    reduce_scatter x2 -> x0, waiting for transfers between devices: 69.8 us -> none  [body(): lax.psum_scatter(jnp.dot(front_rows, w_tilde, precision=highest), 'col',...]
    all_to_all x0 -> x3, blocking collectives: none -> 62.9 us  [body(): a2a = lambda v, axes: lax.all_to_all(v, axes, 0, 0, tiled=True)]
    dot_general x8 -> x0, local copies, waits for them, and re-layouts: 22.9 us -> none  [the longest x2 16.1 us: body(): jnp.einsum('dk,kab->dab', send_pick, sig_blocks, precision=highest)]
    pallas_call x0 -> x7, Pallas kernels: none -> 14.1 us  [the longest x1 6.03 us: body(): call(product_kernel, [SMEM, SMEM, ANY, VMEM], sds((16, 8, 16, 256)), scra...]
    all_gather x2 -> x1, waiting for transfers between devices: 14.1 us -> 24.7 us  [body(): w = lax.all_gather(slices, ROW, axis=0, tiled=False)]
  transfers between devices with their start and end apart: 7 -> 4, of which waited for: 5 -> 4; matrix products, arithmetic and copies ran while one was open for 17% -> 0% of each run, Pallas kernels for 0% -> 1%
where the time goes in v1:
time: 162 us; the launch traced here: 161 us
  blocking collectives  62.9 us (39%)
  waiting for transfers between devices  49.9 us (31%)
  Pallas kernels  14.1 us (9%)
  between operations  14.1 us (9%)
  starting transfers between devices  12.9 us (8%)
  local copies, waits for them, and re-layouts  7.55 us (5%)
    all_to_all x3, blocking collectives, body(): a2a = lambda v, axes: lax.all_to_all(v, axes, 0, 0, tiled=True)  62.9 us
    all_to_all x3, waiting for transfers between devices, body(): a2a = lambda v, axes: lax.all_to_all(v, axes, 0, 0, tiled=True)  25.2 us
    all_gather x1, waiting for transfers between devices, body(): w = lax.all_gather(slices, ROW, axis=0, tiled=False)  24.7 us
    all_to_all x3, starting transfers between devices, body(): a2a = lambda v, axes: lax.all_to_all(v, axes, 0, 0, tiled=True)  12.8 us
    unnamed x14, local copies, waits for them, and re-layouts  6.88 us
    pallas_call x1, Pallas kernels, body(): call(product_kernel, [SMEM, SMEM, ANY, VMEM], sds((16, 8, 16, 256)), scra...  6.03 us
  transfers between devices with their start and end apart: 4, of which 4 were waited for; matrix products, arithmetic and copies ran while one was open for 0% of the time, Pallas kernels for 1%

profile of v1, /device:TPU:1, one launch (start us, length us, event | category | flops | bytes accessed | tf_op | source)
XLA Modules:
  0.0 161.5 jit_solution(234468432003679066)
XLA Ops:
  7.2 0.0 all-gather.3.cloned.1.call-start
  7.2 0.0 copy-start.1
  7.2 1.6 copy-done.1
  8.8 0.0 copy-start.4
  8.8 0.7 copy-done.4
  9.5 0.0 copy-start.5
  9.5 1.5 shard_map.68
  11.0 18.0 %all_to_all.30.inc = f32[8,96,256]{2,1,0:T(8,128)S(1)} all-to-all(f32[8,96,256]{2,1,0:T(8,128)S(1)} %get-tuple-element.9), channel_id=1, replica_groups=mesh['y'=4,'core'=2,'z'=4,'x'=4] {'y','core'}, dimensions={0} | all-to-all | bytes 1572864 | tf_op jit(solution)/shard_map/all_to_all | solution.py:169
  29.0 1.2 shard_map.69
  30.2 0.0 all-gather.3.cloned.1.call-update
  30.2 24.7 %all-gather.3.cloned.1.call-done = f32[32,32,256]{2,1,0:T(8,128)} async-done(((f32[4,32,256]{2,1,0:T(8,128)}), f32[32,32,256]{2,1,0:T(8,128)}) %all-gather.3.cloned.1.call-update) | async-done | bytes 1048592 | tf_op jit(solution)/shard_map/all_gather | solution.py:177
  54.9 0.0 copy-done.5
  54.9 0.0 copy-start
  54.9 3.4 %copy-done = f32[2048,1024]{1,0:T(8,128)S(1)} copy-done((f32[2048,1024]{1,0:T(8,128)S(1)}, f32[2048,1024]{1,0:T(8,128)}, u32[]{:S(2)}) %copy-start) | copy-done | bytes 8388632
  58.3 0.0 copy-start.2
  58.3 1.2 copy-done.2
  59.5 6.0 %shard_map.70 = f32[16,8,16,256]{3,2,1,0:T(8,128)S(1)} custom-call(s32[2,32]{1,0:T(2,128)S(1)} %copy-done.5, s32[32]{0:T(128)S(1)} %get-tuple-element.8.tab, f32[2048,1024]{1,0:T(8,128)S(1)} %copy-done, f32[8,4,32,256]{3,2,1,0:T(8,128)S(1)} %bitcast.3), custom_call_target="tpu_custom_call" | custom-call | tf_op jit(solution)/shard_map/pallas_call | solution.py:178
  65.6 0.0 copy-start.6
  65.6 34.2 %all_to_all.31.parts = f32[16,8,16,256]{3,2,1,0:T(8,128)S(1)} all-to-all(f32[16,8,16,256]{3,2,1,0:T(8,128)S(1)} %shard_map.70), channel_id=1, replica_groups=mesh['y'=4,'core'=2,'z'=4,'x'=4] {'z','x'}, dimensions={0} | all-to-all | bytes 4194304 | tf_op jit(solution)/shard_map/all_to_all | solution.py:169
  99.7 0.0 copy-done.6
  99.7 0.0 copy-start.3
  99.7 1.7 %shard_map.71 = (f32[8,2,16,256]{3,2,1,0:T(8,128)S(1)}, f32[128,4,128]{2,1,0:T(4,128)}) custom-call(s32[32]{0:T(128)S(1)} %get-tuple-element.8.tab, s32[2,4]{1,0:T(2,128)S(1)} %copy-done.6, f32[16,8,16,256]{3,2,1,0:T(8,128)S(1)} %all_to_all.31.parts, f32[8,16,256]{2,1,0:T(8,128)S(1)} %get-tuple-element.11.mine), custom_call_target="tpu_custom_call" | custom-call | tf_op jit(solution)/shard_map/pallas_call | solution.py:185
  101.5 10.8 %all_to_all.32.inc = f32[8,2,16,256]{3,2,1,0:T(8,128)S(1)} all-to-all(f32[8,2,16,256]{3,2,1,0:T(8,128)S(1)} %get-tuple-element.12), channel_id=1, replica_groups=mesh['y'=4,'core'=2,'z'=4,'x'=4] {'y','core'}, dimensions={0} | all-to-all | bytes 524288 | tf_op jit(solution)/shard_map/all_to_all | solution.py:169
  112.3 4.4 %all-to-all-start.4 = ((f32[128,4,128]{2,1,0:T(4,128)}), f32[128,4,128]{2,1,0:T(4,128)S(1)}, u32[]{:S(2)}, u32[]{:S(2)}) async-start(f32[128,4,128]{2,1,0:T(4,128)} %get-tuple-element.13), calls=%async_computation.4 | async-start | bytes 524288 | tf_op jit(solution)/shard_map/all_to_all | solution.py:169
  116.7 1.2 shard_map.72
  118.0 10.4 %all-to-all-done.4.inc = f32[128,4,128]{2,1,0:T(4,128)S(1)} async-done(((f32[128,4,128]{2,1,0:T(4,128)}), f32[128,4,128]{2,1,0:T(4,128)S(1)}, u32[]{:S(2)}, u32[]{:S(2)}) %all-to-all-start.4) | async-done | bytes 262176 | tf_op jit(solution)/shard_map/all_to_all | solution.py:169
  128.3 3.3 %all-to-all-start.3 = ((f32[4,2,16,256]{3,2,1,0:T(8,128)}), f32[4,2,16,256]{3,2,1,0:T(8,128)S(1)}, u32[]{:S(2)}, u32[]{:S(2)}) async-start(f32[4,2,16,256]{3,2,1,0:T(8,128)} %shard_map.72), calls=%async_computation.3 | async-start | bytes 262144 | tf_op jit(solution)/shard_map/all_to_all | solution.py:169
  131.7 0.9 shard_map.73
  132.5 3.9 %all-to-all-done.3 = f32[4,2,16,256]{3,2,1,0:T(8,128)S(1)} async-done(((f32[4,2,16,256]{3,2,1,0:T(8,128)}), f32[4,2,16,256]{3,2,1,0:T(8,128)S(1)}, u32[]{:S(2)}, u32[]{:S(2)}) %all-to-all-start.3) | async-done | bytes 131104 | tf_op jit(solution)/shard_map/all_to_all | solution.py:169
  136.4 5.0 %all-to-all-start.5 = ((f32[128,4,128]{2,1,0:T(4,128)}), f32[128,4,128]{2,1,0:T(4,128)S(1)}, u32[]{:S(2)}, u32[]{:S(2)}) async-start(f32[128,4,128]{2,1,0:T(4,128)} %shard_map.73), calls=%async_computation.5 | async-start | bytes 524288 | tf_op jit(solution)/shard_map/all_to_all | solution.py:169
  141.5 0.7 copy.8
  142.2 10.9 %all-to-all-done.5.packed = f32[128,4,128]{2,1,0:T(4,128)S(1)} async-done(((f32[128,4,128]{2,1,0:T(4,128)}), f32[128,4,128]{2,1,0:T(4,128)S(1)}, u32[]{:S(2)}, u32[]{:S(2)}) %all-to-all-start.5) | async-done | bytes 262176 | tf_op jit(solution)/shard_map/all_to_all | solution.py:169
  153.1 0.0 copy-done.3
  153.1 1.5 shard_map.74
Async XLA Ops:
  7.2 47.8 %all-gather.3.cloned.1.call-start = ((), (), s32[]{:S(2)}) async-start(), calls=%async_computation.6 | async-start | bytes 1179648 | tf_op jit(solution)/shard_map/all_gather | solution.py:177
  7.2 1.6 copy-start.1
  8.8 0.7 copy-start.4
  9.5 45.4 %copy-start.5 = (s32[2,32]{1,0:T(2,128)S(1)}, s32[2,32]{1,0:T(2,128)}, u32[]{:S(2)}) copy-start(s32[2,32]{1,0:T(2,128)} %fb.5) | copy-start | bytes 772
  54.9 3.4 %copy-start = (f32[2048,1024]{1,0:T(8,128)S(1)}, f32[2048,1024]{1,0:T(8,128)}, u32[]{:S(2)}) copy-start(f32[2048,1024]{1,0:T(8,128)} %inverse.1) | copy-start | bytes 25165828
  58.3 1.2 copy-start.2
  65.6 34.2 %copy-start.6 = (s32[2,4]{1,0:T(2,128)S(1)}, s32[2,4]{1,0:T(2,128)}, u32[]{:S(2)}) copy-start(s32[2,4]{1,0:T(2,128)} %bounds.3) | copy-start | bytes 100
  99.7 53.4 %copy-start.3 = (f32[2,256,256]{2,1,0:T(8,128)S(1)}, f32[2,256,256]{2,1,0:T(8,128)}, u32[]{:S(2)}) copy-start(f32[2,256,256]{2,1,0:T(8,128)} %terms.1) | copy-start | bytes 1572868
  112.3 16.1 %all-to-all-start.4 = ((f32[128,4,128]{2,1,0:T(4,128)}), f32[128,4,128]{2,1,0:T(4,128)S(1)}, u32[]{:S(2)}, u32[]{:S(2)}) async-start(f32[128,4,128]{2,1,0:T(4,128)} %get-tuple-element.13), calls=%async_computation.4 | async-start | bytes 524288 | tf_op jit(solution)/shard_map/all_to_all | solution.py:169
  128.3 8.1 %all-to-all-start.3 = ((f32[4,2,16,256]{3,2,1,0:T(8,128)}), f32[4,2,16,256]{3,2,1,0:T(8,128)S(1)}, u32[]{:S(2)}, u32[]{:S(2)}) async-start(f32[4,2,16,256]{3,2,1,0:T(8,128)} %shard_map.72), calls=%async_computation.3 | async-start | bytes 262144 | tf_op jit(solution)/shard_map/all_to_all | solution.py:169
  136.4 16.7 %all-to-all-start.5 = ((f32[128,4,128]{2,1,0:T(4,128)}), f32[128,4,128]{2,1,0:T(4,128)S(1)}, u32[]{:S(2)}, u32[]{:S(2)}) async-start(f32[128,4,128]{2,1,0:T(4,128)} %shard_map.73), calls=%async_computation.5 | async-start | bytes 524288 | tf_op jit(solution)/shard_map/all_to_all | solution.py:169
Sparse Core Ops, SparseCore 0:
  30.4 24.5 all-gather.2

commit v2 on v1

v2 whole, which is shorter than its diff:
```python
import jax
import jax.numpy as jnp
from jax import lax
from jax.experimental import pallas as pl
from jax.experimental.pallas import tpu as pltpu
from jax.sharding import Mesh, PartitionSpec as P

F32 = jnp.float32
BF16 = jnp.bfloat16
ROW = ("y", "core")
COL = ("z", "x")
ALL = ("y", "core", "z", "x")
VMEM = pl.BlockSpec(memory_space=pltpu.VMEM)
SMEM = pl.BlockSpec(memory_space=pltpu.SMEM)
ANY = pl.BlockSpec(memory_space=pl.ANY)
HBM = pl.BlockSpec(memory_space=pltpu.HBM)
MIB = 1024 * 1024


def sds(shape, dtype=F32):
    return jax.ShapeDtypeStruct(shape, dtype)


def split(v):
    hi = v.astype(BF16)
    lo = (v - hi.astype(F32)).astype(BF16)
    return hi, lo


def dot3(a, b, dims):
    (ah, al), (bh, bl) = a, b
    mm = lambda p, q: lax.dot_general(p, q, (dims, ((), ())), preferred_element_type=F32)
    return mm(ah, bh) + (mm(ah, bl) + mm(al, bh))


def pack_kernel(fb, w, out, tab):
    r = lax.axis_index("y") * 2 + lax.axis_index("core")
    z, x = lax.axis_index("z"), lax.axis_index("x")
    c = z * 4 + x
    share = x * 64 + z * 16
    for f in range(2):
        own = [fb[f, 4 * r + i] for i in range(4)]
        piece = jnp.int32(0)
        for i in range(1, 4):
            piece = jnp.where((own[i] >> 2) == c, i, piece)
        for d in range(8):
            at = pl.multiple_of(piece * 256 + (d % 2 * 4 + d // 2) * 32, 32)
            out[d, 32 * f : 32 * f + 32] = w[f, pl.ds(at, 32), :]
            named = jnp.int32(0)
            for i in range(1, 4):
                named = jnp.where((own[i] >> 3) == d, i, named)
            at = pl.multiple_of(named * 256 + share, 16)
            out[d, 64 + 16 * f : 80 + 16 * f] = w[f, pl.ds(at, 16), :]
    for k in range(32):
        tab[k] = 0
    for f in range(2):
        rows = jnp.int32(0)
        cols = jnp.int32(0)
        for p in range(32):
            b = fb[f, p]
            tab[16 * f + rows] = p
            rows = rows + ((b >> 3) == r).astype(jnp.int32)
            tab[16 * f + 8 + cols] = p
            cols = cols + ((b >> 2) == c).astype(jnp.int32)


def pick_kernel(tab, inc, after, slices, mine):
    for f in range(2):
        for t in range(2):
            p = tab[16 * f + 8 + t]
            v = inc[p >> 2, 32 * f : 32 * f + 32, :]
            for d in range(4):
                slices[d, 2 * f + t] = v
        for s in range(4):
            p = tab[16 * f + s]
            mine[4 * f + s] = inc[p >> 2, 64 + 16 * f : 80 + 16 * f, :]


def tile_kernel(fb, tab, inverse, hi, lo, tiles, sems):
    copies = []
    for f in range(2):
        for s in range(4):
            for t in range(2):
                k = (4 * f + s) * 2 + t
                rb = fb[f, tab[16 * f + s]] & 7
                cb = fb[f, tab[16 * f + 8 + t]] & 3
                src = inverse.at[
                    pl.ds(pl.multiple_of(rb * 256, 256), 256),
                    pl.ds(pl.multiple_of(cb * 256, 256), 256),
                ]
                copy = pltpu.make_async_copy(src, tiles.at[k], sems.at[k])
                copy.start()
                copies.append(copy)
    for k in range(16):
        copies[k].wait()
        h, l = split(tiles[k])
        hi[k // 2, :, 256 * (k % 2) : 256 * (k % 2) + 256] = h
        lo[k // 2, :, 256 * (k % 2) : 256 * (k % 2) + 256] = l


def product_kernel(hi, lo, own, other, out, whole):
    core = lax.axis_index("core")
    for k in range(4):
        base = 256 * (k % 2)
        at = pl.multiple_of(base + 128 * core, 128)
        whole[k // 2, pl.ds(at, 128), :] = own[:, k].reshape(128, 256)
        at = pl.multiple_of(base + 128 * (1 - core), 128)
        whole[k // 2, pl.ds(at, 128), :] = other[:, k].reshape(128, 256)
    for f in range(2):
        w = split(whole[f])
        for s in range(4):
            total = dot3((hi[4 * f + s], lo[4 * f + s]), w, ((1,), (0,)))
            for d in range(16):
                at = 64 * (d % 4) + 16 * (d // 4)
                out[d, 4 * f + s] = total[at : at + 16, :]


def same_node(bounds, f):
    a = lax.broadcasted_iota(jnp.int32, (256, 256), 0)
    b = lax.broadcasted_iota(jnp.int32, (256, 256), 1)
    ia = jnp.zeros((256, 256), jnp.int32)
    ib = jnp.zeros((256, 256), jnp.int32)
    end = jnp.int32(0)
    for k in range(4):
        end = end + bounds[f, k]
        ia = ia + (a >= end).astype(jnp.int32)
        ib = ib + (b >= end).astype(jnp.int32)
    return ia == ib


def reduce_kernel(tab, bounds, parts, mine, out):
    for d in range(8):
        out[d, 0:32] = jnp.zeros((32, 256), F32)
    for f in range(2):
        rows = []
        for s in range(4):
            v = parts[0, 4 * f + s]
            for d in range(1, 16):
                v = v + parts[d, 4 * f + s]
            rows.append(v)
            out[tab[16 * f + s] >> 2, 16 * f : 16 * f + 16] = -v
        left = mine[4 * f : 4 * f + 4].reshape(64, 256)
        right = jnp.concatenate(rows, axis=0)
        full = dot3(split(left), split(right), ((0,), (0,)))
        full = jnp.where(same_node(bounds, f), full, 0.0)
        packed = full[:, :128] + full[:, 128:]
        for d in range(4):
            part = packed[64 * d : 64 * d + 64]
            out[4 * f + d, 32:64] = jnp.concatenate([part[:32], part[32:]], axis=1)


def place_kernel(fb, inc, out):
    r = lax.axis_index("y") * 2 + lax.axis_index("core")
    x = lax.axis_index("x")
    total = inc[0, 32:64]
    for d in range(1, 8):
        total = total + inc[d, 32:64]
    for d in range(16):
        out[d, 0:32] = jnp.zeros((32, 256), F32)
        out[d, 32:64] = total
    for f in range(2):
        for i in range(4):
            v = inc[fb[f, 4 * r + i] >> 3, 16 * f : 16 * f + 16, :]
            out[4 * i + x, 16 * f : 16 * f + 16] = v


def border_kernel(inc, border, out):
    x = lax.axis_index("x")
    for z in range(4):
        for f in range(2):
            border[f, 16 * z : 16 * z + 16] = inc[4 * z + x, 16 * f : 16 * f + 16, :]
    total = inc[0, 32:64]
    for d in range(1, 16):
        total = total + inc[d, 32:64]
    for d in range(4):
        out[d] = total


def finish_kernel(bounds, own, other, terms, out, chunks):
    core = lax.axis_index("core")
    for y in range(4):
        chunks[2 * y + core] = own[y]
        chunks[2 * y + 1 - core] = other[y]
    for f in range(2):
        same = same_node(bounds, f)
        for d in range(4):
            v = chunks[4 * f + d]
            v = jnp.concatenate([v[:, :128], v[:, 128:]], axis=0)
            at = slice(64 * d, 64 * d + 64)
            full = terms[f, at] + jnp.concatenate([v, v], axis=1)
            out[f, at] = jnp.where(same[at], full, 0.0)


def call(kernel, ins, out_shape, out_specs=None, scratch=(), limit=40, cost=None):
    if out_specs is None:
        out_specs = jax.tree.map(lambda _: VMEM, out_shape)
    return pl.pallas_call(
        kernel,
        in_specs=ins,
        out_shape=out_shape,
        out_specs=out_specs,
        scratch_shapes=scratch,
        cost_estimate=cost,
        compiler_params=pltpu.CompilerParams(vmem_limit_bytes=limit * MIB),
    )


def a2a(v, axes):
    return lax.all_to_all(v, axes, 0, 0, tiled=True)


def swap(v):
    return lax.ppermute(v, "core", [(0, 1), (1, 0)])


def body(inverse, fb, panels, terms, bounds):
    outgoing, tab = call(
        pack_kernel, [SMEM, VMEM], (sds((8, 96, 256)), sds((32,), jnp.int32)), (VMEM, SMEM)
    )(fb, panels)
    incoming = a2a(outgoing, ROW)
    hi, lo = call(
        tile_kernel,
        [SMEM, SMEM, HBM],
        (sds((8, 256, 512), BF16), sds((8, 256, 512), BF16)),
        scratch=[pltpu.VMEM((16, 256, 256), F32), pltpu.SemaphoreType.DMA((16,))],
        limit=52,
        cost=pl.CostEstimate(flops=4 * MIB, bytes_accessed=12 * MIB, transcendentals=0),
    )(fb, tab, inverse)
    slices, mine = call(
        pick_kernel, [SMEM, VMEM, ANY], (sds((4, 4, 32, 256)), sds((8, 16, 256)))
    )(tab, incoming, hi)
    own = a2a(slices, "y")
    other = swap(own)
    parts = call(
        product_kernel,
        [VMEM, VMEM, VMEM, VMEM],
        sds((16, 8, 16, 256)),
        scratch=[pltpu.VMEM((2, 512, 256), F32)],
    )(hi, lo, own, other)
    parts = a2a(parts, COL)
    v = call(reduce_kernel, [SMEM, SMEM, VMEM, VMEM], sds((8, 64, 256)))(tab, bounds, parts, mine)
    v = a2a(v, ROW)
    v = call(place_kernel, [SMEM, VMEM], sds((16, 64, 256)))(fb, v)
    v = a2a(v, COL)
    border, v = call(border_kernel, [VMEM], (sds((2, 64, 256)), sds((4, 32, 256))))(v)
    own = a2a(v, "y")
    other = swap(own)
    diag = call(
        finish_kernel,
        [SMEM, VMEM, VMEM, VMEM],
        sds((2, 256, 256)),
        scratch=[pltpu.VMEM((8, 32, 256), F32)],
    )(bounds, own, other, terms)
    return border, diag


def solution(mesh):
    grid = Mesh(mesh.devices.reshape(4, 2, 4, 4), ALL)
    placed = (P(ROW, COL), P(), P(None, ROW, None), P(), P())
    return jax.shard_map(
        body,
        mesh=grid,
        in_specs=placed,
        out_specs=(P(None, ALL, None), P()),
        check_vma=False,
    )
```

time: 162 us -> 126 us (0.78)
  waiting for transfers between devices: 49.9 us -> 9.95 us
  blocking collectives: 62.9 us -> 85.5 us
  between operations: 14.1 us -> 0.71 us
  local copies, waits for them, and re-layouts: 7.55 us -> 5.46 us
  starting transfers between devices: 12.9 us -> 11.2 us
    all_gather x1 -> x0, waiting for transfers between devices: 24.7 us -> none  [body(): w = lax.all_gather(slices, ROW, axis=0, tiled=False)]
    all_to_all x3 -> x5, blocking collectives: 62.9 us -> 85.5 us  [a2a(): return lax.all_to_all(v, axes, 0, 0, tiled=True)]
    all_to_all x3 -> x1, waiting for transfers between devices: 25.2 us -> 7.43 us  [a2a(): return lax.all_to_all(v, axes, 0, 0, tiled=True)]
    all_to_all x3 -> x1, starting transfers between devices: 12.8 us -> 5.98 us  [a2a(): return lax.all_to_all(v, axes, 0, 0, tiled=True)]
    ppermute x0 -> x2, starting transfers between devices: none -> 5.18 us  [swap(): return lax.ppermute(v, 'core', [(0, 1), (1, 0)])]
    ppermute x0 -> x2, waiting for transfers between devices: none -> 2.52 us  [swap(): return lax.ppermute(v, 'core', [(0, 1), (1, 0)])]
    unnamed x14 -> x16, local copies, waits for them, and re-layouts: 6.88 us -> 5.46 us
    pallas_call x6 -> x7, Pallas kernels: 12.6 us -> 11.3 us  [the longest x1 4.85 us: body(): call(tile_kernel, [SMEM, SMEM, HBM], (sds((8, 256, 512), BF16), sds((8, 2...]
  transfers between devices with their start and end apart: 4 -> 3, of which waited for: 4 -> 3; matrix products, arithmetic and copies ran while one was open for 0% -> 0% of each run, Pallas kernels for 1% -> 4%
where the time goes in v2:
time: 126 us
  blocking collectives  85.5 us (68%)
  Pallas kernels  12.8 us (10%)
  starting transfers between devices  11.2 us (9%)
  waiting for transfers between devices  9.95 us (8%)
  local copies, waits for them, and re-layouts  5.46 us (4%)
    all_to_all x5, blocking collectives, a2a(): return lax.all_to_all(v, axes, 0, 0, tiled=True)  85.5 us
    all_to_all x1, waiting for transfers between devices, a2a(): return lax.all_to_all(v, axes, 0, 0, tiled=True)  7.43 us
    all_to_all x1, starting transfers between devices, a2a(): return lax.all_to_all(v, axes, 0, 0, tiled=True)  5.98 us
    unnamed x16, local copies, waits for them, and re-layouts  5.46 us
    ppermute x2, starting transfers between devices, swap(): return lax.ppermute(v, 'core', [(0, 1), (1, 0)])  5.18 us
    pallas_call x1, Pallas kernels, body(): call(tile_kernel, [SMEM, SMEM, HBM], (sds((8, 256, 512), BF16), sds((8, 2...  4.85 us
    ppermute x2, waiting for transfers between devices, swap(): return lax.ppermute(v, 'core', [(0, 1), (1, 0)])  2.52 us
  transfers between devices with their start and end apart: 3, of which 3 were waited for; matrix products, arithmetic and copies ran while one was open for 0% of the time, Pallas kernels for 4%

profile of v2, /device:TPU:1, one launch (start us, length us, event | category | flops | bytes accessed | tf_op | source)
XLA Modules:
  0.0 125.6 jit_solution(8629674204443330034)
XLA Ops:
  0.6 0.0 copy-start.3
  0.6 1.6 %copy-done.3 = f32[2,1024,256]{2,1,0:T(8,128)S(1)} copy-done((f32[2,1024,256]{2,1,0:T(8,128)S(1)}, f32[2,1024,256]{2,1,0:T(8,128)}, u32[]{:S(2)}) %copy-start.3) | copy-done | bytes 2097176
  2.2 0.0 copy-start.5
  2.2 0.7 copy-done.5
  2.9 0.0 copy-start.6
  2.9 1.6 %shard_map.68 = (f32[8,96,256]{2,1,0:T(8,128)}, s32[32]{0:T(128)S(1)}) custom-call(s32[2,32]{1,0:T(2,128)S(1)} %copy-done.5, f32[2,1024,256]{2,1,0:T(8,128)S(1)} %copy-done.3), custom_call_target="tpu_custom_call" | custom-call | tf_op jit(solution)/shard_map/pallas_call | solution.py:217
  4.5 6.0 %all-to-all-start = ((f32[8,96,256]{2,1,0:T(8,128)}), f32[8,96,256]{2,1,0:T(8,128)S(1)}, u32[]{:S(2)}, u32[]{:S(2)}) async-start(f32[8,96,256]{2,1,0:T(8,128)} %get-tuple-element.13), calls=%async_computation | async-start | bytes 1572864 | tf_op jit(solution)/shard_map/all_to_all | solution.py:209
  10.4 0.0 copy-done.6
  10.5 4.9 %shard_map.69 = (bf16[8,256,512]{2,1,0:T(8,128)(2,1)}, bf16[8,256,512]{2,1,0:T(8,128)(2,1)}) custom-call(s32[2,32]{1,0:T(2,128)S(1)} %copy-done.6, s32[32]{0:T(128)S(1)} %get-tuple-element.10.tab, f32[2048,1024]{1,0:T(8,128)} %inverse.1), custom_call_target="tpu_custom_call" | custom-call | flops 4194304 | bytes 12582912 | tf_op jit(solution)/shard_map/pallas_call | solution.py:221
  15.3 7.4 %all-to-all-done.inc = f32[8,96,256]{2,1,0:T(8,128)S(1)} async-done(((f32[8,96,256]{2,1,0:T(8,128)}), f32[8,96,256]{2,1,0:T(8,128)S(1)}, u32[]{:S(2)}, u32[]{:S(2)}) %all-to-all-start) | async-done | bytes 786464 | tf_op jit(solution)/shard_map/all_to_all | solution.py:209
  22.7 0.0 copy-start
  22.7 1.6 %copy-done = bf16[8,256,512]{2,1,0:T(8,128)(2,1)S(1)} copy-done((bf16[8,256,512]{2,1,0:T(8,128)(2,1)S(1)}, bf16[8,256,512]{2,1,0:T(8,128)(2,1)}, u32[]{:S(2)}) %copy-start) | copy-done | bytes 2097176
  24.3 0.0 copy-start.1
  24.3 0.6 shard_map.70
  24.9 11.1 %all_to_all.30.own = f32[4,4,32,256]{3,2,1,0:T(8,128)S(1)} all-to-all(f32[4,4,32,256]{3,2,1,0:T(8,128)S(1)} %get-tuple-element.14), channel_id=1, replica_groups=mesh['y'=4,'core'=2,'z'=4,'x'=4] {'y'}, dimensions={0} | all-to-all | bytes 1048576 | tf_op jit(solution)/shard_map/all_to_all | solution.py:209
  36.1 1.8 %collective-permute-start = (f32[4,4,32,256]{3,2,1,0:T(8,128)S(1)}, f32[4,4,32,256]{3,2,1,0:T(8,128)S(1)}, u32[]{:S(2)}, u32[]{:S(2)}) collective-permute-start(f32[4,4,32,256]{3,2,1,0:T(8,128)S(1)} %all_to_all.30.own), channel_id=1, source_target_pairs={{0,16},{16,0},{1,17},{17,1},{2,18},{18,2},{3,19},{19,3},{4,20},{20... | collective-permute-start | bytes 1572872 | tf_op jit(solution)/shard_map/ppermute | solution.py:213
  37.9 1.5 %collective-permute-done.other = f32[4,4,32,256]{3,2,1,0:T(8,128)S(1)} collective-permute-done((f32[4,4,32,256]{3,2,1,0:T(8,128)S(1)}, f32[4,4,32,256]{3,2,1,0:T(8,128)S(1)}, u32[]{:S(2)}, u32[]{:S(2)}) %collective-permute-start) | collective-permute-done | bytes 524320 | tf_op jit(solution)/shard_map/ppermute | solution.py:213
  39.4 0.0 copy-done.1
  39.4 0.0 copy-start.2
  39.4 1.6 %copy-done.2 = bf16[8,256,512]{2,1,0:T(8,128)(2,1)S(1)} copy-done((bf16[8,256,512]{2,1,0:T(8,128)(2,1)S(1)}, bf16[8,256,512]{2,1,0:T(8,128)(2,1)}, u32[]{:S(2)}) %copy-start.2) | copy-done | bytes 2097176
  41.0 1.9 %shard_map.71 = f32[16,8,16,256]{3,2,1,0:T(8,128)S(1)} custom-call(bf16[8,256,512]{2,1,0:T(8,128)(2,1)S(1)} %copy-done.1, bf16[8,256,512]{2,1,0:T(8,128)(2,1)S(1)} %copy-done.2, f32[4,4,32,256]{3,2,1,0:T(8,128)S(1)} %all_to_all.30.own, f32[4,4,32,256]{3,2,1,0:T(8,128)S(1)} %collective-permute-done.other), custom_call_target="tpu_custom_call" | custom-call | tf_op jit(solution)/shard_map/pallas_call | solution.py:234
  42.9 0.0 copy-start.7
  42.9 34.9 %all_to_all.31.parts = f32[16,8,16,256]{3,2,1,0:T(8,128)S(1)} all-to-all(f32[16,8,16,256]{3,2,1,0:T(8,128)S(1)} %shard_map.71), channel_id=1, replica_groups=mesh['y'=4,'core'=2,'z'=4,'x'=4] {'z','x'}, dimensions={0} | all-to-all | bytes 4194304 | tf_op jit(solution)/shard_map/all_to_all | solution.py:209
  77.9 0.0 copy-done.7
  77.9 1.0 shard_map.72
  78.9 13.6 %all_to_all.32.inc = f32[8,64,256]{2,1,0:T(8,128)S(1)} all-to-all(f32[8,64,256]{2,1,0:T(8,128)S(1)} %shard_map.72), channel_id=1, replica_groups=mesh['y'=4,'core'=2,'z'=4,'x'=4] {'y','core'}, dimensions={0} | all-to-all | bytes 1048576 | tf_op jit(solution)/shard_map/all_to_all | solution.py:209
  92.5 0.6 shard_map.73
  93.1 0.0 copy-start.4
  93.1 18.7 %all_to_all.33.inc = f32[16,64,256]{2,1,0:T(8,128)S(1)} all-to-all(f32[16,64,256]{2,1,0:T(8,128)S(1)} %shard_map.73), channel_id=1, replica_groups=mesh['y'=4,'core'=2,'z'=4,'x'=4] {'z','x'}, dimensions={0} | all-to-all | bytes 2097152 | tf_op jit(solution)/shard_map/all_to_all | solution.py:209
  111.8 0.7 shard_map.74
  112.5 7.2 %all_to_all.34.own = f32[4,32,256]{2,1,0:T(8,128)S(1)} all-to-all(f32[4,32,256]{2,1,0:T(8,128)S(1)} %get-tuple-element.17), channel_id=1, replica_groups=mesh['y'=4,'core'=2,'z'=4,'x'=4] {'y'}, dimensions={0} | all-to-all | bytes 262144 | tf_op jit(solution)/shard_map/all_to_all | solution.py:209
  119.7 3.3 %collective-permute-start.1 = (f32[4,32,256]{2,1,0:T(8,128)S(1)}, f32[4,32,256]{2,1,0:T(8,128)S(1)}, u32[]{:S(2)}, u32[]{:S(2)}) collective-permute-start(f32[4,32,256]{2,1,0:T(8,128)S(1)} %all_to_all.34.own), channel_id=1, source_target_pairs={{0,16},{16,0},{1,17},{17,1},{2,18},{18,2},{3,19},{19,3},{4,20},{20... | collective-permute-start | bytes 393224 | tf_op jit(solution)/shard_map/ppermute | solution.py:213
  123.1 1.0 collective-permute-done.1.other
  124.0 0.0 copy-done.4
  124.0 1.6 %shard_map.75 = f32[2,256,256]{2,1,0:T(8,128)} custom-call(s32[2,4]{1,0:T(2,128)S(1)} %copy-done.7, f32[4,32,256]{2,1,0:T(8,128)S(1)} %all_to_all.34.own, f32[4,32,256]{2,1,0:T(8,128)S(1)} %collective-permute-done.1.other, f32[2,256,256]{2,1,0:T(8,128)S(1)} %copy-done.4), custom_call_target="tpu_custom_call" | custom-call | tf_op jit(solution)/shard_map/pallas_call | solution.py:248
Async XLA Ops:
  0.6 1.6 %copy-start.3 = (f32[2,1024,256]{2,1,0:T(8,128)S(1)}, f32[2,1024,256]{2,1,0:T(8,128)}, u32[]{:S(2)}) copy-start(f32[2,1024,256]{2,1,0:T(8,128)} %w.1) | copy-start | bytes 6291460
  2.2 0.7 copy-start.5
  2.9 7.5 %copy-start.6 = (s32[2,32]{1,0:T(2,128)S(1)}, s32[2,32]{1,0:T(2,128)}, u32[]{:S(2)}) copy-start(s32[2,32]{1,0:T(2,128)} %fb.5) | copy-start | bytes 772
  4.5 18.3 %all-to-all-start = ((f32[8,96,256]{2,1,0:T(8,128)}), f32[8,96,256]{2,1,0:T(8,128)S(1)}, u32[]{:S(2)}, u32[]{:S(2)}) async-start(f32[8,96,256]{2,1,0:T(8,128)} %get-tuple-element.13), calls=%async_computation | async-start | bytes 1572864 | tf_op jit(solution)/shard_map/all_to_all | solution.py:209
  22.7 1.6 %copy-start = (bf16[8,256,512]{2,1,0:T(8,128)(2,1)S(1)}, bf16[8,256,512]{2,1,0:T(8,128)(2,1)}, u32[]{:S(2)}) copy-start(bf16[8,256,512]{2,1,0:T(8,128)(2,1)} %get-tuple-element.11.after.hi) | copy-start | bytes 6291460
  24.3 15.1 %copy-start.1 = (bf16[8,256,512]{2,1,0:T(8,128)(2,1)S(1)}, bf16[8,256,512]{2,1,0:T(8,128)(2,1)}, u32[]{:S(2)}) copy-start(bf16[8,256,512]{2,1,0:T(8,128)(2,1)} %get-tuple-element.11.after.hi) | copy-start | bytes 6291460
  36.1 3.4 %collective-permute-start = (f32[4,4,32,256]{3,2,1,0:T(8,128)S(1)}, f32[4,4,32,256]{3,2,1,0:T(8,128)S(1)}, u32[]{:S(2)}, u32[]{:S(2)}) collective-permute-start(f32[4,4,32,256]{3,2,1,0:T(8,128)S(1)} %all_to_all.30.own), channel_id=1, source_target_pairs={{0,16},{16,0},{1,17},{17,1},{2,18},{18,2},{3,19},{19,3},{4,20},{20... | collective-permute-start | bytes 1572872 | tf_op jit(solution)/shard_map/ppermute | solution.py:213
  39.4 1.6 %copy-start.2 = (bf16[8,256,512]{2,1,0:T(8,128)(2,1)S(1)}, bf16[8,256,512]{2,1,0:T(8,128)(2,1)}, u32[]{:S(2)}) copy-start(bf16[8,256,512]{2,1,0:T(8,128)(2,1)} %get-tuple-element.12.lo) | copy-start | bytes 6291460
  42.9 35.0 %copy-start.7 = (s32[2,4]{1,0:T(2,128)S(1)}, s32[2,4]{1,0:T(2,128)}, u32[]{:S(2)}) copy-start(s32[2,4]{1,0:T(2,128)} %bounds.3) | copy-start | bytes 100
  93.1 30.9 %copy-start.4 = (f32[2,256,256]{2,1,0:T(8,128)S(1)}, f32[2,256,256]{2,1,0:T(8,128)}, u32[]{:S(2)}) copy-start(f32[2,256,256]{2,1,0:T(8,128)} %terms.1) | copy-start | bytes 1572868
  119.7 4.3 %collective-permute-start.1 = (f32[4,32,256]{2,1,0:T(8,128)S(1)}, f32[4,32,256]{2,1,0:T(8,128)S(1)}, u32[]{:S(2)}, u32[]{:S(2)}) collective-permute-start(f32[4,32,256]{2,1,0:T(8,128)S(1)} %all_to_all.34.own), channel_id=1, source_target_pairs={{0,16},{16,0},{1,17},{17,1},{2,18},{18,2},{3,19},{19,3},{4,20},{20... | collective-permute-start | bytes 393224 | tf_op jit(solution)/shard_map/ppermute | solution.py:213

commit v3 on v2

--- a/solution.py
+++ b/solution.py
@@ -13,7 +13,6 @@
 VMEM = pl.BlockSpec(memory_space=pltpu.VMEM)
 SMEM = pl.BlockSpec(memory_space=pltpu.SMEM)
 ANY = pl.BlockSpec(memory_space=pl.ANY)
-HBM = pl.BlockSpec(memory_space=pltpu.HBM)
 MIB = 1024 * 1024
 
 
@@ -33,24 +32,34 @@
     return mm(ah, bh) + (mm(ah, bl) + mm(al, bh))
 
 
-def pack_kernel(fb, w, out, tab):
+def pack_kernel(fb, w, out, tab, sems):
     r = lax.axis_index("y") * 2 + lax.axis_index("core")
     z, x = lax.axis_index("z"), lax.axis_index("x")
     c = z * 4 + x
-    share = x * 64 + z * 16
+    part = 2 * x + z // 2
+    row = pl.multiple_of(16 * (z % 2), 16)
+    copies = []
+
+    def start(src, dst):
+        copy = pltpu.make_async_copy(src, dst, sems.at[len(copies)])
+        copy.start()
+        copies.append(copy)
+
     for f in range(2):
         own = [fb[f, 4 * r + i] for i in range(4)]
         piece = jnp.int32(0)
         for i in range(1, 4):
             piece = jnp.where((own[i] >> 2) == c, i, piece)
+        for k in range(2):
+            start(w.at[f, piece, k], out.at[:, k, 32 * f : 32 * f + 32])
         for d in range(8):
-            at = pl.multiple_of(piece * 256 + (d % 2 * 4 + d // 2) * 32, 32)
-            out[d, 32 * f : 32 * f + 32] = w[f, pl.ds(at, 32), :]
             named = jnp.int32(0)
             for i in range(1, 4):
                 named = jnp.where((own[i] >> 3) == d, i, named)
-            at = pl.multiple_of(named * 256 + share, 16)
-            out[d, 64 + 16 * f : 80 + 16 * f] = w[f, pl.ds(at, 16), :]
+            start(
+                w.at[f, named, part // 4, part % 4, pl.ds(row, 16)],
+                out.at[d // 2, d % 2, 64 + 16 * f : 80 + 16 * f],
+            )
     for k in range(32):
         tab[k] = 0
     for f in range(2):
@@ -62,6 +71,8 @@
             rows = rows + ((b >> 3) == r).astype(jnp.int32)
             tab[16 * f + 8 + cols] = p
             cols = cols + ((b >> 2) == c).astype(jnp.int32)
+    for copy in copies:
+        copy.wait()
 
 
 def pick_kernel(tab, inc, after, slices, mine):
@@ -149,29 +160,30 @@
             out[4 * f + d, 32:64] = jnp.concatenate([part[:32], part[32:]], axis=1)
 
 
-def place_kernel(fb, inc, out):
+def place_kernel(fb, inc, route, share):
     r = lax.axis_index("y") * 2 + lax.axis_index("core")
-    x = lax.axis_index("x")
     total = inc[0, 32:64]
     for d in range(1, 8):
         total = total + inc[d, 32:64]
-    for d in range(16):
-        out[d, 0:32] = jnp.zeros((32, 256), F32)
+    for d in range(4):
+        share[d] = total
+    for f in range(2):
+        for i in range(4):
+            route[i, 16 * f : 16 * f + 16] = inc[fb[f, 4 * r + i] >> 3, 16 * f : 16 * f + 16, :]
+
+
+def join_kernel(route, share, out):
+    total = (share[0] + share[1]) + (share[2] + share[3])
+    for d in range(4):
+        out[d, 0:32] = route[d]
         out[d, 32:64] = total
-    for f in range(2):
-        for i in range(4):
-            v = inc[fb[f, 4 * r + i] >> 3, 16 * f : 16 * f + 16, :]
-            out[4 * i + x, 16 * f : 16 * f + 16] = v
 
 
 def border_kernel(inc, border, out):
-    x = lax.axis_index("x")
     for z in range(4):
         for f in range(2):
-            border[f, 16 * z : 16 * z + 16] = inc[4 * z + x, 16 * f : 16 * f + 16, :]
-    total = inc[0, 32:64]
-    for d in range(1, 16):
-        total = total + inc[d, 32:64]
+            border[f, 16 * z : 16 * z + 16] = inc[z, 16 * f : 16 * f + 16, :]
+    total = (inc[0, 32:64] + inc[1, 32:64]) + (inc[2, 32:64] + inc[3, 32:64])
     for d in range(4):
         out[d] = total
 
@@ -209,23 +221,31 @@
     return lax.all_to_all(v, axes, 0, 0, tiled=True)
 
 
+def hbm(v):
+    return pltpu.with_memory_space_constraint(v, pltpu.HBM)
+
+
 def swap(v):
     return lax.ppermute(v, "core", [(0, 1), (1, 0)])
 
 
 def body(inverse, fb, panels, terms, bounds):
     outgoing, tab = call(
-        pack_kernel, [SMEM, VMEM], (sds((8, 96, 256)), sds((32,), jnp.int32)), (VMEM, SMEM)
-    )(fb, panels)
-    incoming = a2a(outgoing, ROW)
+        pack_kernel,
+        [SMEM, ANY],
+        (sds((4, 2, 96, 256)), sds((32,), jnp.int32)),
+        (VMEM, SMEM),
+        scratch=[pltpu.SemaphoreType.DMA((20,))],
+    )(hbm(fb), hbm(panels.reshape(2, 4, 2, 4, 32, 256)))
+    incoming = a2a(outgoing.reshape(8, 96, 256), ROW)
     hi, lo = call(
         tile_kernel,
-        [SMEM, SMEM, HBM],
+        [SMEM, SMEM, ANY],
         (sds((8, 256, 512), BF16), sds((8, 256, 512), BF16)),
         scratch=[pltpu.VMEM((16, 256, 256), F32), pltpu.SemaphoreType.DMA((16,))],
-        limit=52,
+        limit=24,
         cost=pl.CostEstimate(flops=4 * MIB, bytes_accessed=12 * MIB, transcendentals=0),
-    )(fb, tab, inverse)
+    )(fb, tab, hbm(inverse))
     slices, mine = call(
         pick_kernel, [SMEM, VMEM, ANY], (sds((4, 4, 32, 256)), sds((8, 16, 256)))
     )(tab, incoming, hi)
@@ -240,8 +260,10 @@
     parts = a2a(parts, COL)
     v = call(reduce_kernel, [SMEM, SMEM, VMEM, VMEM], sds((8, 64, 256)))(tab, bounds, parts, mine)
     v = a2a(v, ROW)
-    v = call(place_kernel, [SMEM, VMEM], sds((16, 64, 256)))(fb, v)
-    v = a2a(v, COL)
+    route, v = call(place_kernel, [SMEM, VMEM], (sds((4, 32, 256)), sds((4, 32, 256))))(fb, v)
+    v = a2a(v, "x")
+    v = call(join_kernel, [VMEM, VMEM], sds((4, 64, 256)))(route, v)
+    v = a2a(v, "z")
     border, v = call(border_kernel, [VMEM], (sds((2, 64, 256)), sds((4, 32, 256))))(v)
     own = a2a(v, "y")
     other = swap(own)

time: 126 us -> 120 us (0.952)
  local copies, waits for them, and re-layouts: 5.46 us -> 1.34 us
  blocking collectives: 85.5 us -> 82.1 us
    unnamed x16 -> x10, local copies, waits for them, and re-layouts: 5.46 us -> 1.34 us
    all_to_all x5 -> x6, blocking collectives: 85.5 us -> 82.1 us  [a2a(): return lax.all_to_all(v, axes, 0, 0, tiled=True)]
    pallas_call x3 -> x4, Pallas kernels: 7.04 us -> 6.93 us  [the longest x1 3.41 us: body(): call(pack_kernel, [SMEM, ANY], (sds((4, 2, 96, 256)), sds((32,), jnp.int3...]
  transfers between devices with their start and end apart: 3 -> 3, of which waited for: 3 -> 3; matrix products, arithmetic and copies ran while one was open for 0% -> 0% of each run, Pallas kernels for 4% -> 2%
where the time goes in v3:
time: 120 us
  blocking collectives  82.1 us (68%)
  Pallas kernels  12.7 us (11%)
  starting transfers between devices  12.3 us (10%)
  waiting for transfers between devices  10.6 us (9%)
  local copies, waits for them, and re-layouts  1.34 us (1%)
    all_to_all x6, blocking collectives, a2a(): return lax.all_to_all(v, axes, 0, 0, tiled=True)  82.1 us
    all_to_all x1, waiting for transfers between devices, a2a(): return lax.all_to_all(v, axes, 0, 0, tiled=True)  8.04 us
    ppermute x2, starting transfers between devices, swap(): return lax.ppermute(v, 'core', [(0, 1), (1, 0)])  6.32 us
    all_to_all x1, starting transfers between devices, a2a(): return lax.all_to_all(v, axes, 0, 0, tiled=True)  5.98 us
    pallas_call x1, Pallas kernels, body(): call(pack_kernel, [SMEM, ANY], (sds((4, 2, 96, 256)), sds((32,), jnp.int3...  3.41 us
    pallas_call x1, Pallas kernels, body(): call(tile_kernel, [SMEM, SMEM, ANY], (sds((8, 256, 512), BF16), sds((8, 2...  2.92 us
    ppermute x2, waiting for transfers between devices, swap(): return lax.ppermute(v, 'core', [(0, 1), (1, 0)])  2.52 us
  transfers between devices with their start and end apart: 3, of which 3 were waited for; matrix products, arithmetic and copies ran while one was open for 0% of the time, Pallas kernels for 2%

profile of v3, /device:TPU:1, one launch (start us, length us, event | category | flops | bytes accessed | tf_op | source)
XLA Modules:
  0.0 119.7 jit_solution(9841644498756561226)
XLA Ops:
  0.6 0.0 copy-start.3
  0.6 3.4 %shard_map.68 = (f32[4,2,96,256]{3,2,1,0:T(8,128)}, s32[32]{0:T(128)S(1)}) custom-call(s32[2,32]{1,0:T(2,128)} %fb.5, f32[2,4,2,4,32,256]{5,4,3,2,1,0:T(8,128)} %bitcast.2), custom_call_target="tpu_custom_call" | custom-call | tf_op jit(solution)/shard_map/pallas_call | solution.py:233
  4.1 6.0 %all-to-all-start = ((f32[8,96,256]{2,1,0:T(8,128)}), f32[8,96,256]{2,1,0:T(8,128)S(1)}, u32[]{:S(2)}, u32[]{:S(2)}) async-start(f32[8,96,256]{2,1,0:T(8,128)} %bitcast.1), calls=%async_computation | async-start | bytes 1572864 | tf_op jit(solution)/shard_map/all_to_all | solution.py:221
  10.0 0.0 copy-done.3
  10.0 2.9 %shard_map.69 = (bf16[8,256,512]{2,1,0:T(8,128)(2,1)S(1)}, bf16[8,256,512]{2,1,0:T(8,128)(2,1)S(1)}) custom-call(s32[2,32]{1,0:T(2,128)S(1)} %copy-done.3, s32[32]{0:T(128)S(1)} %get-tuple-element.12.tab, f32[2048,1024]{1,0:T(8,128)} %inverse.1), custom_call_target="tpu_custom_call" | custom-call | flops 4194304 | bytes 12582912 | tf_op jit(solution)/shard_map/pallas_call | solution.py:241
  13.0 0.0 copy-start
  13.0 1.3 %copy-done = bf16[8,256,512]{2,1,0:T(8,128)(2,1)} copy-done((bf16[8,256,512]{2,1,0:T(8,128)(2,1)}, bf16[8,256,512]{2,1,0:T(8,128)(2,1)S(1)}, u32[]{:S(2)}) %copy-start) | copy-done | bytes 2097176
  14.3 8.0 %all-to-all-done.inc = f32[8,96,256]{2,1,0:T(8,128)S(1)} async-done(((f32[8,96,256]{2,1,0:T(8,128)}), f32[8,96,256]{2,1,0:T(8,128)S(1)}, u32[]{:S(2)}, u32[]{:S(2)}) %all-to-all-start) | async-done | bytes 786464 | tf_op jit(solution)/shard_map/all_to_all | solution.py:221
  22.3 0.0 copy-start.1
  22.3 0.6 shard_map.70
  22.9 11.1 %all_to_all.35.own = f32[4,4,32,256]{3,2,1,0:T(8,128)S(1)} all-to-all(f32[4,4,32,256]{3,2,1,0:T(8,128)S(1)} %get-tuple-element.16), channel_id=1, replica_groups=mesh['y'=4,'core'=2,'z'=4,'x'=4] {'y'}, dimensions={0} | all-to-all | bytes 1048576 | tf_op jit(solution)/shard_map/all_to_all | solution.py:221
  34.1 1.8 %collective-permute-start = (f32[4,4,32,256]{3,2,1,0:T(8,128)S(1)}, f32[4,4,32,256]{3,2,1,0:T(8,128)S(1)}, u32[]{:S(2)}, u32[]{:S(2)}) collective-permute-start(f32[4,4,32,256]{3,2,1,0:T(8,128)S(1)} %all_to_all.35.own), channel_id=1, source_target_pairs={{0,16},{16,0},{1,17},{17,1},{2,18},{18,2},{3,19},{19,3},{4,20},{20... | collective-permute-start | bytes 1572872 | tf_op jit(solution)/shard_map/ppermute | solution.py:229
  35.9 1.5 %collective-permute-done.other = f32[4,4,32,256]{3,2,1,0:T(8,128)S(1)} collective-permute-done((f32[4,4,32,256]{3,2,1,0:T(8,128)S(1)}, f32[4,4,32,256]{3,2,1,0:T(8,128)S(1)}, u32[]{:S(2)}, u32[]{:S(2)}) %collective-permute-start) | collective-permute-done | bytes 524320 | tf_op jit(solution)/shard_map/ppermute | solution.py:229
  37.4 0.0 copy-done.1
  37.4 1.9 %shard_map.71 = f32[16,8,16,256]{3,2,1,0:T(8,128)S(1)} custom-call(bf16[8,256,512]{2,1,0:T(8,128)(2,1)S(1)} %get-tuple-element.13.after.hi, bf16[8,256,512]{2,1,0:T(8,128)(2,1)S(1)} %copy-done.1, f32[4,4,32,256]{3,2,1,0:T(8,128)S(1)} %all_to_all.35.own, f32[4,4,32,256]{3,2,1,0:T(8,128)S(1)} %collective-permute-done.other), custom_call_target="tpu_custom_call" | custom-call | tf_op jit(solution)/shard_map/pallas_call | solution.py:254
  39.3 0.0 copy-start.4
  39.3 34.9 %all_to_all.36.parts = f32[16,8,16,256]{3,2,1,0:T(8,128)S(1)} all-to-all(f32[16,8,16,256]{3,2,1,0:T(8,128)S(1)} %shard_map.71), channel_id=1, replica_groups=mesh['y'=4,'core'=2,'z'=4,'x'=4] {'z','x'}, dimensions={0} | all-to-all | bytes 4194304 | tf_op jit(solution)/shard_map/all_to_all | solution.py:221
  74.3 0.0 copy-done.4
  74.3 1.0 shard_map.72
  75.3 0.0 copy-start.2
  75.3 13.7 %all_to_all.37.inc = f32[8,64,256]{2,1,0:T(8,128)S(1)} all-to-all(f32[8,64,256]{2,1,0:T(8,128)S(1)} %shard_map.72), channel_id=1, replica_groups=mesh['y'=4,'core'=2,'z'=4,'x'=4] {'y','core'}, dimensions={0} | all-to-all | bytes 1048576 | tf_op jit(solution)/shard_map/all_to_all | solution.py:221
  89.0 0.6 shard_map.73
  89.6 7.2 %all_to_all.38.share = f32[4,32,256]{2,1,0:T(8,128)S(1)} all-to-all(f32[4,32,256]{2,1,0:T(8,128)S(1)} %get-tuple-element.19), channel_id=1, replica_groups=mesh['y'=4,'core'=2,'z'=4,'x'=4] {'x'}, dimensions={0} | all-to-all | bytes 262144 | tf_op jit(solution)/shard_map/all_to_all | solution.py:221
  96.8 7.9 %all_to_all.39.inc = f32[4,64,256]{2,1,0:T(8,128)S(1)} all-to-all(f32[4,64,256]{2,1,0:T(8,128)S(1)} %shard_map.74), channel_id=1, replica_groups=mesh['y'=4,'core'=2,'z'=4,'x'=4] {'z'}, dimensions={0} | all-to-all | bytes 524288 | tf_op jit(solution)/shard_map/all_to_all | solution.py:221
  104.7 0.7 shard_map.75
  105.4 7.2 %all_to_all.40.own = f32[4,32,256]{2,1,0:T(8,128)S(1)} all-to-all(f32[4,32,256]{2,1,0:T(8,128)S(1)} %get-tuple-element.21), channel_id=1, replica_groups=mesh['y'=4,'core'=2,'z'=4,'x'=4] {'y'}, dimensions={0} | all-to-all | bytes 262144 | tf_op jit(solution)/shard_map/all_to_all | solution.py:221
  112.6 4.5 %collective-permute-start.1 = (f32[4,32,256]{2,1,0:T(8,128)S(1)}, f32[4,32,256]{2,1,0:T(8,128)S(1)}, u32[]{:S(2)}, u32[]{:S(2)}) collective-permute-start(f32[4,32,256]{2,1,0:T(8,128)S(1)} %all_to_all.40.own), channel_id=1, source_target_pairs={{0,16},{16,0},{1,17},{17,1},{2,18},{18,2},{3,19},{19,3},{4,20},{20... | collective-permute-start | bytes 393224 | tf_op jit(solution)/shard_map/ppermute | solution.py:229
  117.1 1.0 collective-permute-done.1.other
  118.1 0.0 copy-done.2
  118.1 1.6 %shard_map.76 = f32[2,256,256]{2,1,0:T(8,128)} custom-call(s32[2,4]{1,0:T(2,128)S(1)} %copy-done.4, f32[4,32,256]{2,1,0:T(8,128)S(1)} %all_to_all.40.own, f32[4,32,256]{2,1,0:T(8,128)S(1)} %collective-permute-done.1.other, f32[2,256,256]{2,1,0:T(8,128)S(1)} %copy-done.2), custom_call_target="tpu_custom_call" | custom-call | tf_op jit(solution)/shard_map/pallas_call | solution.py:270
  (1 shorter events, 0.0 us)
Async XLA Ops:
  0.6 9.4 %copy-start.3 = (s32[2,32]{1,0:T(2,128)S(1)}, s32[2,32]{1,0:T(2,128)}, u32[]{:S(2)}) copy-start(s32[2,32]{1,0:T(2,128)} %fb.5) | copy-start | bytes 772
  4.1 18.3 %all-to-all-start = ((f32[8,96,256]{2,1,0:T(8,128)}), f32[8,96,256]{2,1,0:T(8,128)S(1)}, u32[]{:S(2)}, u32[]{:S(2)}) async-start(f32[8,96,256]{2,1,0:T(8,128)} %bitcast.1), calls=%async_computation | async-start | bytes 1572864 | tf_op jit(solution)/shard_map/all_to_all | solution.py:221
  13.0 1.3 %copy-start = (bf16[8,256,512]{2,1,0:T(8,128)(2,1)}, bf16[8,256,512]{2,1,0:T(8,128)(2,1)S(1)}, u32[]{:S(2)}) copy-start(bf16[8,256,512]{2,1,0:T(8,128)(2,1)S(1)} %get-tuple-element.14.lo) | copy-start | bytes 6291460
  22.3 15.1 %copy-start.1 = (bf16[8,256,512]{2,1,0:T(8,128)(2,1)S(1)}, bf16[8,256,512]{2,1,0:T(8,128)(2,1)}, u32[]{:S(2)}) copy-start(bf16[8,256,512]{2,1,0:T(8,128)(2,1)} %copy-done) | copy-start | bytes 6291460
  34.1 3.4 %collective-permute-start = (f32[4,4,32,256]{3,2,1,0:T(8,128)S(1)}, f32[4,4,32,256]{3,2,1,0:T(8,128)S(1)}, u32[]{:S(2)}, u32[]{:S(2)}) collective-permute-start(f32[4,4,32,256]{3,2,1,0:T(8,128)S(1)} %all_to_all.35.own), channel_id=1, source_target_pairs={{0,16},{16,0},{1,17},{17,1},{2,18},{18,2},{3,19},{19,3},{4,20},{20... | collective-permute-start | bytes 1572872 | tf_op jit(solution)/shard_map/ppermute | solution.py:229
  39.3 34.9 %copy-start.4 = (s32[2,4]{1,0:T(2,128)S(1)}, s32[2,4]{1,0:T(2,128)}, u32[]{:S(2)}) copy-start(s32[2,4]{1,0:T(2,128)} %bounds.3) | copy-start | bytes 100
  75.3 42.8 %copy-start.2 = (f32[2,256,256]{2,1,0:T(8,128)S(1)}, f32[2,256,256]{2,1,0:T(8,128)}, u32[]{:S(2)}) copy-start(f32[2,256,256]{2,1,0:T(8,128)} %terms.1) | copy-start | bytes 1572868
  112.6 5.5 %collective-permute-start.1 = (f32[4,32,256]{2,1,0:T(8,128)S(1)}, f32[4,32,256]{2,1,0:T(8,128)S(1)}, u32[]{:S(2)}, u32[]{:S(2)}) collective-permute-start(f32[4,32,256]{2,1,0:T(8,128)S(1)} %all_to_all.40.own), channel_id=1, source_target_pairs={{0,16},{16,0},{1,17},{17,1},{2,18},{18,2},{3,19},{19,3},{4,20},{20... | collective-permute-start | bytes 393224 | tf_op jit(solution)/shard_map/ppermute | solution.py:229

commit v4 on v3

--- a/solution.py
+++ b/solution.py
@@ -32,7 +32,7 @@
     return mm(ah, bh) + (mm(ah, bl) + mm(al, bh))
 
 
-def pack_kernel(fb, w, out, tab, sems):
+def pack_kernel(fb, w, out, sems):
     r = lax.axis_index("y") * 2 + lax.axis_index("core")
     z, x = lax.axis_index("z"), lax.axis_index("x")
     c = z * 4 + x
@@ -60,8 +60,41 @@
                 w.at[f, named, part // 4, part % 4, pl.ds(row, 16)],
                 out.at[d // 2, d % 2, 64 + 16 * f : 80 + 16 * f],
             )
+    for copy in copies:
+        copy.wait()
+
+
+def pick_kernel(tab, inc, slices, mine):
+    for f in range(2):
+        for t in range(2):
+            p = tab[16 * f + 8 + t]
+            v = inc[p >> 2, 32 * f : 32 * f + 32, :]
+            for d in range(4):
+                slices[d, 2 * f + t] = v
+        for s in range(4):
+            p = tab[16 * f + s]
+            mine[4 * f + s] = inc[p >> 2, 64 + 16 * f : 80 + 16 * f, :]
+
+
+def same_node(bounds, f):
+    a = lax.broadcasted_iota(jnp.int32, (256, 256), 0)
+    b = lax.broadcasted_iota(jnp.int32, (256, 256), 1)
+    ia = jnp.zeros((256, 256), jnp.int32)
+    ib = jnp.zeros((256, 256), jnp.int32)
+    end = jnp.int32(0)
+    for k in range(4):
+        end = end + bounds[f, k]
+        ia = ia + (a >= end).astype(jnp.int32)
+        ib = ib + (b >= end).astype(jnp.int32)
+    return ia == ib
+
+
+def tile_kernel(fb, bounds, terms, inverse, hi, lo, tab, mask, base, tiles, sems):
+    r = lax.axis_index("y") * 2 + lax.axis_index("core")
+    c = lax.axis_index("z") * 4 + lax.axis_index("x")
     for k in range(32):
         tab[k] = 0
+    copies = []
     for f in range(2):
         rows = jnp.int32(0)
         cols = jnp.int32(0)
@@ -71,25 +104,6 @@
             rows = rows + ((b >> 3) == r).astype(jnp.int32)
             tab[16 * f + 8 + cols] = p
             cols = cols + ((b >> 2) == c).astype(jnp.int32)
-    for copy in copies:
-        copy.wait()
-
-
-def pick_kernel(tab, inc, after, slices, mine):
-    for f in range(2):
-        for t in range(2):
-            p = tab[16 * f + 8 + t]
-            v = inc[p >> 2, 32 * f : 32 * f + 32, :]
-            for d in range(4):
-                slices[d, 2 * f + t] = v
-        for s in range(4):
-            p = tab[16 * f + s]
-            mine[4 * f + s] = inc[p >> 2, 64 + 16 * f : 80 + 16 * f, :]
-
-
-def tile_kernel(fb, tab, inverse, hi, lo, tiles, sems):
-    copies = []
-    for f in range(2):
         for s in range(4):
             for t in range(2):
                 k = (4 * f + s) * 2 + t
@@ -102,6 +116,10 @@
                 copy = pltpu.make_async_copy(src, tiles.at[k], sems.at[k])
                 copy.start()
                 copies.append(copy)
+    for f in range(2):
+        same = same_node(bounds, f)
+        mask[f] = same.astype(F32)
+        base[f] = jnp.where(same, terms[f], 0.0)
     for k in range(16):
         copies[k].wait()
         h, l = split(tiles[k])
@@ -126,20 +144,7 @@
                 out[d, 4 * f + s] = total[at : at + 16, :]
 
 
-def same_node(bounds, f):
-    a = lax.broadcasted_iota(jnp.int32, (256, 256), 0)
-    b = lax.broadcasted_iota(jnp.int32, (256, 256), 1)
-    ia = jnp.zeros((256, 256), jnp.int32)
-    ib = jnp.zeros((256, 256), jnp.int32)
-    end = jnp.int32(0)
-    for k in range(4):
-        end = end + bounds[f, k]
-        ia = ia + (a >= end).astype(jnp.int32)
-        ib = ib + (b >= end).astype(jnp.int32)
-    return ia == ib
-
-
-def reduce_kernel(tab, bounds, parts, mine, out):
+def reduce_kernel(tab, mask, parts, mine, out):
     for d in range(8):
         out[d, 0:32] = jnp.zeros((32, 256), F32)
     for f in range(2):
@@ -153,30 +158,23 @@
         left = mine[4 * f : 4 * f + 4].reshape(64, 256)
         right = jnp.concatenate(rows, axis=0)
         full = dot3(split(left), split(right), ((0,), (0,)))
-        full = jnp.where(same_node(bounds, f), full, 0.0)
+        full = full * mask[f]
         packed = full[:, :128] + full[:, 128:]
         for d in range(4):
             part = packed[64 * d : 64 * d + 64]
             out[4 * f + d, 32:64] = jnp.concatenate([part[:32], part[32:]], axis=1)
 
 
-def place_kernel(fb, inc, route, share):
+def place_kernel(fb, inc, out):
     r = lax.axis_index("y") * 2 + lax.axis_index("core")
     total = inc[0, 32:64]
     for d in range(1, 8):
         total = total + inc[d, 32:64]
     for d in range(4):
-        share[d] = total
+        out[d, 32:64] = total
     for f in range(2):
         for i in range(4):
-            route[i, 16 * f : 16 * f + 16] = inc[fb[f, 4 * r + i] >> 3, 16 * f : 16 * f + 16, :]
-
-
-def join_kernel(route, share, out):
-    total = (share[0] + share[1]) + (share[2] + share[3])
-    for d in range(4):
-        out[d, 0:32] = route[d]
-        out[d, 32:64] = total
+            out[i, 16 * f : 16 * f + 16] = inc[fb[f, 4 * r + i] >> 3, 16 * f : 16 * f + 16, :]
 
 
 def border_kernel(inc, border, out):
@@ -184,23 +182,27 @@
         for f in range(2):
             border[f, 16 * z : 16 * z + 16] = inc[z, 16 * f : 16 * f + 16, :]
     total = (inc[0, 32:64] + inc[1, 32:64]) + (inc[2, 32:64] + inc[3, 32:64])
-    for d in range(4):
+    for d in range(16):
         out[d] = total
 
 
-def finish_kernel(bounds, own, other, terms, out, chunks):
+def chunk_kernel(inc, out):
+    for y in range(4):
+        at = 4 * y
+        out[y] = (inc[at] + inc[at + 1]) + (inc[at + 2] + inc[at + 3])
+
+
+def finish_kernel(own, other, mask, base, out, chunks):
     core = lax.axis_index("core")
     for y in range(4):
         chunks[2 * y + core] = own[y]
         chunks[2 * y + 1 - core] = other[y]
     for f in range(2):
-        same = same_node(bounds, f)
         for d in range(4):
             v = chunks[4 * f + d]
             v = jnp.concatenate([v[:, :128], v[:, 128:]], axis=0)
             at = slice(64 * d, 64 * d + 64)
-            full = terms[f, at] + jnp.concatenate([v, v], axis=1)
-            out[f, at] = jnp.where(same[at], full, 0.0)
+            out[f, at] = base[f, at] + mask[f, at] * jnp.concatenate([v, v], axis=1)
 
 
 def call(kernel, ins, out_shape, out_specs=None, scratch=(), limit=40, cost=None):
@@ -230,25 +232,31 @@
 
 
 def body(inverse, fb, panels, terms, bounds):
-    outgoing, tab = call(
+    outgoing = call(
         pack_kernel,
         [SMEM, ANY],
-        (sds((4, 2, 96, 256)), sds((32,), jnp.int32)),
-        (VMEM, SMEM),
+        sds((4, 2, 96, 256)),
         scratch=[pltpu.SemaphoreType.DMA((20,))],
     )(hbm(fb), hbm(panels.reshape(2, 4, 2, 4, 32, 256)))
     incoming = a2a(outgoing.reshape(8, 96, 256), ROW)
-    hi, lo = call(
+    hi, lo, tab, mask, base = call(
         tile_kernel,
-        [SMEM, SMEM, ANY],
-        (sds((8, 256, 512), BF16), sds((8, 256, 512), BF16)),
+        [SMEM, SMEM, VMEM, ANY],
+        (
+            sds((8, 256, 512), BF16),
+            sds((8, 256, 512), BF16),
+            sds((32,), jnp.int32),
+            sds((2, 256, 256)),
+            sds((2, 256, 256)),
+        ),
+        (VMEM, VMEM, SMEM, VMEM, VMEM),
         scratch=[pltpu.VMEM((16, 256, 256), F32), pltpu.SemaphoreType.DMA((16,))],
         limit=24,
         cost=pl.CostEstimate(flops=4 * MIB, bytes_accessed=12 * MIB, transcendentals=0),
-    )(fb, tab, hbm(inverse))
+    )(fb, bounds, terms, hbm(inverse))
     slices, mine = call(
-        pick_kernel, [SMEM, VMEM, ANY], (sds((4, 4, 32, 256)), sds((8, 16, 256)))
-    )(tab, incoming, hi)
+        pick_kernel, [SMEM, VMEM], (sds((4, 4, 32, 256)), sds((8, 16, 256)))
+    )(tab, incoming)
     own = a2a(slices, "y")
     other = swap(own)
     parts = call(
@@ -258,21 +266,20 @@
         scratch=[pltpu.VMEM((2, 512, 256), F32)],
     )(hi, lo, own, other)
     parts = a2a(parts, COL)
-    v = call(reduce_kernel, [SMEM, SMEM, VMEM, VMEM], sds((8, 64, 256)))(tab, bounds, parts, mine)
+    v = call(reduce_kernel, [SMEM, VMEM, VMEM, VMEM], sds((8, 64, 256)))(tab, mask, parts, mine)
     v = a2a(v, ROW)
-    route, v = call(place_kernel, [SMEM, VMEM], (sds((4, 32, 256)), sds((4, 32, 256))))(fb, v)
-    v = a2a(v, "x")
-    v = call(join_kernel, [VMEM, VMEM], sds((4, 64, 256)))(route, v)
+    v = call(place_kernel, [SMEM, VMEM], sds((4, 64, 256)))(fb, v)
     v = a2a(v, "z")
-    border, v = call(border_kernel, [VMEM], (sds((2, 64, 256)), sds((4, 32, 256))))(v)
-    own = a2a(v, "y")
+    border, v = call(border_kernel, [VMEM], (sds((2, 64, 256)), sds((16, 32, 256))))(v)
+    v = a2a(v, ("y", "x"))
+    own = call(chunk_kernel, [VMEM], sds((4, 32, 256)))(v)
     other = swap(own)
     diag = call(
         finish_kernel,
-        [SMEM, VMEM, VMEM, VMEM],
+        [VMEM, VMEM, VMEM, VMEM],
         sds((2, 256, 256)),
         scratch=[pltpu.VMEM((8, 32, 256), F32)],
-    )(bounds, own, other, terms)
+    )(own, other, mask, base)
     return border, diag
 
 

time: 120 us -> 117 us (0.975)
  local copies, waits for them, and re-layouts: 1.34 us -> 4.75 us
  waiting for transfers between devices: 10.6 us -> 7.96 us
  blocking collectives: 82.1 us -> 79.5 us
  starting transfers between devices: 12.3 us -> 11.1 us
    unnamed x10 -> x14, local copies, waits for them, and re-layouts: 1.34 us -> 4.75 us
    all_to_all x1, waiting for transfers between devices: 8.04 us -> 5.44 us  [a2a(): return lax.all_to_all(v, axes, 0, 0, tiled=True)]
    all_to_all x6 -> x5, blocking collectives: 82.1 us -> 79.5 us  [a2a(): return lax.all_to_all(v, axes, 0, 0, tiled=True)]
    ppermute x2, starting transfers between devices: 6.32 us -> 5.09 us  [swap(): return lax.ppermute(v, 'core', [(0, 1), (1, 0)])]
  transfers between devices with their start and end apart: 3 -> 3, of which waited for: 3 -> 3; matrix products, arithmetic and copies ran while one was open for 0% -> 0% of each run, Pallas kernels for 2% -> 3%
where the time goes in v4:
time: 117 us; the launch traced here: 116 us
  blocking collectives  79.5 us (68%)
  Pallas kernels  12.4 us (11%)
  starting transfers between devices  11.1 us (9%)
  waiting for transfers between devices  7.96 us (7%)
  local copies, waits for them, and re-layouts  4.75 us (4%)
    all_to_all x5, blocking collectives, a2a(): return lax.all_to_all(v, axes, 0, 0, tiled=True)  79.5 us
    all_to_all x1, starting transfers between devices, a2a(): return lax.all_to_all(v, axes, 0, 0, tiled=True)  5.98 us
    all_to_all x1, waiting for transfers between devices, a2a(): return lax.all_to_all(v, axes, 0, 0, tiled=True)  5.44 us
    ppermute x2, starting transfers between devices, swap(): return lax.ppermute(v, 'core', [(0, 1), (1, 0)])  5.09 us
    unnamed x14, local copies, waits for them, and re-layouts  4.75 us
    pallas_call x1, Pallas kernels, body(): call(tile_kernel, [SMEM, SMEM, VMEM, ANY], (sds((8, 256, 512), BF16), sds...  3.67 us
    pallas_call x1, Pallas kernels, body(): call(pack_kernel, [SMEM, ANY], sds((4, 2, 96, 256)), scratch=[pltpu.Semap...  3.14 us
    ppermute x2, waiting for transfers between devices, swap(): return lax.ppermute(v, 'core', [(0, 1), (1, 0)])  2.52 us
  transfers between devices with their start and end apart: 3, of which 3 were waited for; matrix products, arithmetic and copies ran while one was open for 0% of the time, Pallas kernels for 3%

profile of v4, /device:TPU:1, one launch (start us, length us, event | category | flops | bytes accessed | tf_op | source)
XLA Modules:
  0.0 116.5 jit_solution(7257114118352269011)
XLA Ops:
  0.6 0.0 copy-start.5
  0.6 0.0 copy-start.6
  0.7 3.1 %shard_map.69 = f32[4,2,96,256]{3,2,1,0:T(8,128)} custom-call(s32[2,32]{1,0:T(2,128)} %fb.5, f32[2,4,2,4,32,256]{5,4,3,2,1,0:T(8,128)} %bitcast.2), custom_call_target="tpu_custom_call" | custom-call | tf_op jit(solution)/shard_map/pallas_call | solution.py:235
  3.8 6.0 %all-to-all-start = ((f32[8,96,256]{2,1,0:T(8,128)}), f32[8,96,256]{2,1,0:T(8,128)S(1)}, u32[]{:S(2)}, u32[]{:S(2)}) async-start(f32[8,96,256]{2,1,0:T(8,128)} %bitcast.1), calls=%async_computation | async-start | bytes 1572864 | tf_op jit(solution)/shard_map/all_to_all | solution.py:223
  9.8 0.0 copy-done.5
  9.8 0.0 copy-done.6
  9.8 0.0 copy-start.2
  9.8 1.0 copy-done.2
  10.8 3.7 %shard_map.68 = (bf16[8,256,512]{2,1,0:T(8,128)(2,1)S(1)}, bf16[8,256,512]{2,1,0:T(8,128)(2,1)S(1)}, s32[32]{0:T(128)S(1)}, f32[2,256,256]{2,1,0:T(8,128)S(1)}, f32[2,256,256]{2,1,0:T(8,128)S(1)}) custom-call(s32[2,32]{1,0:T(2,128)S(1)} %copy-done.5, s32[2,4]{1,0:T(2,128)S(1)} %copy-done.6, f32[2,256,256]{2,1,0:T(8,128)S(1)} %copy-done.2, f32[2048,1024]{1,0:T(8,128)} %inverse.1), custom_call_target="tpu_custom_call" | custom-call | flops 4194304 | bytes 12582912 | tf_op jit(solution)/shard_map/pallas_call | solution.py:242
  14.5 0.0 copy-start
  14.5 1.3 %copy-done = bf16[8,256,512]{2,1,0:T(8,128)(2,1)} copy-done((bf16[8,256,512]{2,1,0:T(8,128)(2,1)}, bf16[8,256,512]{2,1,0:T(8,128)(2,1)S(1)}, u32[]{:S(2)}) %copy-start) | copy-done | bytes 2097176
  15.8 0.0 copy-start.3
  15.8 0.8 copy-done.3
  16.6 5.4 %all-to-all-done.inc = f32[8,96,256]{2,1,0:T(8,128)S(1)} async-done(((f32[8,96,256]{2,1,0:T(8,128)}), f32[8,96,256]{2,1,0:T(8,128)S(1)}, u32[]{:S(2)}, u32[]{:S(2)}) %all-to-all-start) | async-done | bytes 786464 | tf_op jit(solution)/shard_map/all_to_all | solution.py:223
  22.1 0.6 shard_map.70
  22.7 11.0 %all_to_all.30.own = f32[4,4,32,256]{3,2,1,0:T(8,128)S(1)} all-to-all(f32[4,4,32,256]{3,2,1,0:T(8,128)S(1)} %get-tuple-element.15), channel_id=1, replica_groups=mesh['y'=4,'core'=2,'z'=4,'x'=4] {'y'}, dimensions={0} | all-to-all | bytes 1048576 | tf_op jit(solution)/shard_map/all_to_all | solution.py:223
  33.7 1.8 %collective-permute-start = (f32[4,4,32,256]{3,2,1,0:T(8,128)S(1)}, f32[4,4,32,256]{3,2,1,0:T(8,128)S(1)}, u32[]{:S(2)}, u32[]{:S(2)}) collective-permute-start(f32[4,4,32,256]{3,2,1,0:T(8,128)S(1)} %all_to_all.30.own), channel_id=1, source_target_pairs={{0,16},{16,0},{1,17},{17,1},{2,18},{18,2},{3,19},{19,3},{4,20},{20... | collective-permute-start | bytes 1572872 | tf_op jit(solution)/shard_map/ppermute | solution.py:231
  35.5 1.5 %collective-permute-done.other = f32[4,4,32,256]{3,2,1,0:T(8,128)S(1)} collective-permute-done((f32[4,4,32,256]{3,2,1,0:T(8,128)S(1)}, f32[4,4,32,256]{3,2,1,0:T(8,128)S(1)}, u32[]{:S(2)}, u32[]{:S(2)}) %collective-permute-start) | collective-permute-done | bytes 524320 | tf_op jit(solution)/shard_map/ppermute | solution.py:231
  37.0 0.0 copy-start.1
  37.0 1.6 %copy-done.1 = bf16[8,256,512]{2,1,0:T(8,128)(2,1)S(1)} copy-done((bf16[8,256,512]{2,1,0:T(8,128)(2,1)S(1)}, bf16[8,256,512]{2,1,0:T(8,128)(2,1)}, u32[]{:S(2)}) %copy-start.1) | copy-done | bytes 2097176
  38.6 1.9 %shard_map.71 = f32[16,8,16,256]{3,2,1,0:T(8,128)S(1)} custom-call(bf16[8,256,512]{2,1,0:T(8,128)(2,1)S(1)} %get-tuple-element.13.hi, bf16[8,256,512]{2,1,0:T(8,128)(2,1)S(1)} %copy-done.1, f32[4,4,32,256]{3,2,1,0:T(8,128)S(1)} %all_to_all.30.own, f32[4,4,32,256]{3,2,1,0:T(8,128)S(1)} %collective-permute-done.other), custom_call_target="tpu_custom_call" | custom-call | tf_op jit(solution)/shard_map/pallas_call | solution.py:262
  40.5 35.0 %all_to_all.31.parts = f32[16,8,16,256]{3,2,1,0:T(8,128)S(1)} all-to-all(f32[16,8,16,256]{3,2,1,0:T(8,128)S(1)} %shard_map.71), channel_id=1, replica_groups=mesh['y'=4,'core'=2,'z'=4,'x'=4] {'z','x'}, dimensions={0} | all-to-all | bytes 4194304 | tf_op jit(solution)/shard_map/all_to_all | solution.py:223
  75.5 1.0 shard_map.72
  76.5 0.0 copy-start.4
  76.5 13.7 %all_to_all.32.inc = f32[8,64,256]{2,1,0:T(8,128)S(1)} all-to-all(f32[8,64,256]{2,1,0:T(8,128)S(1)} %shard_map.72), channel_id=1, replica_groups=mesh['y'=4,'core'=2,'z'=4,'x'=4] {'y','core'}, dimensions={0} | all-to-all | bytes 1048576 | tf_op jit(solution)/shard_map/all_to_all | solution.py:223
  90.2 0.6 shard_map.73
  90.8 7.9 %all_to_all.33.inc = f32[4,64,256]{2,1,0:T(8,128)S(1)} all-to-all(f32[4,64,256]{2,1,0:T(8,128)S(1)} %shard_map.73), channel_id=1, replica_groups=mesh['y'=4,'core'=2,'z'=4,'x'=4] {'z'}, dimensions={0} | all-to-all | bytes 524288 | tf_op jit(solution)/shard_map/all_to_all | solution.py:223
  98.7 0.7 shard_map.74
  99.4 11.9 %all_to_all.34.inc = f32[16,32,256]{2,1,0:T(8,128)S(1)} all-to-all(f32[16,32,256]{2,1,0:T(8,128)S(1)} %get-tuple-element.18), channel_id=1, replica_groups=mesh['y'=4,'core'=2,'z'=4,'x'=4] {'y','x'}, dimensions={0} | all-to-all | bytes 1048576 | tf_op jit(solution)/shard_map/all_to_all | solution.py:223
  111.3 3.3 %collective-permute-start.1 = (f32[4,32,256]{2,1,0:T(8,128)S(1)}, f32[4,32,256]{2,1,0:T(8,128)S(1)}, u32[]{:S(2)}, u32[]{:S(2)}) collective-permute-start(f32[4,32,256]{2,1,0:T(8,128)S(1)} %shard_map.75.own), channel_id=1, source_target_pairs={{0,16},{16,0},{1,17},{17,1},{2,18},{18,2},{3,19},{19,3},{4,20},{20... | collective-permute-start | bytes 393224 | tf_op jit(solution)/shard_map/ppermute | solution.py:231
  114.6 1.0 collective-permute-done.1.other
  115.6 0.0 copy-done.4
  115.6 0.9 shard_map.76
  (1 shorter events, 0.0 us)
Async XLA Ops:
  0.6 9.2 %copy-start.5 = (s32[2,32]{1,0:T(2,128)S(1)}, s32[2,32]{1,0:T(2,128)}, u32[]{:S(2)}) copy-start(s32[2,32]{1,0:T(2,128)} %fb.5) | copy-start | bytes 772
  0.6 9.1 %copy-start.6 = (s32[2,4]{1,0:T(2,128)S(1)}, s32[2,4]{1,0:T(2,128)}, u32[]{:S(2)}) copy-start(s32[2,4]{1,0:T(2,128)} %bounds.1) | copy-start | bytes 100
  3.8 18.3 %all-to-all-start = ((f32[8,96,256]{2,1,0:T(8,128)}), f32[8,96,256]{2,1,0:T(8,128)S(1)}, u32[]{:S(2)}, u32[]{:S(2)}) async-start(f32[8,96,256]{2,1,0:T(8,128)} %bitcast.1), calls=%async_computation | async-start | bytes 1572864 | tf_op jit(solution)/shard_map/all_to_all | solution.py:223
  9.8 1.0 copy-start.2
  14.5 1.3 %copy-start = (bf16[8,256,512]{2,1,0:T(8,128)(2,1)}, bf16[8,256,512]{2,1,0:T(8,128)(2,1)S(1)}, u32[]{:S(2)}) copy-start(bf16[8,256,512]{2,1,0:T(8,128)(2,1)S(1)} %get-tuple-element.14.lo) | copy-start | bytes 6291460
  15.8 0.8 copy-start.3
  33.7 3.4 %collective-permute-start = (f32[4,4,32,256]{3,2,1,0:T(8,128)S(1)}, f32[4,4,32,256]{3,2,1,0:T(8,128)S(1)}, u32[]{:S(2)}, u32[]{:S(2)}) collective-permute-start(f32[4,4,32,256]{3,2,1,0:T(8,128)S(1)} %all_to_all.30.own), channel_id=1, source_target_pairs={{0,16},{16,0},{1,17},{17,1},{2,18},{18,2},{3,19},{19,3},{4,20},{20... | collective-permute-start | bytes 1572872 | tf_op jit(solution)/shard_map/ppermute | solution.py:231
  37.0 1.6 %copy-start.1 = (bf16[8,256,512]{2,1,0:T(8,128)(2,1)S(1)}, bf16[8,256,512]{2,1,0:T(8,128)(2,1)}, u32[]{:S(2)}) copy-start(bf16[8,256,512]{2,1,0:T(8,128)(2,1)} %copy-done) | copy-start | bytes 6291460
  76.5 39.1 %copy-start.4 = (f32[2,256,256]{2,1,0:T(8,128)S(1)}, f32[2,256,256]{2,1,0:T(8,128)}, u32[]{:S(2)}) copy-start(f32[2,256,256]{2,1,0:T(8,128)} %copy-done.3) | copy-start | bytes 1572868
  111.3 4.2 %collective-permute-start.1 = (f32[4,32,256]{2,1,0:T(8,128)S(1)}, f32[4,32,256]{2,1,0:T(8,128)S(1)}, u32[]{:S(2)}, u32[]{:S(2)}) collective-permute-start(f32[4,32,256]{2,1,0:T(8,128)S(1)} %shard_map.75.own), channel_id=1, source_target_pairs={{0,16},{16,0},{1,17},{17,1},{2,18},{18,2},{3,19},{19,3},{4,20},{20... | collective-permute-start | bytes 393224 | tf_op jit(solution)/shard_map/ppermute | solution.py:231

commit v5 on v4

--- a/solution.py
+++ b/solution.py
@@ -144,9 +144,11 @@
                 out[d, 4 * f + s] = total[at : at + 16, :]
 
 
-def reduce_kernel(tab, mask, parts, mine, out):
-    for d in range(8):
-        out[d, 0:32] = jnp.zeros((32, 256), F32)
+def reduce_kernel(tab, mask, parts, mine, keep, send):
+    core = lax.axis_index("core")
+    for ref in (keep, send):
+        for d in range(4):
+            ref[d, 0:32] = jnp.zeros((32, 256), F32)
     for f in range(2):
         rows = []
         for s in range(4):
@@ -154,27 +156,55 @@
             for d in range(1, 16):
                 v = v + parts[d, 4 * f + s]
             rows.append(v)
-            out[tab[16 * f + s] >> 2, 16 * f : 16 * f + 16] = -v
+            owner = tab[16 * f + s] >> 2
+
+            @pl.when((owner & 1) == core)
+            def _():
+                keep[owner >> 1, 16 * f : 16 * f + 16] = -v
+
+            @pl.when((owner & 1) != core)
+            def _():
+                send[owner >> 1, 16 * f : 16 * f + 16] = -v
+
         left = mine[4 * f : 4 * f + 4].reshape(64, 256)
         right = jnp.concatenate(rows, axis=0)
         full = dot3(split(left), split(right), ((0,), (0,)))
         full = full * mask[f]
         packed = full[:, :128] + full[:, 128:]
+        chunks = []
         for d in range(4):
             part = packed[64 * d : 64 * d + 64]
-            out[4 * f + d, 32:64] = jnp.concatenate([part[:32], part[32:]], axis=1)
+            chunks.append(jnp.concatenate([part[:32], part[32:]], axis=1))
+
+        @pl.when(core == f)
+        def _():
+            for d in range(4):
+                keep[d, 32:64] = chunks[d]
+
+        @pl.when(core != f)
+        def _():
+            for d in range(4):
+                send[d, 32:64] = chunks[d]
+
+
+def join_kernel(keep, got, out):
+    for d in range(4):
+        out[d, 0:32] = keep[d, 0:32]
+        out[d, 32:64] = got[d, 0:32]
+        out[d, 64:96] = keep[d, 32:64] + got[d, 32:64]
 
 
 def place_kernel(fb, inc, out):
-    r = lax.axis_index("y") * 2 + lax.axis_index("core")
-    total = inc[0, 32:64]
-    for d in range(1, 8):
-        total = total + inc[d, 32:64]
+    core = lax.axis_index("core")
+    r = lax.axis_index("y") * 2 + core
+    total = (inc[0, 64:96] + inc[1, 64:96]) + (inc[2, 64:96] + inc[3, 64:96])
     for d in range(4):
         out[d, 32:64] = total
     for f in range(2):
         for i in range(4):
-            out[i, 16 * f : 16 * f + 16] = inc[fb[f, 4 * r + i] >> 3, 16 * f : 16 * f + 16, :]
+            source = fb[f, 4 * r + i] >> 3
+            at = pl.multiple_of(32 * ((source & 1) ^ core) + 16 * f, 16)
+            out[i, 16 * f : 16 * f + 16] = inc[source >> 1, pl.ds(at, 16), :]
 
 
 def border_kernel(inc, border, out):
@@ -192,20 +222,18 @@
         out[y] = (inc[at] + inc[at + 1]) + (inc[at + 2] + inc[at + 3])
 
 
-def finish_kernel(own, other, mask, base, out, chunks):
+def finish_kernel(own, other, mask, base, out):
     core = lax.axis_index("core")
-    for y in range(4):
-        chunks[2 * y + core] = own[y]
-        chunks[2 * y + 1 - core] = other[y]
-    for f in range(2):
+    for rel, chunks in enumerate((own, other)):
+        f = core ^ rel
         for d in range(4):
-            v = chunks[4 * f + d]
+            v = chunks[d]
             v = jnp.concatenate([v[:, :128], v[:, 128:]], axis=0)
             at = slice(64 * d, 64 * d + 64)
             out[f, at] = base[f, at] + mask[f, at] * jnp.concatenate([v, v], axis=1)
 
 
-def call(kernel, ins, out_shape, out_specs=None, scratch=(), limit=40, cost=None):
+def call(kernel, ins, out_shape, out_specs=None, scratch=(), limit=8, cost=None):
     if out_specs is None:
         out_specs = jax.tree.map(lambda _: VMEM, out_shape)
     return pl.pallas_call(
@@ -251,7 +279,7 @@
         ),
         (VMEM, VMEM, SMEM, VMEM, VMEM),
         scratch=[pltpu.VMEM((16, 256, 256), F32), pltpu.SemaphoreType.DMA((16,))],
-        limit=24,
+        limit=16,
         cost=pl.CostEstimate(flops=4 * MIB, bytes_accessed=12 * MIB, transcendentals=0),
     )(fb, bounds, terms, hbm(inverse))
     slices, mine = call(
@@ -264,10 +292,14 @@
         [VMEM, VMEM, VMEM, VMEM],
         sds((16, 8, 16, 256)),
         scratch=[pltpu.VMEM((2, 512, 256), F32)],
+        limit=16,
     )(hi, lo, own, other)
     parts = a2a(parts, COL)
-    v = call(reduce_kernel, [SMEM, VMEM, VMEM, VMEM], sds((8, 64, 256)))(tab, mask, parts, mine)
-    v = a2a(v, ROW)
+    keep, send = call(
+        reduce_kernel, [SMEM, VMEM, VMEM, VMEM], (sds((4, 64, 256)), sds((4, 64, 256)))
+    )(tab, mask, parts, mine)
+    v = call(join_kernel, [VMEM, VMEM], sds((4, 96, 256)))(keep, swap(send))
+    v = a2a(v, "y")
     v = call(place_kernel, [SMEM, VMEM], sds((4, 64, 256)))(fb, v)
     v = a2a(v, "z")
     border, v = call(border_kernel, [VMEM], (sds((2, 64, 256)), sds((16, 32, 256))))(v)
@@ -278,7 +310,6 @@
         finish_kernel,
         [VMEM, VMEM, VMEM, VMEM],
         sds((2, 256, 256)),
-        scratch=[pltpu.VMEM((8, 32, 256), F32)],
     )(own, other, mask, base)
     return border, diag
 

time: 117 us -> 117 us (level)
  blocking collectives: 79.5 us -> 76.2 us
  starting transfers between devices: 11.1 us -> 13.1 us
    all_to_all x5, blocking collectives: 79.5 us -> 76.2 us  [a2a(): return lax.all_to_all(v, axes, 0, 0, tiled=True)]
    ppermute x2 -> x3, starting transfers between devices: 5.09 us -> 7.1 us  [swap(): return lax.ppermute(v, 'core', [(0, 1), (1, 0)])]
    ppermute x2 -> x3, waiting for transfers between devices: 2.52 us -> 3.69 us  [swap(): return lax.ppermute(v, 'core', [(0, 1), (1, 0)])]
    pallas_call x2 -> x3, Pallas kernels: 1.87 us -> 2.38 us  [the longest x1 1.49 us: body(): call(reduce_kernel, [SMEM, VMEM, VMEM, VMEM], (sds((4, 64, 256)), sds((4,...]
  transfers between devices with their start and end apart: 3 -> 4, of which waited for: 3 -> 4; matrix products, arithmetic and copies ran while one was open for 0% -> 0% of each run, Pallas kernels for 3% -> 3%
where the time goes in v5:
time: 117 us
  blocking collectives  76.2 us (65%)
  starting transfers between devices  13.1 us (11%)
  Pallas kernels  13 us (11%)
  waiting for transfers between devices  9.11 us (8%)
  local copies, waits for them, and re-layouts  4.76 us (4%)
    all_to_all x5, blocking collectives, a2a(): return lax.all_to_all(v, axes, 0, 0, tiled=True)  76.2 us
    ppermute x3, starting transfers between devices, swap(): return lax.ppermute(v, 'core', [(0, 1), (1, 0)])  7.1 us
    all_to_all x1, starting transfers between devices, a2a(): return lax.all_to_all(v, axes, 0, 0, tiled=True)  5.98 us
    all_to_all x1, waiting for transfers between devices, a2a(): return lax.all_to_all(v, axes, 0, 0, tiled=True)  5.43 us
    unnamed x14, local copies, waits for them, and re-layouts  4.76 us
    ppermute x3, waiting for transfers between devices, swap(): return lax.ppermute(v, 'core', [(0, 1), (1, 0)])  3.69 us
    pallas_call x1, Pallas kernels, body(): call(tile_kernel, [SMEM, SMEM, VMEM, ANY], (sds((8, 256, 512), BF16), sds...  3.67 us
    pallas_call x1, Pallas kernels, body(): call(pack_kernel, [SMEM, ANY], sds((4, 2, 96, 256)), scratch=[pltpu.Semap...  3.15 us
  transfers between devices with their start and end apart: 4, of which 4 were waited for; matrix products, arithmetic and copies ran while one was open for 0% of the time, Pallas kernels for 3%

profile of v5, /device:TPU:1, one launch (start us, length us, event | category | flops | bytes accessed | tf_op | source)
XLA Modules:
  0.0 116.8 jit_solution(12170648841294735014)
XLA Ops:
  0.6 0.0 copy-start.5
  0.6 0.0 copy-start.6
  0.7 3.1 %shard_map.69 = f32[4,2,96,256]{3,2,1,0:T(8,128)} custom-call(s32[2,32]{1,0:T(2,128)} %fb.5, f32[2,4,2,4,32,256]{5,4,3,2,1,0:T(8,128)} %bitcast.2), custom_call_target="tpu_custom_call" | custom-call | tf_op jit(solution)/shard_map/pallas_call | solution.py:263
  3.8 6.0 %all-to-all-start = ((f32[8,96,256]{2,1,0:T(8,128)}), f32[8,96,256]{2,1,0:T(8,128)S(1)}, u32[]{:S(2)}, u32[]{:S(2)}) async-start(f32[8,96,256]{2,1,0:T(8,128)} %bitcast.1), calls=%async_computation | async-start | bytes 1572864 | tf_op jit(solution)/shard_map/all_to_all | solution.py:251
  9.8 0.0 copy-done.5
  9.8 0.0 copy-done.6
  9.8 0.0 copy-start.2
  9.8 1.0 copy-done.2
  10.8 3.7 %shard_map.68 = (bf16[8,256,512]{2,1,0:T(8,128)(2,1)S(1)}, bf16[8,256,512]{2,1,0:T(8,128)(2,1)S(1)}, s32[32]{0:T(128)S(1)}, f32[2,256,256]{2,1,0:T(8,128)S(1)}, f32[2,256,256]{2,1,0:T(8,128)S(1)}) custom-call(s32[2,32]{1,0:T(2,128)S(1)} %copy-done.5, s32[2,4]{1,0:T(2,128)S(1)} %copy-done.6, f32[2,256,256]{2,1,0:T(8,128)S(1)} %copy-done.2, f32[2048,1024]{1,0:T(8,128)} %inverse.1), custom_call_target="tpu_custom_call" | custom-call | flops 4194304 | bytes 12582912 | tf_op jit(solution)/shard_map/pallas_call | solution.py:270
  14.5 0.0 copy-start
  14.5 1.3 %copy-done = bf16[8,256,512]{2,1,0:T(8,128)(2,1)} copy-done((bf16[8,256,512]{2,1,0:T(8,128)(2,1)}, bf16[8,256,512]{2,1,0:T(8,128)(2,1)S(1)}, u32[]{:S(2)}) %copy-start) | copy-done | bytes 2097176
  15.9 0.0 copy-start.3
  15.9 0.8 copy-done.3
  16.7 5.4 %all-to-all-done.inc = f32[8,96,256]{2,1,0:T(8,128)S(1)} async-done(((f32[8,96,256]{2,1,0:T(8,128)}), f32[8,96,256]{2,1,0:T(8,128)S(1)}, u32[]{:S(2)}, u32[]{:S(2)}) %all-to-all-start) | async-done | bytes 786464 | tf_op jit(solution)/shard_map/all_to_all | solution.py:251
  22.1 0.6 shard_map.70
  22.7 11.0 %all_to_all.30.own = f32[4,4,32,256]{3,2,1,0:T(8,128)S(1)} all-to-all(f32[4,4,32,256]{3,2,1,0:T(8,128)S(1)} %get-tuple-element.17), channel_id=1, replica_groups=mesh['y'=4,'core'=2,'z'=4,'x'=4] {'y'}, dimensions={0} | all-to-all | bytes 1048576 | tf_op jit(solution)/shard_map/all_to_all | solution.py:251
  33.7 1.8 %collective-permute-start = (f32[4,4,32,256]{3,2,1,0:T(8,128)S(1)}, f32[4,4,32,256]{3,2,1,0:T(8,128)S(1)}, u32[]{:S(2)}, u32[]{:S(2)}) collective-permute-start(f32[4,4,32,256]{3,2,1,0:T(8,128)S(1)} %all_to_all.30.own), channel_id=1, source_target_pairs={{0,16},{16,0},{1,17},{17,1},{2,18},{18,2},{3,19},{19,3},{4,20},{20... | collective-permute-start | bytes 1572872 | tf_op jit(solution)/shard_map/ppermute | solution.py:259
  35.5 1.5 %collective-permute-done.other = f32[4,4,32,256]{3,2,1,0:T(8,128)S(1)} collective-permute-done((f32[4,4,32,256]{3,2,1,0:T(8,128)S(1)}, f32[4,4,32,256]{3,2,1,0:T(8,128)S(1)}, u32[]{:S(2)}, u32[]{:S(2)}) %collective-permute-start) | collective-permute-done | bytes 524320 | tf_op jit(solution)/shard_map/ppermute | solution.py:259
  37.0 0.0 copy-start.1
  37.0 1.6 %copy-done.1 = bf16[8,256,512]{2,1,0:T(8,128)(2,1)S(1)} copy-done((bf16[8,256,512]{2,1,0:T(8,128)(2,1)S(1)}, bf16[8,256,512]{2,1,0:T(8,128)(2,1)}, u32[]{:S(2)}) %copy-start.1) | copy-done | bytes 2097176
  38.6 1.9 %shard_map.71 = f32[16,8,16,256]{3,2,1,0:T(8,128)S(1)} custom-call(bf16[8,256,512]{2,1,0:T(8,128)(2,1)S(1)} %get-tuple-element.15.hi, bf16[8,256,512]{2,1,0:T(8,128)(2,1)S(1)} %copy-done.1, f32[4,4,32,256]{3,2,1,0:T(8,128)S(1)} %all_to_all.30.own, f32[4,4,32,256]{3,2,1,0:T(8,128)S(1)} %collective-permute-done.other), custom_call_target="tpu_custom_call" | custom-call | tf_op jit(solution)/shard_map/pallas_call | solution.py:290
  40.5 35.0 %all_to_all.31.parts = f32[16,8,16,256]{3,2,1,0:T(8,128)S(1)} all-to-all(f32[16,8,16,256]{3,2,1,0:T(8,128)S(1)} %shard_map.71), channel_id=1, replica_groups=mesh['y'=4,'core'=2,'z'=4,'x'=4] {'z','x'}, dimensions={0} | all-to-all | bytes 4194304 | tf_op jit(solution)/shard_map/all_to_all | solution.py:251
  75.5 1.5 %shard_map.72 = (f32[4,64,256]{2,1,0:T(8,128)S(1)}, f32[4,64,256]{2,1,0:T(8,128)S(1)}) custom-call(s32[32]{0:T(128)S(1)} %get-tuple-element.13.tab, f32[2,256,256]{2,1,0:T(8,128)S(1)} %get-tuple-element.14.mask, f32[16,8,16,256]{3,2,1,0:T(8,128)S(1)} %all_to_all.31.parts, f32[8,16,256]{2,1,0:T(8,128)S(1)} %get-tuple-element.18.mine), custom_call_target="tpu_custom_call" | custom-call | tf_op jit(solution)/shard_map/pallas_call | solution.py:298
  77.0 1.9 %collective-permute-start.1 = (f32[4,64,256]{2,1,0:T(8,128)S(1)}, f32[4,64,256]{2,1,0:T(8,128)S(1)}, u32[]{:S(2)}, u32[]{:S(2)}) collective-permute-start(f32[4,64,256]{2,1,0:T(8,128)S(1)} %get-tuple-element.20), channel_id=1, source_target_pairs={{0,16},{16,0},{1,17},{17,1},{2,18},{18,2},{3,19},{19,3},{4,20},{20... | collective-permute-start | bytes 786440 | tf_op jit(solution)/shard_map/ppermute | solution.py:259
  78.8 1.2 collective-permute-done.1.got
  80.0 0.0 copy-start.4
  80.1 10.4 %all_to_all.32.inc = f32[4,96,256]{2,1,0:T(8,128)S(1)} all-to-all(f32[4,96,256]{2,1,0:T(8,128)S(1)} %shard_map.73), channel_id=1, replica_groups=mesh['y'=4,'core'=2,'z'=4,'x'=4] {'y'}, dimensions={0} | all-to-all | bytes 786432 | tf_op jit(solution)/shard_map/all_to_all | solution.py:251
  90.4 0.6 shard_map.74
  91.0 7.9 %all_to_all.33.inc = f32[4,64,256]{2,1,0:T(8,128)S(1)} all-to-all(f32[4,64,256]{2,1,0:T(8,128)S(1)} %shard_map.74), channel_id=1, replica_groups=mesh['y'=4,'core'=2,'z'=4,'x'=4] {'z'}, dimensions={0} | all-to-all | bytes 524288 | tf_op jit(solution)/shard_map/all_to_all | solution.py:251
  98.9 0.7 shard_map.75
  99.6 11.9 %all_to_all.34.inc = f32[16,32,256]{2,1,0:T(8,128)S(1)} all-to-all(f32[16,32,256]{2,1,0:T(8,128)S(1)} %get-tuple-element.22), channel_id=1, replica_groups=mesh['y'=4,'core'=2,'z'=4,'x'=4] {'y','x'}, dimensions={0} | all-to-all | bytes 1048576 | tf_op jit(solution)/shard_map/all_to_all | solution.py:251
  111.6 3.4 %collective-permute-start.2 = (f32[4,32,256]{2,1,0:T(8,128)S(1)}, f32[4,32,256]{2,1,0:T(8,128)S(1)}, u32[]{:S(2)}, u32[]{:S(2)}) collective-permute-start(f32[4,32,256]{2,1,0:T(8,128)S(1)} %shard_map.76.own), channel_id=1, source_target_pairs={{0,16},{16,0},{1,17},{17,1},{2,18},{18,2},{3,19},{19,3},{4,20},{20... | collective-permute-start | bytes 393224 | tf_op jit(solution)/shard_map/ppermute | solution.py:259
  115.0 1.0 collective-permute-done.2.other
  116.0 0.0 copy-done.4
  116.0 0.9 shard_map.77
  (2 shorter events, 0.1 us)
Async XLA Ops:
  0.6 9.2 %copy-start.5 = (s32[2,32]{1,0:T(2,128)S(1)}, s32[2,32]{1,0:T(2,128)}, u32[]{:S(2)}) copy-start(s32[2,32]{1,0:T(2,128)} %fb.5) | copy-start | bytes 772
  0.6 9.2 %copy-start.6 = (s32[2,4]{1,0:T(2,128)S(1)}, s32[2,4]{1,0:T(2,128)}, u32[]{:S(2)}) copy-start(s32[2,4]{1,0:T(2,128)} %bounds.1) | copy-start | bytes 100
  3.8 18.3 %all-to-all-start = ((f32[8,96,256]{2,1,0:T(8,128)}), f32[8,96,256]{2,1,0:T(8,128)S(1)}, u32[]{:S(2)}, u32[]{:S(2)}) async-start(f32[8,96,256]{2,1,0:T(8,128)} %bitcast.1), calls=%async_computation | async-start | bytes 1572864 | tf_op jit(solution)/shard_map/all_to_all | solution.py:251
  9.8 1.0 copy-start.2
  14.5 1.3 %copy-start = (bf16[8,256,512]{2,1,0:T(8,128)(2,1)}, bf16[8,256,512]{2,1,0:T(8,128)(2,1)S(1)}, u32[]{:S(2)}) copy-start(bf16[8,256,512]{2,1,0:T(8,128)(2,1)S(1)} %get-tuple-element.16.lo) | copy-start | bytes 6291460
  15.9 0.8 copy-start.3
  33.7 3.4 %collective-permute-start = (f32[4,4,32,256]{3,2,1,0:T(8,128)S(1)}, f32[4,4,32,256]{3,2,1,0:T(8,128)S(1)}, u32[]{:S(2)}, u32[]{:S(2)}) collective-permute-start(f32[4,4,32,256]{3,2,1,0:T(8,128)S(1)} %all_to_all.30.own), channel_id=1, source_target_pairs={{0,16},{16,0},{1,17},{17,1},{2,18},{18,2},{3,19},{19,3},{4,20},{20... | collective-permute-start | bytes 1572872 | tf_op jit(solution)/shard_map/ppermute | solution.py:259
  37.0 1.6 %copy-start.1 = (bf16[8,256,512]{2,1,0:T(8,128)(2,1)S(1)}, bf16[8,256,512]{2,1,0:T(8,128)(2,1)}, u32[]{:S(2)}) copy-start(bf16[8,256,512]{2,1,0:T(8,128)(2,1)} %copy-done) | copy-start | bytes 6291460
  77.0 3.0 %collective-permute-start.1 = (f32[4,64,256]{2,1,0:T(8,128)S(1)}, f32[4,64,256]{2,1,0:T(8,128)S(1)}, u32[]{:S(2)}, u32[]{:S(2)}) collective-permute-start(f32[4,64,256]{2,1,0:T(8,128)S(1)} %get-tuple-element.20), channel_id=1, source_target_pairs={{0,16},{16,0},{1,17},{17,1},{2,18},{18,2},{3,19},{19,3},{4,20},{20... | collective-permute-start | bytes 786440 | tf_op jit(solution)/shard_map/ppermute | solution.py:259
  80.0 35.9 %copy-start.4 = (f32[2,256,256]{2,1,0:T(8,128)S(1)}, f32[2,256,256]{2,1,0:T(8,128)}, u32[]{:S(2)}) copy-start(f32[2,256,256]{2,1,0:T(8,128)} %copy-done.3) | copy-start | bytes 1572868
  111.6 4.4 %collective-permute-start.2 = (f32[4,32,256]{2,1,0:T(8,128)S(1)}, f32[4,32,256]{2,1,0:T(8,128)S(1)}, u32[]{:S(2)}, u32[]{:S(2)}) collective-permute-start(f32[4,32,256]{2,1,0:T(8,128)S(1)} %shard_map.76.own), channel_id=1, source_target_pairs={{0,16},{16,0},{1,17},{17,1},{2,18},{18,2},{3,19},{19,3},{4,20},{20... | collective-permute-start | bytes 393224 | tf_op jit(solution)/shard_map/ppermute | solution.py:259

commit v6 on v4

--- a/solution.py
+++ b/solution.py
@@ -127,8 +127,13 @@
         lo[k // 2, :, 256 * (k % 2) : 256 * (k % 2) + 256] = l
 
 
-def product_kernel(hi, lo, own, other, out, whole):
+def product_kernel(hi, lo, own, other, out, whole, high, sems):
     core = lax.axis_index("core")
+    copies = []
+    for k in range(8):
+        copy = pltpu.make_async_copy(hi.at[k], high.at[k], sems.at[k])
+        copy.start()
+        copies.append(copy)
     for k in range(4):
         base = 256 * (k % 2)
         at = pl.multiple_of(base + 128 * core, 128)
@@ -138,10 +143,20 @@
     for f in range(2):
         w = split(whole[f])
         for s in range(4):
-            total = dot3((hi[4 * f + s], lo[4 * f + s]), w, ((1,), (0,)))
-            for d in range(16):
-                at = 64 * (d % 4) + 16 * (d // 4)
-                out[d, 4 * f + s] = total[at : at + 16, :]
+            copies[4 * f + s].wait()
+            total = dot3((high[4 * f + s], lo[4 * f + s]), w, ((1,), (0,)))
+            for x in range(4):
+                for z in range(4):
+                    at = 64 * x + 16 * z
+                    first = jnp.where(core == 0, x, z)
+                    second = jnp.where(core == 0, z, x)
+                    out[first, second, 4 * f + s] = total[at : at + 16, :]
+
+
+def half_kernel(inc, out):
+    for d in range(4):
+        for k in range(8):
+            out[d, k] = (inc[0, d, k] + inc[1, d, k]) + (inc[2, d, k] + inc[3, d, k])
 
 
 def reduce_kernel(tab, mask, parts, mine, out):
@@ -150,9 +165,8 @@
     for f in range(2):
         rows = []
         for s in range(4):
-            v = parts[0, 4 * f + s]
-            for d in range(1, 16):
-                v = v + parts[d, 4 * f + s]
+            k = 4 * f + s
+            v = (parts[0, k] + parts[1, k]) + (parts[2, k] + parts[3, k])
             rows.append(v)
             out[tab[16 * f + s] >> 2, 16 * f : 16 * f + 16] = -v
         left = mine[4 * f : 4 * f + 4].reshape(64, 256)
@@ -205,7 +219,7 @@
             out[f, at] = base[f, at] + mask[f, at] * jnp.concatenate([v, v], axis=1)
 
 
-def call(kernel, ins, out_shape, out_specs=None, scratch=(), limit=40, cost=None):
+def call(kernel, ins, out_shape, out_specs=None, scratch=(), limit=8, cost=None):
     if out_specs is None:
         out_specs = jax.tree.map(lambda _: VMEM, out_shape)
     return pl.pallas_call(
@@ -223,6 +237,16 @@
     return lax.all_to_all(v, axes, 0, 0, tiled=True)
 
 
+def grouped(v, stage):
+    groups = []
+    for line in range(8):
+        for o in range(4):
+            along_x = [16 * line + 4 * o + i for i in range(4)]
+            along_z = [16 * line + 4 * i + o for i in range(4)]
+            groups.append(along_x if line % 2 == stage else along_z)
+    return lax.all_to_all(v, ALL, 0, 0, tiled=True, axis_index_groups=groups)
+
+
 def hbm(v):
     return pltpu.with_memory_space_constraint(v, pltpu.HBM)
 
@@ -236,6 +260,7 @@
         pack_kernel,
         [SMEM, ANY],
         sds((4, 2, 96, 256)),
+        ANY,
         scratch=[pltpu.SemaphoreType.DMA((20,))],
     )(hbm(fb), hbm(panels.reshape(2, 4, 2, 4, 32, 256)))
     incoming = a2a(outgoing.reshape(8, 96, 256), ROW)
@@ -251,7 +276,7 @@
         ),
         (VMEM, VMEM, SMEM, VMEM, VMEM),
         scratch=[pltpu.VMEM((16, 256, 256), F32), pltpu.SemaphoreType.DMA((16,))],
-        limit=24,
+        limit=16,
         cost=pl.CostEstimate(flops=4 * MIB, bytes_accessed=12 * MIB, transcendentals=0),
     )(fb, bounds, terms, hbm(inverse))
     slices, mine = call(
@@ -261,11 +286,18 @@
     other = swap(own)
     parts = call(
         product_kernel,
-        [VMEM, VMEM, VMEM, VMEM],
-        sds((16, 8, 16, 256)),
-        scratch=[pltpu.VMEM((2, 512, 256), F32)],
-    )(hi, lo, own, other)
-    parts = a2a(parts, COL)
+        [ANY, VMEM, VMEM, VMEM],
+        sds((4, 4, 8, 16, 256)),
+        scratch=[
+            pltpu.VMEM((2, 512, 256), F32),
+            pltpu.VMEM((8, 256, 512), BF16),
+            pltpu.SemaphoreType.DMA((8,)),
+        ],
+        limit=16,
+    )(hbm(hi), lo, own, other)
+    parts = grouped(parts, 0)
+    parts = call(half_kernel, [VMEM], sds((4, 8, 16, 256)))(parts)
+    parts = grouped(parts, 1)
     v = call(reduce_kernel, [SMEM, VMEM, VMEM, VMEM], sds((8, 64, 256)))(tab, mask, parts, mine)
     v = a2a(v, ROW)
     v = call(place_kernel, [SMEM, VMEM], sds((4, 64, 256)))(fb, v)

time: 117 us -> 139 us (1.19)
  Pallas kernels: 12.4 us -> 38.9 us
  blocking collectives: 79.5 us -> 77 us
  local copies, waits for them, and re-layouts: 4.75 us -> 3.17 us
    all_to_all x5 -> x4, blocking collectives: 79.5 us -> 46 us  [a2a(): return lax.all_to_all(v, axes, 0, 0, tiled=True)]
    all_to_all x0 -> x2, blocking collectives: none -> 30.9 us  [grouped(): return lax.all_to_all(v, ALL, 0, 0, tiled=True, axis_index_groups=groups)]
    pallas_call x2 -> x3, Pallas kernels: 5.01 us -> 31.5 us  [the longest x1 25.9 us: body(): call(pack_kernel, [SMEM, ANY], sds((4, 2, 96, 256)), ANY, scratch=[pltpu....]
    unnamed x14 -> x12, local copies, waits for them, and re-layouts: 4.75 us -> 3.17 us
where the time goes in v6:
time: 139 us
  blocking collectives  77 us (55%)
  Pallas kernels  38.9 us (28%)
  starting transfers between devices  11.1 us (8%)
  waiting for transfers between devices  7.95 us (6%)
  local copies, waits for them, and re-layouts  3.17 us (2%)
    all_to_all x4, blocking collectives, a2a(): return lax.all_to_all(v, axes, 0, 0, tiled=True)  46 us
    all_to_all x2, blocking collectives, grouped(): return lax.all_to_all(v, ALL, 0, 0, tiled=True, axis_index_groups=groups)  30.9 us
    pallas_call x1, Pallas kernels, body(): call(pack_kernel, [SMEM, ANY], sds((4, 2, 96, 256)), ANY, scratch=[pltpu....  25.9 us
    all_to_all x1, starting transfers between devices, a2a(): return lax.all_to_all(v, axes, 0, 0, tiled=True)  5.98 us
    pallas_call x1, Pallas kernels, body(): call(product_kernel, [ANY, VMEM, VMEM, VMEM], sds((4, 4, 8, 16, 256)), sc...  5.47 us
    all_to_all x1, waiting for transfers between devices, a2a(): return lax.all_to_all(v, axes, 0, 0, tiled=True)  5.43 us
    ppermute x2, starting transfers between devices, swap(): return lax.ppermute(v, 'core', [(0, 1), (1, 0)])  5.14 us
    pallas_call x1, Pallas kernels, body(): call(tile_kernel, [SMEM, SMEM, VMEM, ANY], (sds((8, 256, 512), BF16), sds...  3.67 us
  transfers between devices with their start and end apart: 3, of which 3 were waited for; matrix products, arithmetic and copies ran while one was open for 0% of the time, Pallas kernels for 3%

profile of v6, /device:TPU:1, one launch (start us, length us, event | category | flops | bytes accessed | tf_op | source)
XLA Modules:
  0.0 138.9 jit_solution(15412055175477675535)
XLA Ops:
  0.6 0.0 copy-start.4
  0.6 0.0 copy-start.5
  0.7 25.9 %shard_map.69 = f32[4,2,96,256]{3,2,1,0:T(8,128)} custom-call(s32[2,32]{1,0:T(2,128)} %fb.5, f32[2,4,2,4,32,256]{5,4,3,2,1,0:T(8,128)} %bitcast.2), custom_call_target="tpu_custom_call" | custom-call | tf_op jit(solution)/shard_map/pallas_call | solution.py:259
  26.6 6.0 %all-to-all-start = ((f32[8,96,256]{2,1,0:T(8,128)}), f32[8,96,256]{2,1,0:T(8,128)S(1)}, u32[]{:S(2)}, u32[]{:S(2)}) async-start(f32[8,96,256]{2,1,0:T(8,128)} %bitcast.1), calls=%async_computation | async-start | bytes 1572864 | tf_op jit(solution)/shard_map/all_to_all | solution.py:237
  32.6 0.0 copy-done.4
  32.6 0.0 copy-done.5
  32.6 0.0 copy-start.1
  32.6 1.0 copy-done.1
  33.6 3.7 %shard_map.68 = (bf16[8,256,512]{2,1,0:T(8,128)(2,1)S(1)}, bf16[8,256,512]{2,1,0:T(8,128)(2,1)S(1)}, s32[32]{0:T(128)S(1)}, f32[2,256,256]{2,1,0:T(8,128)S(1)}, f32[2,256,256]{2,1,0:T(8,128)S(1)}) custom-call(s32[2,32]{1,0:T(2,128)S(1)} %copy-done.4, s32[2,4]{1,0:T(2,128)S(1)} %copy-done.5, f32[2,256,256]{2,1,0:T(8,128)S(1)} %copy-done.1, f32[2048,1024]{1,0:T(8,128)} %inverse.1), custom_call_target="tpu_custom_call" | custom-call | flops 4194304 | bytes 12582912 | tf_op jit(solution)/shard_map/pallas_call | solution.py:267
  37.3 0.0 copy-start
  37.3 1.3 copy-done
  38.7 0.0 copy-start.2
  38.7 0.8 copy-done.2
  39.4 5.4 %all-to-all-done.inc = f32[8,96,256]{2,1,0:T(8,128)S(1)} async-done(((f32[8,96,256]{2,1,0:T(8,128)}), f32[8,96,256]{2,1,0:T(8,128)S(1)}, u32[]{:S(2)}, u32[]{:S(2)}) %all-to-all-start) | async-done | bytes 786464 | tf_op jit(solution)/shard_map/all_to_all | solution.py:237
  44.9 0.6 shard_map.70
  45.5 11.0 %all_to_all.35.own = f32[4,4,32,256]{3,2,1,0:T(8,128)S(1)} all-to-all(f32[4,4,32,256]{3,2,1,0:T(8,128)S(1)} %get-tuple-element.15), channel_id=1, replica_groups=mesh['y'=4,'core'=2,'z'=4,'x'=4] {'y'}, dimensions={0} | all-to-all | bytes 1048576 | tf_op jit(solution)/shard_map/all_to_all | solution.py:237
  56.5 1.8 %collective-permute-start = (f32[4,4,32,256]{3,2,1,0:T(8,128)S(1)}, f32[4,4,32,256]{3,2,1,0:T(8,128)S(1)}, u32[]{:S(2)}, u32[]{:S(2)}) collective-permute-start(f32[4,4,32,256]{3,2,1,0:T(8,128)S(1)} %all_to_all.35.own), channel_id=1, source_target_pairs={{0,16},{16,0},{1,17},{17,1},{2,18},{18,2},{3,19},{19,3},{4,20},{20... | collective-permute-start | bytes 1572872 | tf_op jit(solution)/shard_map/ppermute | solution.py:255
  58.3 1.5 %collective-permute-done.other = f32[4,4,32,256]{3,2,1,0:T(8,128)S(1)} collective-permute-done((f32[4,4,32,256]{3,2,1,0:T(8,128)S(1)}, f32[4,4,32,256]{3,2,1,0:T(8,128)S(1)}, u32[]{:S(2)}, u32[]{:S(2)}) %collective-permute-start) | collective-permute-done | bytes 524320 | tf_op jit(solution)/shard_map/ppermute | solution.py:255
  59.8 5.5 %shard_map.71 = f32[4,4,8,16,256]{4,3,2,1,0:T(8,128)S(1)} custom-call(bf16[8,256,512]{2,1,0:T(8,128)(2,1)} %copy-done, bf16[8,256,512]{2,1,0:T(8,128)(2,1)S(1)} %get-tuple-element.14.lo, f32[4,4,32,256]{3,2,1,0:T(8,128)S(1)} %all_to_all.35.own, f32[4,4,32,256]{3,2,1,0:T(8,128)S(1)} %collective-permute-done.other), custom_call_target="tpu_custom_call" | custom-call | tf_op jit(solution)/shard_map/pallas_call | solution.py:287
  65.3 20.5 %all_to_all.36.inc = f32[4,4,8,16,256]{4,3,2,1,0:T(8,128)S(1)} all-to-all(f32[4,4,8,16,256]{4,3,2,1,0:T(8,128)S(1)} %shard_map.71), channel_id=1, replica_groups={{0,1,2,3},{4,5,6,7},{8,9,10,11},{12,13,14,15},{16,20,24,28},{17,21,25,2..., dimensions={0} | all-to-all | bytes 4194304 | tf_op jit(solution)/shard_map/all_to_all | solution.py:247
  85.8 0.1 shard_map.72
  85.9 10.5 %all_to_all.37.parts = f32[4,8,16,256]{3,2,1,0:T(8,128)S(1)} all-to-all(f32[4,8,16,256]{3,2,1,0:T(8,128)S(1)} %shard_map.72), channel_id=1, replica_groups={{0,4,8,12},{1,5,9,13},{2,6,10,14},{3,7,11,15},{16,17,18,19},{20,21,22,2..., dimensions={0} | all-to-all | bytes 1048576 | tf_op jit(solution)/shard_map/all_to_all | solution.py:247
  96.4 0.9 shard_map.73
  97.3 0.0 copy-start.3
  97.3 15.1 %all_to_all.38.inc = f32[8,64,256]{2,1,0:T(8,128)S(1)} all-to-all(f32[8,64,256]{2,1,0:T(8,128)S(1)} %shard_map.73), channel_id=1, replica_groups=mesh['y'=4,'core'=2,'z'=4,'x'=4] {'y','core'}, dimensions={0} | all-to-all | bytes 1048576 | tf_op jit(solution)/shard_map/all_to_all | solution.py:237
  112.5 0.6 shard_map.74
  113.0 7.9 %all_to_all.39.inc = f32[4,64,256]{2,1,0:T(8,128)S(1)} all-to-all(f32[4,64,256]{2,1,0:T(8,128)S(1)} %shard_map.74), channel_id=1, replica_groups=mesh['y'=4,'core'=2,'z'=4,'x'=4] {'z'}, dimensions={0} | all-to-all | bytes 524288 | tf_op jit(solution)/shard_map/all_to_all | solution.py:237
  121.0 0.7 shard_map.75
  121.7 12.0 %all_to_all.40.inc = f32[16,32,256]{2,1,0:T(8,128)S(1)} all-to-all(f32[16,32,256]{2,1,0:T(8,128)S(1)} %get-tuple-element.18), channel_id=1, replica_groups=mesh['y'=4,'core'=2,'z'=4,'x'=4] {'y','x'}, dimensions={0} | all-to-all | bytes 1048576 | tf_op jit(solution)/shard_map/all_to_all | solution.py:237
  133.7 3.3 %collective-permute-start.1 = (f32[4,32,256]{2,1,0:T(8,128)S(1)}, f32[4,32,256]{2,1,0:T(8,128)S(1)}, u32[]{:S(2)}, u32[]{:S(2)}) collective-permute-start(f32[4,32,256]{2,1,0:T(8,128)S(1)} %shard_map.76.own), channel_id=1, source_target_pairs={{0,16},{16,0},{1,17},{17,1},{2,18},{18,2},{3,19},{19,3},{4,20},{20... | collective-permute-start | bytes 393224 | tf_op jit(solution)/shard_map/ppermute | solution.py:255
  137.0 1.0 collective-permute-done.1.other
  138.0 0.0 copy-done.3
  138.0 0.9 shard_map.77
  (1 shorter events, 0.0 us)
Async XLA Ops:
  0.6 32.0 %copy-start.4 = (s32[2,32]{1,0:T(2,128)S(1)}, s32[2,32]{1,0:T(2,128)}, u32[]{:S(2)}) copy-start(s32[2,32]{1,0:T(2,128)} %fb.5) | copy-start | bytes 772
  0.6 32.0 %copy-start.5 = (s32[2,4]{1,0:T(2,128)S(1)}, s32[2,4]{1,0:T(2,128)}, u32[]{:S(2)}) copy-start(s32[2,4]{1,0:T(2,128)} %bounds.1) | copy-start | bytes 100
  26.6 18.3 %all-to-all-start = ((f32[8,96,256]{2,1,0:T(8,128)}), f32[8,96,256]{2,1,0:T(8,128)S(1)}, u32[]{:S(2)}, u32[]{:S(2)}) async-start(f32[8,96,256]{2,1,0:T(8,128)} %bitcast.1), calls=%async_computation | async-start | bytes 1572864 | tf_op jit(solution)/shard_map/all_to_all | solution.py:237
  32.6 1.0 copy-start.1
  37.3 1.3 copy-start
  38.7 0.8 copy-start.2
  56.5 3.4 %collective-permute-start = (f32[4,4,32,256]{3,2,1,0:T(8,128)S(1)}, f32[4,4,32,256]{3,2,1,0:T(8,128)S(1)}, u32[]{:S(2)}, u32[]{:S(2)}) collective-permute-start(f32[4,4,32,256]{3,2,1,0:T(8,128)S(1)} %all_to_all.35.own), channel_id=1, source_target_pairs={{0,16},{16,0},{1,17},{17,1},{2,18},{18,2},{3,19},{19,3},{4,20},{20... | collective-permute-start | bytes 1572872 | tf_op jit(solution)/shard_map/ppermute | solution.py:255
  97.3 40.7 %copy-start.3 = (f32[2,256,256]{2,1,0:T(8,128)S(1)}, f32[2,256,256]{2,1,0:T(8,128)}, u32[]{:S(2)}) copy-start(f32[2,256,256]{2,1,0:T(8,128)} %copy-done.2) | copy-start | bytes 1572868
  133.7 4.3 %collective-permute-start.1 = (f32[4,32,256]{2,1,0:T(8,128)S(1)}, f32[4,32,256]{2,1,0:T(8,128)S(1)}, u32[]{:S(2)}, u32[]{:S(2)}) collective-permute-start(f32[4,32,256]{2,1,0:T(8,128)S(1)} %shard_map.76.own), channel_id=1, source_target_pairs={{0,16},{16,0},{1,17},{17,1},{2,18},{18,2},{3,19},{19,3},{4,20},{20... | collective-permute-start | bytes 393224 | tf_op jit(solution)/shard_map/ppermute | solution.py:255

commit v7 on v6

--- a/solution.py
+++ b/solution.py
@@ -89,12 +89,32 @@
     return ia == ib
 
 
-def tile_kernel(fb, bounds, terms, inverse, hi, lo, tab, mask, base, tiles, sems):
+def fetch_tiles(f, fb, tab, inverse, hi, lo, tiles, sems):
+    copies = []
+    for s in range(4):
+        for t in range(2):
+            k = 2 * s + t
+            rb = fb[f, tab[16 * f + s]] & 7
+            cb = fb[f, tab[16 * f + 8 + t]] & 3
+            src = inverse.at[
+                pl.ds(pl.multiple_of(rb * 256, 256), 256),
+                pl.ds(pl.multiple_of(cb * 256, 256), 256),
+            ]
+            copy = pltpu.make_async_copy(src, tiles.at[k], sems.at[k])
+            copy.start()
+            copies.append(copy)
+    for k in range(8):
+        copies[k].wait()
+        h, l = split(tiles[k])
+        hi[k // 2, :, 256 * (k % 2) : 256 * (k % 2) + 256] = h
+        lo[k // 2, :, 256 * (k % 2) : 256 * (k % 2) + 256] = l
+
+
+def first_kernel(fb, bounds, inverse, hi, lo, tab, mask, tiles, sems):
     r = lax.axis_index("y") * 2 + lax.axis_index("core")
     c = lax.axis_index("z") * 4 + lax.axis_index("x")
     for k in range(32):
         tab[k] = 0
-    copies = []
     for f in range(2):
         rows = jnp.int32(0)
         cols = jnp.int32(0)
@@ -104,36 +124,17 @@
             rows = rows + ((b >> 3) == r).astype(jnp.int32)
             tab[16 * f + 8 + cols] = p
             cols = cols + ((b >> 2) == c).astype(jnp.int32)
-        for s in range(4):
-            for t in range(2):
-                k = (4 * f + s) * 2 + t
-                rb = fb[f, tab[16 * f + s]] & 7
-                cb = fb[f, tab[16 * f + 8 + t]] & 3
-                src = inverse.at[
-                    pl.ds(pl.multiple_of(rb * 256, 256), 256),
-                    pl.ds(pl.multiple_of(cb * 256, 256), 256),
-                ]
-                copy = pltpu.make_async_copy(src, tiles.at[k], sems.at[k])
-                copy.start()
-                copies.append(copy)
-    for f in range(2):
-        same = same_node(bounds, f)
-        mask[f] = same.astype(F32)
-        base[f] = jnp.where(same, terms[f], 0.0)
-    for k in range(16):
-        copies[k].wait()
-        h, l = split(tiles[k])
-        hi[k // 2, :, 256 * (k % 2) : 256 * (k % 2) + 256] = h
-        lo[k // 2, :, 256 * (k % 2) : 256 * (k % 2) + 256] = l
-
-
-def product_kernel(hi, lo, own, other, out, whole, high, sems):
+    for f in range(2):
+        mask[f] = same_node(bounds, f).astype(F32)
+    fetch_tiles(0, fb, tab, inverse, hi, lo, tiles, sems)
+
+
+def second_kernel(fb, tab, inverse, after, hi, lo, tiles, sems):
+    fetch_tiles(1, fb, tab, inverse, hi, lo, tiles, sems)
+
+
+def product_kernel(hi0, lo0, hi1, lo1, own, other, out, whole):
     core = lax.axis_index("core")
-    copies = []
-    for k in range(8):
-        copy = pltpu.make_async_copy(hi.at[k], high.at[k], sems.at[k])
-        copy.start()
-        copies.append(copy)
     for k in range(4):
         base = 256 * (k % 2)
         at = pl.multiple_of(base + 128 * core, 128)
@@ -142,9 +143,9 @@
         whole[k // 2, pl.ds(at, 128), :] = other[:, k].reshape(128, 256)
     for f in range(2):
         w = split(whole[f])
+        hi, lo = ((hi0, lo0), (hi1, lo1))[f]
         for s in range(4):
-            copies[4 * f + s].wait()
-            total = dot3((high[4 * f + s], lo[4 * f + s]), w, ((1,), (0,)))
+            total = dot3((hi[s], lo[s]), w, ((1,), (0,)))
             for x in range(4):
                 for z in range(4):
                     at = 64 * x + 16 * z
@@ -206,7 +207,7 @@
         out[y] = (inc[at] + inc[at + 1]) + (inc[at + 2] + inc[at + 3])
 
 
-def finish_kernel(own, other, mask, base, out, chunks):
+def finish_kernel(own, other, mask, terms, out, chunks):
     core = lax.axis_index("core")
     for y in range(4):
         chunks[2 * y + core] = own[y]
@@ -216,7 +217,7 @@
             v = chunks[4 * f + d]
             v = jnp.concatenate([v[:, :128], v[:, 128:]], axis=0)
             at = slice(64 * d, 64 * d + 64)
-            out[f, at] = base[f, at] + mask[f, at] * jnp.concatenate([v, v], axis=1)
+            out[f, at] = mask[f, at] * (terms[f, at] + jnp.concatenate([v, v], axis=1))
 
 
 def call(kernel, ins, out_shape, out_specs=None, scratch=(), limit=8, cost=None):
@@ -260,41 +261,36 @@
         pack_kernel,
         [SMEM, ANY],
         sds((4, 2, 96, 256)),
-        ANY,
         scratch=[pltpu.SemaphoreType.DMA((20,))],
     )(hbm(fb), hbm(panels.reshape(2, 4, 2, 4, 32, 256)))
     incoming = a2a(outgoing.reshape(8, 96, 256), ROW)
-    hi, lo, tab, mask, base = call(
-        tile_kernel,
-        [SMEM, SMEM, VMEM, ANY],
-        (
-            sds((8, 256, 512), BF16),
-            sds((8, 256, 512), BF16),
-            sds((32,), jnp.int32),
-            sds((2, 256, 256)),
-            sds((2, 256, 256)),
-        ),
-        (VMEM, VMEM, SMEM, VMEM, VMEM),
-        scratch=[pltpu.VMEM((16, 256, 256), F32), pltpu.SemaphoreType.DMA((16,))],
+    tiles = (sds((4, 256, 512), BF16), sds((4, 256, 512), BF16))
+    buffers = [pltpu.VMEM((8, 256, 256), F32), pltpu.SemaphoreType.DMA((8,))]
+    cost = pl.CostEstimate(flops=2 * MIB, bytes_accessed=6 * MIB, transcendentals=0)
+    hi0, lo0, tab, mask = call(
+        first_kernel,
+        [SMEM, SMEM, ANY],
+        (*tiles, sds((32,), jnp.int32), sds((2, 256, 256))),
+        (VMEM, VMEM, SMEM, VMEM),
+        scratch=buffers,
         limit=16,
-        cost=pl.CostEstimate(flops=4 * MIB, bytes_accessed=12 * MIB, transcendentals=0),
-    )(fb, bounds, terms, hbm(inverse))
+        cost=cost,
+    )(fb, bounds, hbm(inverse))
     slices, mine = call(
         pick_kernel, [SMEM, VMEM], (sds((4, 4, 32, 256)), sds((8, 16, 256)))
     )(tab, incoming)
     own = a2a(slices, "y")
     other = swap(own)
+    hi1, lo1 = call(
+        second_kernel, [SMEM, SMEM, ANY, ANY], tiles, scratch=buffers, limit=16, cost=cost
+    )(fb, tab, hbm(inverse), own)
     parts = call(
         product_kernel,
-        [ANY, VMEM, VMEM, VMEM],
+        [VMEM] * 6,
         sds((4, 4, 8, 16, 256)),
-        scratch=[
-            pltpu.VMEM((2, 512, 256), F32),
-            pltpu.VMEM((8, 256, 512), BF16),
-            pltpu.SemaphoreType.DMA((8,)),
-        ],
+        scratch=[pltpu.VMEM((2, 512, 256), F32)],
         limit=16,
-    )(hbm(hi), lo, own, other)
+    )(hi0, lo0, hi1, lo1, own, other)
     parts = grouped(parts, 0)
     parts = call(half_kernel, [VMEM], sds((4, 8, 16, 256)))(parts)
     parts = grouped(parts, 1)
@@ -311,7 +307,7 @@
         [VMEM, VMEM, VMEM, VMEM],
         sds((2, 256, 256)),
         scratch=[pltpu.VMEM((8, 32, 256), F32)],
-    )(own, other, mask, base)
+    )(own, other, mask, terms)
     return border, diag
 
 

time: 139 us -> 113 us (0.81)
  Pallas kernels: 38.9 us -> 14.1 us
  local copies, waits for them, and re-layouts: 3.17 us -> 0.01 us
  waiting for transfers between devices: 7.95 us -> 10.2 us
    pallas_call x3 -> x4, Pallas kernels: 35.1 us -> 10.3 us  [the longest x1 3.13 us: body(): call(pack_kernel, [SMEM, ANY], sds((4, 2, 96, 256)), scratch=[pltpu.Semap...]
    all_to_all x1, waiting for transfers between devices: 5.43 us -> 9.19 us  [a2a(): return lax.all_to_all(v, axes, 0, 0, tiled=True)]
    unnamed x12 -> x6, local copies, waits for them, and re-layouts: 3.17 us -> 0.01 us
    ppermute x2, waiting for transfers between devices: 2.52 us -> 0.99 us  [swap(): return lax.ppermute(v, 'core', [(0, 1), (1, 0)])]
  transfers between devices with their start and end apart: 3 -> 3, of which waited for: 3 -> 2; matrix products, arithmetic and copies ran while one was open for 0% -> 0% of each run, Pallas kernels for 3% -> 5%
where the time goes in v7:
time: 113 us
  blocking collectives  76.6 us (68%)
  Pallas kernels  14.1 us (12%)
  starting transfers between devices  11.1 us (10%)
  waiting for transfers between devices  10.2 us (9%)
    all_to_all x4, blocking collectives, a2a(): return lax.all_to_all(v, axes, 0, 0, tiled=True)  45.4 us
    all_to_all x2, blocking collectives, grouped(): return lax.all_to_all(v, ALL, 0, 0, tiled=True, axis_index_groups=groups)  31.2 us
    all_to_all x1, waiting for transfers between devices, a2a(): return lax.all_to_all(v, axes, 0, 0, tiled=True)  9.19 us
    all_to_all x1, starting transfers between devices, a2a(): return lax.all_to_all(v, axes, 0, 0, tiled=True)  5.98 us
    ppermute x2, starting transfers between devices, swap(): return lax.ppermute(v, 'core', [(0, 1), (1, 0)])  5.14 us
    pallas_call x1, Pallas kernels, body(): call(pack_kernel, [SMEM, ANY], sds((4, 2, 96, 256)), scratch=[pltpu.Semap...  3.13 us
    pallas_call x1, Pallas kernels, body(): call(first_kernel, [SMEM, SMEM, ANY], (*tiles, sds((32,), jnp.int32), sds...  3.08 us
  transfers between devices with their start and end apart: 3, of which 2 were waited for; matrix products, arithmetic and copies ran while one was open for 0% of the time, Pallas kernels for 5%

profile of v7, /device:TPU:1, one launch (start us, length us, event | category | flops | bytes accessed | tf_op | source)
XLA Modules:
  0.0 112.8 jit_solution(18133602762886136446)
XLA Ops:
  0.6 0.0 copy-start.1
  0.6 0.0 copy-start.2
  0.7 3.1 %shard_map.69 = f32[4,2,96,256]{3,2,1,0:T(8,128)} custom-call(s32[2,32]{1,0:T(2,128)} %fb.7, f32[2,4,2,4,32,256]{5,4,3,2,1,0:T(8,128)} %bitcast.2), custom_call_target="tpu_custom_call" | custom-call | tf_op jit(solution)/shard_map/pallas_call | solution.py:260
  3.8 6.0 %all-to-all-start = ((f32[8,96,256]{2,1,0:T(8,128)}), f32[8,96,256]{2,1,0:T(8,128)S(1)}, u32[]{:S(2)}, u32[]{:S(2)}) async-start(f32[8,96,256]{2,1,0:T(8,128)} %bitcast.1), calls=%async_computation | async-start | bytes 1572864 | tf_op jit(solution)/shard_map/all_to_all | solution.py:238
  9.8 0.0 copy-done.1
  9.8 0.0 copy-done.2
  9.8 3.1 %shard_map.68 = (bf16[4,256,512]{2,1,0:T(8,128)(2,1)S(1)}, bf16[4,256,512]{2,1,0:T(8,128)(2,1)S(1)}, s32[32]{0:T(128)S(1)}, f32[2,256,256]{2,1,0:T(8,128)S(1)}) custom-call(s32[2,32]{1,0:T(2,128)S(1)} %copy-done.1, s32[2,4]{1,0:T(2,128)S(1)} %copy-done.2, f32[2048,1024]{1,0:T(8,128)} %inverse.3), custom_call_target="tpu_custom_call" | custom-call | flops 2097152 | bytes 6291456 | tf_op jit(solution)/shard_map/pallas_call | solution.py:270
  12.9 9.2 %all-to-all-done.inc = f32[8,96,256]{2,1,0:T(8,128)S(1)} async-done(((f32[8,96,256]{2,1,0:T(8,128)}), f32[8,96,256]{2,1,0:T(8,128)S(1)}, u32[]{:S(2)}, u32[]{:S(2)}) %all-to-all-start) | async-done | bytes 786464 | tf_op jit(solution)/shard_map/all_to_all | solution.py:238
  22.1 0.6 shard_map.70
  22.7 11.0 %all_to_all.35.after.own = f32[4,4,32,256]{3,2,1,0:T(8,128)S(1)} all-to-all(f32[4,4,32,256]{3,2,1,0:T(8,128)S(1)} %get-tuple-element.16), channel_id=1, replica_groups=mesh['y'=4,'core'=2,'z'=4,'x'=4] {'y'}, dimensions={0} | all-to-all | bytes 1048576 | tf_op jit(solution)/shard_map/all_to_all | solution.py:238
  33.7 1.8 %collective-permute-start = (f32[4,4,32,256]{3,2,1,0:T(8,128)S(1)}, f32[4,4,32,256]{3,2,1,0:T(8,128)S(1)}, u32[]{:S(2)}, u32[]{:S(2)}) collective-permute-start(f32[4,4,32,256]{3,2,1,0:T(8,128)S(1)} %all_to_all.35.after.own), channel_id=1, source_target_pairs={{0,16},{16,0},{1,17},{17,1},{2,18},{18,2},{3,19},{19,3},{4,20},{20... | collective-permute-start | bytes 1572872 | tf_op jit(solution)/shard_map/ppermute | solution.py:256
  35.5 2.2 %shard_map.71 = (bf16[4,256,512]{2,1,0:T(8,128)(2,1)S(1)}, bf16[4,256,512]{2,1,0:T(8,128)(2,1)S(1)}) custom-call(s32[2,32]{1,0:T(2,128)S(1)} %copy-done.1, s32[32]{0:T(128)S(1)} %get-tuple-element.12.tab, f32[2048,1024]{1,0:T(8,128)} %inverse.3, f32[4,4,32,256]{3,2,1,0:T(8,128)S(1)} %all_to_all.35.after.own), custom_call_target="tpu_custom_call" | custom-call | flops 2097152 | bytes 6291456 | tf_op jit(solution)/shard_map/pallas_call | solution.py:284
  37.7 0.0 collective-permute-done.other
  37.7 1.9 %shard_map.72 = f32[4,4,8,16,256]{4,3,2,1,0:T(8,128)S(1)} custom-call(bf16[4,256,512]{2,1,0:T(8,128)(2,1)S(1)} %get-tuple-element.14.hi0, bf16[4,256,512]{2,1,0:T(8,128)(2,1)S(1)} %get-tuple-element.15.lo0, bf16[4,256,512]{2,1,0:T(8,128)(2,1)S(1)} %get-tuple-element.17.hi1, bf16[4,256,512]{2,1,0:T(8,128)(2,1)S(1)} %get-tuple-element.18.lo1, ...), custom_call_target="tpu_custom_call" | custom-call | tf_op jit(solution)/shard_map/pallas_call | solution.py:287
  39.6 20.2 %all_to_all.36.inc = f32[4,4,8,16,256]{4,3,2,1,0:T(8,128)S(1)} all-to-all(f32[4,4,8,16,256]{4,3,2,1,0:T(8,128)S(1)} %shard_map.72), channel_id=1, replica_groups={{0,1,2,3},{4,5,6,7},{8,9,10,11},{12,13,14,15},{16,20,24,28},{17,21,25,2..., dimensions={0} | all-to-all | bytes 4194304 | tf_op jit(solution)/shard_map/all_to_all | solution.py:248
  59.8 0.1 shard_map.73
  59.9 11.0 %all_to_all.37.parts = f32[4,8,16,256]{3,2,1,0:T(8,128)S(1)} all-to-all(f32[4,8,16,256]{3,2,1,0:T(8,128)S(1)} %shard_map.73), channel_id=1, replica_groups={{0,4,8,12},{1,5,9,13},{2,6,10,14},{3,7,11,15},{16,17,18,19},{20,21,22,2..., dimensions={0} | all-to-all | bytes 1048576 | tf_op jit(solution)/shard_map/all_to_all | solution.py:248
  70.9 0.9 shard_map.74
  71.9 0.0 copy-start
  71.9 14.5 %all_to_all.38.inc = f32[8,64,256]{2,1,0:T(8,128)S(1)} all-to-all(f32[8,64,256]{2,1,0:T(8,128)S(1)} %shard_map.74), channel_id=1, replica_groups=mesh['y'=4,'core'=2,'z'=4,'x'=4] {'y','core'}, dimensions={0} | all-to-all | bytes 1048576 | tf_op jit(solution)/shard_map/all_to_all | solution.py:238
  86.3 0.6 shard_map.75
  86.9 7.9 %all_to_all.39.inc = f32[4,64,256]{2,1,0:T(8,128)S(1)} all-to-all(f32[4,64,256]{2,1,0:T(8,128)S(1)} %shard_map.75), channel_id=1, replica_groups=mesh['y'=4,'core'=2,'z'=4,'x'=4] {'z'}, dimensions={0} | all-to-all | bytes 524288 | tf_op jit(solution)/shard_map/all_to_all | solution.py:238
  94.9 0.7 shard_map.76
  95.6 12.0 %all_to_all.40.inc = f32[16,32,256]{2,1,0:T(8,128)S(1)} all-to-all(f32[16,32,256]{2,1,0:T(8,128)S(1)} %get-tuple-element.21), channel_id=1, replica_groups=mesh['y'=4,'core'=2,'z'=4,'x'=4] {'y','x'}, dimensions={0} | all-to-all | bytes 1048576 | tf_op jit(solution)/shard_map/all_to_all | solution.py:238
  107.6 3.3 %collective-permute-start.1 = (f32[4,32,256]{2,1,0:T(8,128)S(1)}, f32[4,32,256]{2,1,0:T(8,128)S(1)}, u32[]{:S(2)}, u32[]{:S(2)}) collective-permute-start(f32[4,32,256]{2,1,0:T(8,128)S(1)} %shard_map.77.own), channel_id=1, source_target_pairs={{0,16},{16,0},{1,17},{17,1},{2,18},{18,2},{3,19},{19,3},{4,20},{20... | collective-permute-start | bytes 393224 | tf_op jit(solution)/shard_map/ppermute | solution.py:256
  110.9 1.0 collective-permute-done.1.other
  111.9 0.0 copy-done
  111.9 0.9 shard_map.78
  (1 shorter events, 0.0 us)
Async XLA Ops:
  0.6 9.1 %copy-start.1 = (s32[2,32]{1,0:T(2,128)S(1)}, s32[2,32]{1,0:T(2,128)}, u32[]{:S(2)}) copy-start(s32[2,32]{1,0:T(2,128)} %fb.7) | copy-start | bytes 772
  0.6 9.1 %copy-start.2 = (s32[2,4]{1,0:T(2,128)S(1)}, s32[2,4]{1,0:T(2,128)}, u32[]{:S(2)}) copy-start(s32[2,4]{1,0:T(2,128)} %bounds.1) | copy-start | bytes 100
  3.8 18.3 %all-to-all-start = ((f32[8,96,256]{2,1,0:T(8,128)}), f32[8,96,256]{2,1,0:T(8,128)S(1)}, u32[]{:S(2)}, u32[]{:S(2)}) async-start(f32[8,96,256]{2,1,0:T(8,128)} %bitcast.1), calls=%async_computation | async-start | bytes 1572864 | tf_op jit(solution)/shard_map/all_to_all | solution.py:238
  33.7 4.0 %collective-permute-start = (f32[4,4,32,256]{3,2,1,0:T(8,128)S(1)}, f32[4,4,32,256]{3,2,1,0:T(8,128)S(1)}, u32[]{:S(2)}, u32[]{:S(2)}) collective-permute-start(f32[4,4,32,256]{3,2,1,0:T(8,128)S(1)} %all_to_all.35.after.own), channel_id=1, source_target_pairs={{0,16},{16,0},{1,17},{17,1},{2,18},{18,2},{3,19},{19,3},{4,20},{20... | collective-permute-start | bytes 1572872 | tf_op jit(solution)/shard_map/ppermute | solution.py:256
  71.9 40.0 %copy-start = (f32[2,256,256]{2,1,0:T(8,128)S(1)}, f32[2,256,256]{2,1,0:T(8,128)}, u32[]{:S(2)}) copy-start(f32[2,256,256]{2,1,0:T(8,128)} %terms.1) | copy-start | bytes 1572868
  107.6 4.3 %collective-permute-start.1 = (f32[4,32,256]{2,1,0:T(8,128)S(1)}, f32[4,32,256]{2,1,0:T(8,128)S(1)}, u32[]{:S(2)}, u32[]{:S(2)}) collective-permute-start(f32[4,32,256]{2,1,0:T(8,128)S(1)} %shard_map.77.own), channel_id=1, source_target_pairs={{0,16},{16,0},{1,17},{17,1},{2,18},{18,2},{3,19},{19,3},{4,20},{20... | collective-permute-start | bytes 393224 | tf_op jit(solution)/shard_map/ppermute | solution.py:256

commit v8 on v7

--- a/solution.py
+++ b/solution.py
@@ -32,36 +32,46 @@
     return mm(ah, bh) + (mm(ah, bl) + mm(al, bh))
 
 
-def pack_kernel(fb, w, out, sems):
+def pack_kernel(fb, w, out, stage, ins, outs):
     r = lax.axis_index("y") * 2 + lax.axis_index("core")
     z, x = lax.axis_index("z"), lax.axis_index("x")
     c = z * 4 + x
     part = 2 * x + z // 2
     row = pl.multiple_of(16 * (z % 2), 16)
-    copies = []
-
-    def start(src, dst):
-        copy = pltpu.make_async_copy(src, dst, sems.at[len(copies)])
-        copy.start()
-        copies.append(copy)
-
+    pieces, mine = [], []
     for f in range(2):
         own = [fb[f, 4 * r + i] for i in range(4)]
         piece = jnp.int32(0)
         for i in range(1, 4):
             piece = jnp.where((own[i] >> 2) == c, i, piece)
-        for k in range(2):
-            start(w.at[f, piece, k], out.at[:, k, 32 * f : 32 * f + 32])
+        at = (slice(None), slice(32 * f, 32 * f + 32))
+        copy = pltpu.make_async_copy(w.at[f, piece], stage.at[at], ins.at[f])
+        copy.start()
+        pieces.append((copy, pltpu.make_async_copy(stage.at[at], out.at[at], outs.at[f])))
+    for f in range(2):
+        own = [fb[f, 4 * r + i] for i in range(4)]
         for d in range(8):
             named = jnp.int32(0)
             for i in range(1, 4):
                 named = jnp.where((own[i] >> 3) == d, i, named)
-            start(
-                w.at[f, named, part // 4, part % 4, pl.ds(row, 16)],
-                out.at[d // 2, d % 2, 64 + 16 * f : 80 + 16 * f],
+            copy = pltpu.make_async_copy(
+                w.at[f, named, part, pl.ds(row, 16)],
+                stage.at[d, 64 + 16 * f : 80 + 16 * f],
+                ins.at[2 + 8 * f + d],
             )
-    for copy in copies:
+            copy.start()
+            mine.append(copy)
+    for first, second in pieces:
+        first.wait()
+        second.start()
+    for copy in mine:
         copy.wait()
+    at = (slice(None), slice(64, 96))
+    last = pltpu.make_async_copy(stage.at[at], out.at[at], outs.at[2])
+    last.start()
+    for first, second in pieces:
+        second.wait()
+    last.wait()
 
 
 def pick_kernel(tab, inc, slices, mine):
@@ -136,11 +146,12 @@
 def product_kernel(hi0, lo0, hi1, lo1, own, other, out, whole):
     core = lax.axis_index("core")
     for k in range(4):
-        base = 256 * (k % 2)
-        at = pl.multiple_of(base + 128 * core, 128)
-        whole[k // 2, pl.ds(at, 128), :] = own[:, k].reshape(128, 256)
-        at = pl.multiple_of(base + 128 * (1 - core), 128)
-        whole[k // 2, pl.ds(at, 128), :] = other[:, k].reshape(128, 256)
+        for y in range(4):
+            base = 256 * (k % 2) + 64 * y
+            at = pl.multiple_of(base + 32 * core, 32)
+            whole[k // 2, pl.ds(at, 32), :] = own[y, k]
+            at = pl.multiple_of(base + 32 * (1 - core), 32)
+            whole[k // 2, pl.ds(at, 32), :] = other[y, k]
     for f in range(2):
         w = split(whole[f])
         hi, lo = ((hi0, lo0), (hi1, lo1))[f]
@@ -192,10 +203,13 @@
             out[i, 16 * f : 16 * f + 16] = inc[fb[f, 4 * r + i] >> 3, 16 * f : 16 * f + 16, :]
 
 
-def border_kernel(inc, border, out):
+def border_kernel(inc, border):
     for z in range(4):
         for f in range(2):
             border[f, 16 * z : 16 * z + 16] = inc[z, 16 * f : 16 * f + 16, :]
+
+
+def spread_kernel(inc, out):
     total = (inc[0, 32:64] + inc[1, 32:64]) + (inc[2, 32:64] + inc[3, 32:64])
     for d in range(16):
         out[d] = total
@@ -260,10 +274,15 @@
     outgoing = call(
         pack_kernel,
         [SMEM, ANY],
-        sds((4, 2, 96, 256)),
-        scratch=[pltpu.SemaphoreType.DMA((20,))],
-    )(hbm(fb), hbm(panels.reshape(2, 4, 2, 4, 32, 256)))
-    incoming = a2a(outgoing.reshape(8, 96, 256), ROW)
+        sds((8, 96, 256)),
+        ANY,
+        scratch=[
+            pltpu.VMEM((8, 96, 256), F32),
+            pltpu.SemaphoreType.DMA((18,)),
+            pltpu.SemaphoreType.DMA((3,)),
+        ],
+    )(hbm(fb), hbm(panels.reshape(2, 4, 8, 32, 256)))
+    incoming = a2a(outgoing, ROW)
     tiles = (sds((4, 256, 512), BF16), sds((4, 256, 512), BF16))
     buffers = [pltpu.VMEM((8, 256, 256), F32), pltpu.SemaphoreType.DMA((8,))]
     cost = pl.CostEstimate(flops=2 * MIB, bytes_accessed=6 * MIB, transcendentals=0)
@@ -298,10 +317,12 @@
     v = a2a(v, ROW)
     v = call(place_kernel, [SMEM, VMEM], sds((4, 64, 256)))(fb, v)
     v = a2a(v, "z")
-    border, v = call(border_kernel, [VMEM], (sds((2, 64, 256)), sds((16, 32, 256))))(v)
-    v = a2a(v, ("y", "x"))
-    own = call(chunk_kernel, [VMEM], sds((4, 32, 256)))(v)
+    sums = call(spread_kernel, [VMEM], sds((16, 32, 256)))(v)
+    sums = a2a(sums, ("y", "x"))
+    own = call(chunk_kernel, [VMEM], sds((4, 32, 256)))(sums)
     other = swap(own)
+    v, own = lax.optimization_barrier((v, own))
+    border = call(border_kernel, [VMEM], sds((2, 64, 256)))(v)
     diag = call(
         finish_kernel,
         [VMEM, VMEM, VMEM, VMEM],

time: 113 us -> 112 us (level)
    pallas_call x3 -> x4, Pallas kernels: 3.86 us -> 3.81 us  [the longest x1 3.07 us: body(): call(pack_kernel, [SMEM, ANY], sds((8, 96, 256)), ANY, scratch=[pltpu.VME...]
where the time goes in v8:
time: 112 us
  blocking collectives  76.5 us (68%)
  Pallas kernels  14 us (12%)
  starting transfers between devices  11.1 us (10%)
  waiting for transfers between devices  9.52 us (8%)
    all_to_all x4, blocking collectives, a2a(): return lax.all_to_all(v, axes, 0, 0, tiled=True)  45.3 us
    all_to_all x2, blocking collectives, grouped(): return lax.all_to_all(v, ALL, 0, 0, tiled=True, axis_index_groups=groups)  31.2 us
    all_to_all x1, waiting for transfers between devices, a2a(): return lax.all_to_all(v, axes, 0, 0, tiled=True)  9.19 us
    all_to_all x1, starting transfers between devices, a2a(): return lax.all_to_all(v, axes, 0, 0, tiled=True)  6.01 us
    ppermute x2, starting transfers between devices, swap(): return lax.ppermute(v, 'core', [(0, 1), (1, 0)])  5.14 us
    pallas_call x1, Pallas kernels, body(): call(first_kernel, [SMEM, SMEM, ANY], (*tiles, sds((32,), jnp.int32), sds...  3.08 us
    pallas_call x1, Pallas kernels, body(): call(pack_kernel, [SMEM, ANY], sds((8, 96, 256)), ANY, scratch=[pltpu.VME...  3.07 us
  transfers between devices with their start and end apart: 3, of which 2 were waited for; matrix products, arithmetic and copies ran while one was open for 0% of the time, Pallas kernels for 5%

profile of v8, /device:TPU:1, one launch (start us, length us, event | category | flops | bytes accessed | tf_op | source)
XLA Modules:
  0.0 112.0 jit_solution(12421208690318934054)
XLA Ops:
  0.6 0.0 copy-start.1
  0.6 0.0 copy-start.2
  0.7 3.1 %shard_map.69 = f32[8,96,256]{2,1,0:T(8,128)} custom-call(s32[2,32]{1,0:T(2,128)} %fb.7, f32[2,4,8,32,256]{4,3,2,1,0:T(8,128)} %bitcast.1), custom_call_target="tpu_custom_call" | custom-call | tf_op jit(solution)/shard_map/pallas_call | solution.py:274
  3.7 6.0 %all-to-all-start = ((f32[8,96,256]{2,1,0:T(8,128)}), f32[8,96,256]{2,1,0:T(8,128)S(1)}, u32[]{:S(2)}, u32[]{:S(2)}) async-start(f32[8,96,256]{2,1,0:T(8,128)} %shard_map.69), calls=%async_computation | async-start | bytes 1572864 | tf_op jit(solution)/shard_map/all_to_all | solution.py:252
  9.7 0.0 copy-done.1
  9.7 0.0 copy-done.2
  9.7 3.1 %shard_map.68 = (bf16[4,256,512]{2,1,0:T(8,128)(2,1)S(1)}, bf16[4,256,512]{2,1,0:T(8,128)(2,1)S(1)}, s32[32]{0:T(128)S(1)}, f32[2,256,256]{2,1,0:T(8,128)S(1)}) custom-call(s32[2,32]{1,0:T(2,128)S(1)} %copy-done.1, s32[2,4]{1,0:T(2,128)S(1)} %copy-done.2, f32[2048,1024]{1,0:T(8,128)} %inverse.3), custom_call_target="tpu_custom_call" | custom-call | flops 2097152 | bytes 6291456 | tf_op jit(solution)/shard_map/pallas_call | solution.py:289
  12.8 9.2 %all-to-all-done.inc = f32[8,96,256]{2,1,0:T(8,128)S(1)} async-done(((f32[8,96,256]{2,1,0:T(8,128)}), f32[8,96,256]{2,1,0:T(8,128)S(1)}, u32[]{:S(2)}, u32[]{:S(2)}) %all-to-all-start) | async-done | bytes 786464 | tf_op jit(solution)/shard_map/all_to_all | solution.py:252
  22.0 0.6 shard_map.70
  22.6 11.0 %all_to_all.35.after.own = f32[4,4,32,256]{3,2,1,0:T(8,128)S(1)} all-to-all(f32[4,4,32,256]{3,2,1,0:T(8,128)S(1)} %get-tuple-element.16), channel_id=1, replica_groups=mesh['y'=4,'core'=2,'z'=4,'x'=4] {'y'}, dimensions={0} | all-to-all | bytes 1048576 | tf_op jit(solution)/shard_map/all_to_all | solution.py:252
  33.6 1.8 %collective-permute-start = (f32[4,4,32,256]{3,2,1,0:T(8,128)S(1)}, f32[4,4,32,256]{3,2,1,0:T(8,128)S(1)}, u32[]{:S(2)}, u32[]{:S(2)}) collective-permute-start(f32[4,4,32,256]{3,2,1,0:T(8,128)S(1)} %all_to_all.35.after.own), channel_id=1, source_target_pairs={{0,16},{16,0},{1,17},{17,1},{2,18},{18,2},{3,19},{19,3},{4,20},{20... | collective-permute-start | bytes 1572872 | tf_op jit(solution)/shard_map/ppermute | solution.py:270
  35.5 2.2 %shard_map.71 = (bf16[4,256,512]{2,1,0:T(8,128)(2,1)S(1)}, bf16[4,256,512]{2,1,0:T(8,128)(2,1)S(1)}) custom-call(s32[2,32]{1,0:T(2,128)S(1)} %copy-done.1, s32[32]{0:T(128)S(1)} %get-tuple-element.12.tab, f32[2048,1024]{1,0:T(8,128)} %inverse.3, f32[4,4,32,256]{3,2,1,0:T(8,128)S(1)} %all_to_all.35.after.own), custom_call_target="tpu_custom_call" | custom-call | flops 2097152 | bytes 6291456 | tf_op jit(solution)/shard_map/pallas_call | solution.py:303
  37.7 0.0 collective-permute-done.other
  37.7 1.9 %shard_map.72 = f32[4,4,8,16,256]{4,3,2,1,0:T(8,128)S(1)} custom-call(bf16[4,256,512]{2,1,0:T(8,128)(2,1)S(1)} %get-tuple-element.14.hi0, bf16[4,256,512]{2,1,0:T(8,128)(2,1)S(1)} %get-tuple-element.15.lo0, bf16[4,256,512]{2,1,0:T(8,128)(2,1)S(1)} %get-tuple-element.17.hi1, bf16[4,256,512]{2,1,0:T(8,128)(2,1)S(1)} %get-tuple-element.18.lo1, ...), custom_call_target="tpu_custom_call" | custom-call | tf_op jit(solution)/shard_map/pallas_call | solution.py:306
  39.5 20.1 %all_to_all.36.inc = f32[4,4,8,16,256]{4,3,2,1,0:T(8,128)S(1)} all-to-all(f32[4,4,8,16,256]{4,3,2,1,0:T(8,128)S(1)} %shard_map.72), channel_id=1, replica_groups={{0,1,2,3},{4,5,6,7},{8,9,10,11},{12,13,14,15},{16,20,24,28},{17,21,25,2..., dimensions={0} | all-to-all | bytes 4194304 | tf_op jit(solution)/shard_map/all_to_all | solution.py:262
  59.7 0.1 shard_map.73
  59.8 11.1 %all_to_all.37.parts = f32[4,8,16,256]{3,2,1,0:T(8,128)S(1)} all-to-all(f32[4,8,16,256]{3,2,1,0:T(8,128)S(1)} %shard_map.73), channel_id=1, replica_groups={{0,4,8,12},{1,5,9,13},{2,6,10,14},{3,7,11,15},{16,17,18,19},{20,21,22,2..., dimensions={0} | all-to-all | bytes 1048576 | tf_op jit(solution)/shard_map/all_to_all | solution.py:262
  70.9 0.9 shard_map.74
  71.8 14.3 %all_to_all.38.inc = f32[8,64,256]{2,1,0:T(8,128)S(1)} all-to-all(f32[8,64,256]{2,1,0:T(8,128)S(1)} %shard_map.74), channel_id=1, replica_groups=mesh['y'=4,'core'=2,'z'=4,'x'=4] {'y','core'}, dimensions={0} | all-to-all | bytes 1048576 | tf_op jit(solution)/shard_map/all_to_all | solution.py:252
  86.2 0.0 copy-start
  86.2 0.6 shard_map.75
  86.8 7.9 %all_to_all.39.inc = f32[4,64,256]{2,1,0:T(8,128)S(1)} all-to-all(f32[4,64,256]{2,1,0:T(8,128)S(1)} %shard_map.75), channel_id=1, replica_groups=mesh['y'=4,'core'=2,'z'=4,'x'=4] {'z'}, dimensions={0} | all-to-all | bytes 524288 | tf_op jit(solution)/shard_map/all_to_all | solution.py:252
  94.8 12.0 %all_to_all.40.inc = f32[16,32,256]{2,1,0:T(8,128)S(1)} all-to-all(f32[16,32,256]{2,1,0:T(8,128)S(1)} %shard_map.76), channel_id=1, replica_groups=mesh['y'=4,'core'=2,'z'=4,'x'=4] {'y','x'}, dimensions={0} | all-to-all | bytes 1048576 | tf_op jit(solution)/shard_map/all_to_all | solution.py:252
  106.8 3.3 %collective-permute-start.1 = (f32[4,32,256]{2,1,0:T(8,128)S(1)}, f32[4,32,256]{2,1,0:T(8,128)S(1)}, u32[]{:S(2)}, u32[]{:S(2)}) collective-permute-start(f32[4,32,256]{2,1,0:T(8,128)S(1)} %shard_map.77.own), channel_id=1, source_target_pairs={{0,16},{16,0},{1,17},{17,1},{2,18},{18,2},{3,19},{19,3},{4,20},{20... | collective-permute-start | bytes 393224 | tf_op jit(solution)/shard_map/ppermute | solution.py:270
  110.1 0.7 shard_map.78
  110.8 0.3 collective-permute-done.1.other
  111.1 0.0 copy-done
  111.1 0.9 shard_map.79
  (2 shorter events, 0.1 us)
Async XLA Ops:
  0.6 9.1 %copy-start.1 = (s32[2,32]{1,0:T(2,128)S(1)}, s32[2,32]{1,0:T(2,128)}, u32[]{:S(2)}) copy-start(s32[2,32]{1,0:T(2,128)} %fb.7) | copy-start | bytes 772
  0.6 9.1 %copy-start.2 = (s32[2,4]{1,0:T(2,128)S(1)}, s32[2,4]{1,0:T(2,128)}, u32[]{:S(2)}) copy-start(s32[2,4]{1,0:T(2,128)} %bounds.1) | copy-start | bytes 100
  3.7 18.3 %all-to-all-start = ((f32[8,96,256]{2,1,0:T(8,128)}), f32[8,96,256]{2,1,0:T(8,128)S(1)}, u32[]{:S(2)}, u32[]{:S(2)}) async-start(f32[8,96,256]{2,1,0:T(8,128)} %shard_map.69), calls=%async_computation | async-start | bytes 1572864 | tf_op jit(solution)/shard_map/all_to_all | solution.py:252
  33.6 4.0 %collective-permute-start = (f32[4,4,32,256]{3,2,1,0:T(8,128)S(1)}, f32[4,4,32,256]{3,2,1,0:T(8,128)S(1)}, u32[]{:S(2)}, u32[]{:S(2)}) collective-permute-start(f32[4,4,32,256]{3,2,1,0:T(8,128)S(1)} %all_to_all.35.after.own), channel_id=1, source_target_pairs={{0,16},{16,0},{1,17},{17,1},{2,18},{18,2},{3,19},{19,3},{4,20},{20... | collective-permute-start | bytes 1572872 | tf_op jit(solution)/shard_map/ppermute | solution.py:270
  86.2 24.9 %copy-start = (f32[2,256,256]{2,1,0:T(8,128)S(1)}, f32[2,256,256]{2,1,0:T(8,128)}, u32[]{:S(2)}) copy-start(f32[2,256,256]{2,1,0:T(8,128)} %terms.1) | copy-start | bytes 1572868
  106.8 4.3 %collective-permute-start.1 = (f32[4,32,256]{2,1,0:T(8,128)S(1)}, f32[4,32,256]{2,1,0:T(8,128)S(1)}, u32[]{:S(2)}, u32[]{:S(2)}) collective-permute-start(f32[4,32,256]{2,1,0:T(8,128)S(1)} %shard_map.77.own), channel_id=1, source_target_pairs={{0,16},{16,0},{1,17},{17,1},{2,18},{18,2},{3,19},{19,3},{4,20},{20... | collective-permute-start | bytes 393224 | tf_op jit(solution)/shard_map/ppermute | solution.py:270

commit v9 on v8

--- a/solution.py
+++ b/solution.py
@@ -78,9 +78,7 @@
     for f in range(2):
         for t in range(2):
             p = tab[16 * f + 8 + t]
-            v = inc[p >> 2, 32 * f : 32 * f + 32, :]
-            for d in range(4):
-                slices[d, 2 * f + t] = v
+            slices[2 * f + t] = inc[p >> 2, 32 * f : 32 * f + 32, :]
         for s in range(4):
             p = tab[16 * f + s]
             mine[4 * f + s] = inc[p >> 2, 64 + 16 * f : 80 + 16 * f, :]
@@ -143,15 +141,18 @@
     fetch_tiles(1, fb, tab, inverse, hi, lo, tiles, sems)
 
 
-def product_kernel(hi0, lo0, hi1, lo1, own, other, out, whole):
+def product_kernel(hi0, lo0, hi1, lo1, *refs):
+    own, other, (out, whole) = refs[:4], refs[4:8], refs[8:]
+    here = lax.axis_index("y")
     core = lax.axis_index("core")
-    for k in range(4):
-        for y in range(4):
+    for step, mine, theirs in zip((0, 1, 3, 2), own, other):
+        y = (here - step) & 3
+        for k in range(4):
             base = 256 * (k % 2) + 64 * y
             at = pl.multiple_of(base + 32 * core, 32)
-            whole[k // 2, pl.ds(at, 32), :] = own[y, k]
+            whole[k // 2, pl.ds(at, 32), :] = mine[k]
             at = pl.multiple_of(base + 32 * (1 - core), 32)
-            whole[k // 2, pl.ds(at, 32), :] = other[y, k]
+            whole[k // 2, pl.ds(at, 32), :] = theirs[k]
     for f in range(2):
         w = split(whole[f])
         hi, lo = ((hi0, lo0), (hi1, lo1))[f]
@@ -171,16 +172,21 @@
             out[d, k] = (inc[0, d, k] + inc[1, d, k]) + (inc[2, d, k] + inc[3, d, k])
 
 
-def reduce_kernel(tab, mask, parts, mine, out):
-    for d in range(8):
-        out[d, 0:32] = jnp.zeros((32, 256), F32)
+def reduce_kernel(tab, mask, parts, mine, *refs):
+    outs, buf = refs[:4], refs[4]
+    core, here = lax.axis_index("core"), lax.axis_index("y")
+    for step in range(4):
+        for rel in range(2):
+            buf[step, rel, 0:32] = jnp.zeros((32, 256), F32)
     for f in range(2):
         rows = []
         for s in range(4):
             k = 4 * f + s
             v = (parts[0, k] + parts[1, k]) + (parts[2, k] + parts[3, k])
             rows.append(v)
-            out[tab[16 * f + s] >> 2, 16 * f : 16 * f + 16] = -v
+            owner = tab[16 * f + s] >> 2
+            step, rel = ((owner >> 1) - here) & 3, (owner & 1) ^ core
+            buf[step, rel, 16 * f : 16 * f + 16] = -v
         left = mine[4 * f : 4 * f + 4].reshape(64, 256)
         right = jnp.concatenate(rows, axis=0)
         full = dot3(split(left), split(right), ((0,), (0,)))
@@ -188,29 +194,48 @@
         packed = full[:, :128] + full[:, 128:]
         for d in range(4):
             part = packed[64 * d : 64 * d + 64]
-            out[4 * f + d, 32:64] = jnp.concatenate([part[:32], part[32:]], axis=1)
-
-
-def place_kernel(fb, inc, out):
-    r = lax.axis_index("y") * 2 + lax.axis_index("core")
-    total = inc[0, 32:64]
-    for d in range(1, 8):
-        total = total + inc[d, 32:64]
-    for d in range(4):
-        out[d, 32:64] = total
-    for f in range(2):
-        for i in range(4):
-            out[i, 16 * f : 16 * f + 16] = inc[fb[f, 4 * r + i] >> 3, 16 * f : 16 * f + 16, :]
-
-
-def border_kernel(inc, border):
-    for z in range(4):
+            owner = 4 * f + d
+            step, rel = (owner // 2 - here) & 3, (owner % 2) ^ core
+            buf[step, rel, 32:64] = jnp.concatenate([part[:32], part[32:]], axis=1)
+    for step in range(4):
+        outs[step][...] = buf[step]
+
+
+def place_kernel(fb, *refs):
+    own, other, outs, got = refs[:4], refs[4:8], refs[8:12], refs[12]
+    core, here = lax.axis_index("core"), lax.axis_index("y")
+    z = lax.axis_index("z")
+    total = None
+    for step in range(4):
+        y = (here - step) & 3
+        got[0, y] = own[step][0, 0:32]
+        got[1, y] = other[step][1, 0:32]
+        both = own[step][0, 32:64] + other[step][1, 32:64]
+        total = both if total is None else total + both
+    for step in range(4):
+        i = (z + step) & 3
         for f in range(2):
-            border[f, 16 * z : 16 * z + 16] = inc[z, 16 * f : 16 * f + 16, :]
-
-
-def spread_kernel(inc, out):
-    total = (inc[0, 32:64] + inc[1, 32:64]) + (inc[2, 32:64] + inc[3, 32:64])
+            source = fb[f, 4 * (2 * here + core) + i] >> 3
+            v = got[(source & 1) ^ core, source >> 1, 16 * f : 16 * f + 16, :]
+            outs[step][16 * f : 16 * f + 16] = v
+        outs[step][32:64] = total
+
+
+def border_kernel(*refs):
+    border = refs[4]
+    z = lax.axis_index("z")
+    for step in range(4):
+        at = pl.multiple_of(16 * ((z - step) & 3), 16)
+        for f in range(2):
+            border[f, pl.ds(at, 16), :] = refs[step][16 * f : 16 * f + 16]
+
+
+def spread_kernel(*refs):
+    out, got = refs[4:]
+    z = lax.axis_index("z")
+    for step in range(4):
+        got[(z - step) & 3] = refs[step][32:64]
+    total = (got[0] + got[1]) + (got[2] + got[3])
     for d in range(16):
         out[d] = total
 
@@ -264,6 +289,10 @@
 
 def hbm(v):
     return pltpu.with_memory_space_constraint(v, pltpu.HBM)
+
+
+def shift(v, axis, step):
+    return lax.ppermute(v, axis, [(i, (i + step) % 4) for i in range(4)])
 
 
 def swap(v):
@@ -296,33 +325,58 @@
         cost=cost,
     )(fb, bounds, hbm(inverse))
     slices, mine = call(
-        pick_kernel, [SMEM, VMEM], (sds((4, 4, 32, 256)), sds((8, 16, 256)))
+        pick_kernel, [SMEM, VMEM], (sds((4, 32, 256)), sds((8, 16, 256)))
     )(tab, incoming)
-    own = a2a(slices, "y")
-    other = swap(own)
+    own = [slices]
+    for step in (1, 3, 2):
+        own.append(shift(slices, "y", step))
     hi1, lo1 = call(
         second_kernel, [SMEM, SMEM, ANY, ANY], tiles, scratch=buffers, limit=16, cost=cost
-    )(fb, tab, hbm(inverse), own)
+    )(fb, tab, hbm(inverse), slices)
+    own[2], hi1 = lax.optimization_barrier((own[2], hi1))
+    own[3], hi1 = lax.optimization_barrier((own[3], hi1))
+    other = [swap(v) for v in own]
     parts = call(
         product_kernel,
-        [VMEM] * 6,
+        [VMEM] * 12,
         sds((4, 4, 8, 16, 256)),
         scratch=[pltpu.VMEM((2, 512, 256), F32)],
         limit=16,
-    )(hi0, lo0, hi1, lo1, own, other)
+    )(hi0, lo0, hi1, lo1, *own, *other)
     parts = grouped(parts, 0)
     parts = call(half_kernel, [VMEM], sds((4, 8, 16, 256)))(parts)
     parts = grouped(parts, 1)
-    v = call(reduce_kernel, [SMEM, VMEM, VMEM, VMEM], sds((8, 64, 256)))(tab, mask, parts, mine)
-    v = a2a(v, ROW)
-    v = call(place_kernel, [SMEM, VMEM], sds((4, 64, 256)))(fb, v)
-    v = a2a(v, "z")
-    sums = call(spread_kernel, [VMEM], sds((16, 32, 256)))(v)
+    pair = sds((2, 64, 256))
+    outs = call(
+        reduce_kernel,
+        [SMEM, VMEM, VMEM, VMEM],
+        (pair,) * 4,
+        scratch=[pltpu.VMEM((4, 2, 64, 256), F32)],
+    )(tab, mask, parts, mine)
+    own = [outs[0]] + [None] * 3
+    for step in (1, 3, 2):
+        own[step] = shift(outs[step], "y", step)
+    other = [swap(v) for v in own]
+    outs = call(
+        place_kernel,
+        [SMEM] + [VMEM] * 8,
+        (sds((64, 256)),) * 4,
+        scratch=[pltpu.VMEM((2, 4, 32, 256), F32)],
+    )(fb, *own, *other)
+    v = [outs[0]] + [None] * 3
+    for step in (1, 3, 2):
+        v[step] = shift(outs[step], "z", step)
+    sums = call(
+        spread_kernel,
+        [VMEM] * 4,
+        sds((16, 32, 256)),
+        scratch=[pltpu.VMEM((4, 32, 256), F32)],
+    )(*v)
     sums = a2a(sums, ("y", "x"))
     own = call(chunk_kernel, [VMEM], sds((4, 32, 256)))(sums)
     other = swap(own)
     v, own = lax.optimization_barrier((v, own))
-    border = call(border_kernel, [VMEM], sds((2, 64, 256)))(v)
+    border = call(border_kernel, [VMEM] * 4, sds((2, 64, 256)))(*v)
     diag = call(
         finish_kernel,
         [VMEM, VMEM, VMEM, VMEM],

time: 112 us -> 108 us (0.964)
  blocking collectives: 76.5 us -> 45.4 us
  starting transfers between devices: 11.1 us -> 31 us
  waiting for transfers between devices: 9.52 us -> 15.9 us
    all_to_all x4 -> x1, blocking collectives: 45.3 us -> 14.2 us  [a2a(): return lax.all_to_all(v, axes, 0, 0, tiled=True)]
    ppermute x2 -> x9, starting transfers between devices: 5.14 us -> 16.7 us  [swap(): return lax.ppermute(v, 'core', [(0, 1), (1, 0)])]
    ppermute x0 -> x9, starting transfers between devices: none -> 8.3 us  [shift(): return lax.ppermute(v, axis, [(i, (i + step) % 4) for i in range(4)])]
    ppermute x0 -> x9, waiting for transfers between devices: none -> 4.06 us  [shift(): return lax.ppermute(v, axis, [(i, (i + step) % 4) for i in range(4)])]
    ppermute x2 -> x9, waiting for transfers between devices: 0.32 us -> 2.64 us  [swap(): return lax.ppermute(v, 'core', [(0, 1), (1, 0)])]
  transfers between devices with their start and end apart: 3 -> 19, of which waited for: 2 -> 12; matrix products, arithmetic and copies ran while one was open for 0% -> 0% of each run, Pallas kernels for 5% -> 6%
where the time goes in v9:
time: 108 us; the launch traced here: 107 us
  blocking collectives  45.4 us (42%)
  starting transfers between devices  31 us (29%)
  waiting for transfers between devices  15.9 us (15%)
  Pallas kernels  14.1 us (13%)
    all_to_all x2, blocking collectives, grouped(): return lax.all_to_all(v, ALL, 0, 0, tiled=True, axis_index_groups=groups)  31.3 us
    ppermute x9, starting transfers between devices, swap(): return lax.ppermute(v, 'core', [(0, 1), (1, 0)])  16.7 us
    all_to_all x1, blocking collectives, a2a(): return lax.all_to_all(v, axes, 0, 0, tiled=True)  14.2 us
    all_to_all x1, waiting for transfers between devices, a2a(): return lax.all_to_all(v, axes, 0, 0, tiled=True)  9.19 us
    ppermute x9, starting transfers between devices, shift(): return lax.ppermute(v, axis, [(i, (i + step) % 4) for i in range(4)])  8.3 us
    all_to_all x1, starting transfers between devices, a2a(): return lax.all_to_all(v, axes, 0, 0, tiled=True)  5.95 us
    ppermute x9, waiting for transfers between devices, shift(): return lax.ppermute(v, axis, [(i, (i + step) % 4) for i in range(4)])  4.06 us
    pallas_call x1, Pallas kernels, body(): call(pack_kernel, [SMEM, ANY], sds((8, 96, 256)), ANY, scratch=[pltpu.VME...  3.09 us
  transfers between devices with their start and end apart: 19, of which 12 were waited for; matrix products, arithmetic and copies ran while one was open for 0% of the time, Pallas kernels for 6%

profile of v9, /device:TPU:1, one launch (start us, length us, event | category | flops | bytes accessed | tf_op | source)
XLA Modules:
  0.0 107.2 jit_solution(809547047816712887)
XLA Ops:
  0.6 0.0 copy-start.1
  0.6 0.0 copy-start.2
  0.7 3.1 %shard_map.69 = f32[8,96,256]{2,1,0:T(8,128)} custom-call(s32[2,32]{1,0:T(2,128)} %fb.7, f32[2,4,8,32,256]{4,3,2,1,0:T(8,128)} %bitcast.1), custom_call_target="tpu_custom_call" | custom-call | tf_op jit(solution)/shard_map/pallas_call | solution.py:303
  3.8 6.0 %all-to-all-start = ((f32[8,96,256]{2,1,0:T(8,128)}), f32[8,96,256]{2,1,0:T(8,128)S(1)}, u32[]{:S(2)}, u32[]{:S(2)}) async-start(f32[8,96,256]{2,1,0:T(8,128)} %shard_map.69), calls=%async_computation | async-start | bytes 1572864 | tf_op jit(solution)/shard_map/all_to_all | solution.py:277
  9.7 0.0 copy-done.1
  9.7 0.0 copy-done.2
  9.7 3.1 %shard_map.68 = (bf16[4,256,512]{2,1,0:T(8,128)(2,1)S(1)}, bf16[4,256,512]{2,1,0:T(8,128)(2,1)S(1)}, s32[32]{0:T(128)S(1)}, f32[2,256,256]{2,1,0:T(8,128)S(1)}) custom-call(s32[2,32]{1,0:T(2,128)S(1)} %copy-done.1, s32[2,4]{1,0:T(2,128)S(1)} %copy-done.2, f32[2048,1024]{1,0:T(8,128)} %inverse.3), custom_call_target="tpu_custom_call" | custom-call | flops 2097152 | bytes 6291456 | tf_op jit(solution)/shard_map/pallas_call | solution.py:318
  12.8 9.2 %all-to-all-done.inc = f32[8,96,256]{2,1,0:T(8,128)S(1)} async-done(((f32[8,96,256]{2,1,0:T(8,128)}), f32[8,96,256]{2,1,0:T(8,128)S(1)}, u32[]{:S(2)}, u32[]{:S(2)}) %all-to-all-start) | async-done | bytes 786464 | tf_op jit(solution)/shard_map/all_to_all | solution.py:277
  22.0 0.6 shard_map.70
  22.6 1.0 collective-permute-start.1
  23.5 1.2 %collective-permute-start = (f32[4,32,256]{2,1,0:T(8,128)S(1)}, f32[4,32,256]{2,1,0:T(8,128)S(1)}, u32[]{:S(2)}, u32[]{:S(2)}) collective-permute-start(f32[4,32,256]{2,1,0:T(8,128)S(1)} %get-tuple-element.31.after.refs_0_), channel_id=1, source_target_pairs={{0,64},{32,96},{64,0},{96,32},{1,65},{33,97},{65,1},{97,33},{2,66}... | collective-permute-start | bytes 393224 | tf_op jit(solution)/shard_map/ppermute | solution.py:295
  24.7 0.0 collective-permute-start.2
  24.7 1.4 %collective-permute-start.3 = (f32[4,32,256]{2,1,0:T(8,128)S(1)}, f32[4,32,256]{2,1,0:T(8,128)S(1)}, u32[]{:S(2)}, u32[]{:S(2)}) collective-permute-start(f32[4,32,256]{2,1,0:T(8,128)S(1)} %get-tuple-element.31.after.refs_0_), channel_id=1, source_target_pairs={{0,16},{16,0},{1,17},{17,1},{2,18},{18,2},{3,19},{19,3},{4,20},{20... | collective-permute-start | bytes 393224 | tf_op jit(solution)/shard_map/ppermute | solution.py:299
  26.1 2.2 %shard_map.71 = (bf16[4,256,512]{2,1,0:T(8,128)(2,1)S(1)}, bf16[4,256,512]{2,1,0:T(8,128)(2,1)S(1)}) custom-call(s32[2,32]{1,0:T(2,128)S(1)} %copy-done.1, s32[32]{0:T(128)S(1)} %get-tuple-element.27.tab, f32[2048,1024]{1,0:T(8,128)} %inverse.3, f32[4,32,256]{2,1,0:T(8,128)S(1)} %get-tuple-element.31.after.refs_0_), custom_call_target="tpu_custom_call" | custom-call | flops 2097152 | bytes 6291456 | tf_op jit(solution)/shard_map/pallas_call | solution.py:333
  28.3 0.0 collective-permute-done.1.refs_2_
  28.4 0.5 collective-permute-done.refs_3_
  28.9 3.5 %collective-permute-start.6 = (f32[4,32,256]{2,1,0:T(8,128)S(1)}, f32[4,32,256]{2,1,0:T(8,128)S(1)}, u32[]{:S(2)}, u32[]{:S(2)}) collective-permute-start(f32[4,32,256]{2,1,0:T(8,128)S(1)} %collective-permute-done.refs_3_), channel_id=1, source_target_pairs={{0,16},{16,0},{1,17},{17,1},{2,18},{18,2},{3,19},{19,3},{4,20},{20... | collective-permute-start | bytes 393224 | tf_op jit(solution)/shard_map/ppermute | solution.py:299
  32.4 0.1 collective-permute-done.2.refs_1_
  32.5 1.3 %collective-permute-start.4 = (f32[4,32,256]{2,1,0:T(8,128)S(1)}, f32[4,32,256]{2,1,0:T(8,128)S(1)}, u32[]{:S(2)}, u32[]{:S(2)}) collective-permute-start(f32[4,32,256]{2,1,0:T(8,128)S(1)} %collective-permute-done.2.refs_1_), channel_id=1, source_target_pairs={{0,16},{16,0},{1,17},{17,1},{2,18},{18,2},{3,19},{19,3},{4,20},{20... | collective-permute-start | bytes 393224 | tf_op jit(solution)/shard_map/ppermute | solution.py:299
  33.7 0.0 collective-permute-start.5
  33.8 0.0 collective-permute-done.3.refs_4_
  33.8 1.0 collective-permute-done.4.refs_5_
  34.7 0.0 collective-permute-done.6.refs_7_
  34.7 0.4 collective-permute-done.5.refs_6_
  35.1 1.9 %shard_map.72 = f32[4,4,8,16,256]{4,3,2,1,0:T(8,128)S(1)} custom-call(bf16[4,256,512]{2,1,0:T(8,128)(2,1)S(1)} %get-tuple-element.29.hi0, bf16[4,256,512]{2,1,0:T(8,128)(2,1)S(1)} %get-tuple-element.30.lo0, bf16[4,256,512]{2,1,0:T(8,128)(2,1)S(1)} %get-tuple-element.34.hi1, bf16[4,256,512]{2,1,0:T(8,128)(2,1)S(1)} %get-tuple-element.35.lo1, ...), custom_call_target="tpu_custom_call" | custom-call | tf_op jit(solution)/shard_map/pallas_call | solution.py:339
  37.0 20.3 %all_to_all.20.inc = f32[4,4,8,16,256]{4,3,2,1,0:T(8,128)S(1)} all-to-all(f32[4,4,8,16,256]{4,3,2,1,0:T(8,128)S(1)} %shard_map.72), channel_id=1, replica_groups={{0,1,2,3},{4,5,6,7},{8,9,10,11},{12,13,14,15},{16,20,24,28},{17,21,25,2..., dimensions={0} | all-to-all | bytes 4194304 | tf_op jit(solution)/shard_map/all_to_all | solution.py:287
  57.3 0.1 shard_map.73
  57.4 10.9 %all_to_all.21.parts = f32[4,8,16,256]{3,2,1,0:T(8,128)S(1)} all-to-all(f32[4,8,16,256]{3,2,1,0:T(8,128)S(1)} %shard_map.73), channel_id=1, replica_groups={{0,4,8,12},{1,5,9,13},{2,6,10,14},{3,7,11,15},{16,17,18,19},{20,21,22,2..., dimensions={0} | all-to-all | bytes 1048576 | tf_op jit(solution)/shard_map/all_to_all | solution.py:287
  68.3 1.0 shard_map.74
  69.3 0.0 copy-start
  69.3 0.1 collective-permute-start.7
  69.4 1.5 %collective-permute-start.8 = (f32[2,64,256]{2,1,0:T(8,128)S(1)}, f32[2,64,256]{2,1,0:T(8,128)S(1)}, u32[]{:S(2)}, u32[]{:S(2)}) collective-permute-start(f32[2,64,256]{2,1,0:T(8,128)S(1)} %get-tuple-element.41), channel_id=1, source_target_pairs={{0,64},{32,96},{64,0},{96,32},{1,65},{33,97},{65,1},{97,33},{2,66}... | collective-permute-start | bytes 393224 | tf_op jit(solution)/shard_map/ppermute | solution.py:295
  70.9 1.8 %collective-permute-start.9 = (f32[2,64,256]{2,1,0:T(8,128)S(1)}, f32[2,64,256]{2,1,0:T(8,128)S(1)}, u32[]{:S(2)}, u32[]{:S(2)}) collective-permute-start(f32[2,64,256]{2,1,0:T(8,128)S(1)} %get-tuple-element.42), channel_id=1, source_target_pairs={{0,96},{32,0},{64,32},{96,64},{1,97},{33,1},{65,33},{97,65},{2,98}... | collective-permute-start | bytes 393224 | tf_op jit(solution)/shard_map/ppermute | solution.py:295
  72.7 3.6 %collective-permute-start.10 = (f32[2,64,256]{2,1,0:T(8,128)S(1)}, f32[2,64,256]{2,1,0:T(8,128)S(1)}, u32[]{:S(2)}, u32[]{:S(2)}) collective-permute-start(f32[2,64,256]{2,1,0:T(8,128)S(1)} %get-tuple-element.39.refs_0_), channel_id=1, source_target_pairs={{0,16},{16,0},{1,17},{17,1},{2,18},{18,2},{3,19},{19,3},{4,20},{20... | collective-permute-start | bytes 393224 | tf_op jit(solution)/shard_map/ppermute | solution.py:299
  76.3 0.0 collective-permute-done.7.refs_1_
  76.3 3.5 %collective-permute-start.11 = (f32[2,64,256]{2,1,0:T(8,128)S(1)}, f32[2,64,256]{2,1,0:T(8,128)S(1)}, u32[]{:S(2)}, u32[]{:S(2)}) collective-permute-start(f32[2,64,256]{2,1,0:T(8,128)S(1)} %collective-permute-done.7.refs_1_), channel_id=1, source_target_pairs={{0,16},{16,0},{1,17},{17,1},{2,18},{18,2},{3,19},{19,3},{4,20},{20... | collective-permute-start | bytes 393224 | tf_op jit(solution)/shard_map/ppermute | solution.py:299
  79.7 0.0 collective-permute-done.8.refs_2_
  79.7 0.0 collective-permute-start.12
  79.7 0.0 collective-permute-done.9.refs_3_
  79.8 0.8 collective-permute-start.13
  80.6 0.0 collective-permute-done.10.refs_4_
  80.6 0.1 collective-permute-done.11.refs_5_
  80.7 0.4 collective-permute-done.12.refs_6_
  81.1 0.5 collective-permute-done.13.refs_7_
  81.6 0.6 shard_map.75
  82.2 0.4 collective-permute-start.14
  82.6 1.8 %collective-permute-start.15 = (f32[64,256]{1,0:T(8,128)S(1)}, f32[64,256]{1,0:T(8,128)S(1)}, u32[]{:S(2)}, u32[]{:S(2)}) collective-permute-start(f32[64,256]{1,0:T(8,128)S(1)} %get-tuple-element.45), channel_id=1, source_target_pairs={{0,8},{4,12},{8,0},{12,4},{1,9},{5,13},{9,1},{13,5},{2,10},{6,14},... | collective-permute-start | bytes 196616 | tf_op jit(solution)/shard_map/ppermute | solution.py:295
  84.3 0.7 collective-permute-start.16
  85.0 2.2 %collective-permute-done.14.refs_1_ = f32[64,256]{1,0:T(8,128)S(1)} collective-permute-done((f32[64,256]{1,0:T(8,128)S(1)}, f32[64,256]{1,0:T(8,128)S(1)}, u32[]{:S(2)}, u32[]{:S(2)}) %collective-permute-start.14) | collective-permute-done | bytes 65568 | tf_op jit(solution)/shard_map/ppermute | solution.py:295
  87.2 0.3 collective-permute-done.15.refs_2_
  87.5 0.9 collective-permute-done.16.refs_3_
  88.5 0.1 shard_map.76
  88.5 14.2 %all_to_all.22.inc = f32[16,32,256]{2,1,0:T(8,128)S(1)} all-to-all(f32[16,32,256]{2,1,0:T(8,128)S(1)} %shard_map.76), channel_id=1, replica_groups=mesh['y'=4,'core'=2,'z'=4,'x'=4] {'y','x'}, dimensions={0} | all-to-all | bytes 1048576 | tf_op jit(solution)/shard_map/all_to_all | solution.py:277
  102.7 2.6 %collective-permute-start.17 = (f32[4,32,256]{2,1,0:T(8,128)S(1)}, f32[4,32,256]{2,1,0:T(8,128)S(1)}, u32[]{:S(2)}, u32[]{:S(2)}) collective-permute-start(f32[4,32,256]{2,1,0:T(8,128)S(1)} %shard_map.77.own), channel_id=1, source_target_pairs={{0,16},{16,0},{1,17},{17,1},{2,18},{18,2},{3,19},{19,3},{4,20},{20... | collective-permute-start | bytes 393224 | tf_op jit(solution)/shard_map/ppermute | solution.py:299
  105.3 0.7 shard_map.78
  106.0 0.3 collective-permute-done.17.other
  106.3 0.0 copy-done
  106.3 0.9 shard_map.79
  (1 shorter events, 0.0 us)
Async XLA Ops:
  0.6 9.1 %copy-start.1 = (s32[2,32]{1,0:T(2,128)S(1)}, s32[2,32]{1,0:T(2,128)}, u32[]{:S(2)}) copy-start(s32[2,32]{1,0:T(2,128)} %fb.7) | copy-start | bytes 772
  0.6 9.1 %copy-start.2 = (s32[2,4]{1,0:T(2,128)S(1)}, s32[2,4]{1,0:T(2,128)}, u32[]{:S(2)}) copy-start(s32[2,4]{1,0:T(2,128)} %bounds.1) | copy-start | bytes 100
  3.8 18.2 %all-to-all-start = ((f32[8,96,256]{2,1,0:T(8,128)}), f32[8,96,256]{2,1,0:T(8,128)S(1)}, u32[]{:S(2)}, u32[]{:S(2)}) async-start(f32[8,96,256]{2,1,0:T(8,128)} %shard_map.69), calls=%async_computation | async-start | bytes 1572864 | tf_op jit(solution)/shard_map/all_to_all | solution.py:277
  22.6 5.8 %collective-permute-start.1 = (f32[4,32,256]{2,1,0:T(8,128)S(1)}, f32[4,32,256]{2,1,0:T(8,128)S(1)}, u32[]{:S(2)}, u32[]{:S(2)}) collective-permute-start(f32[4,32,256]{2,1,0:T(8,128)S(1)} %get-tuple-element.31.after.refs_0_), channel_id=1, source_target_pairs={{0,96},{32,0},{64,32},{96,64},{1,97},{33,1},{65,33},{97,65},{2,98}... | collective-permute-start | bytes 393224 | tf_op jit(solution)/shard_map/ppermute | solution.py:295
  23.5 5.4 %collective-permute-start = (f32[4,32,256]{2,1,0:T(8,128)S(1)}, f32[4,32,256]{2,1,0:T(8,128)S(1)}, u32[]{:S(2)}, u32[]{:S(2)}) collective-permute-start(f32[4,32,256]{2,1,0:T(8,128)S(1)} %get-tuple-element.31.after.refs_0_), channel_id=1, source_target_pairs={{0,64},{32,96},{64,0},{96,32},{1,65},{33,97},{65,1},{97,33},{2,66}... | collective-permute-start | bytes 393224 | tf_op jit(solution)/shard_map/ppermute | solution.py:295
  24.7 7.8 %collective-permute-start.2 = (f32[4,32,256]{2,1,0:T(8,128)S(1)}, f32[4,32,256]{2,1,0:T(8,128)S(1)}, u32[]{:S(2)}, u32[]{:S(2)}) collective-permute-start(f32[4,32,256]{2,1,0:T(8,128)S(1)} %get-tuple-element.31.after.refs_0_), channel_id=1, source_target_pairs={{0,32},{32,64},{64,96},{96,0},{1,33},{33,65},{65,97},{97,1},{2,34}... | collective-permute-start | bytes 393224 | tf_op jit(solution)/shard_map/ppermute | solution.py:295
  24.7 9.0 %collective-permute-start.3 = (f32[4,32,256]{2,1,0:T(8,128)S(1)}, f32[4,32,256]{2,1,0:T(8,128)S(1)}, u32[]{:S(2)}, u32[]{:S(2)}) collective-permute-start(f32[4,32,256]{2,1,0:T(8,128)S(1)} %get-tuple-element.31.after.refs_0_), channel_id=1, source_target_pairs={{0,16},{16,0},{1,17},{17,1},{2,18},{18,2},{3,19},{19,3},{4,20},{20... | collective-permute-start | bytes 393224 | tf_op jit(solution)/shard_map/ppermute | solution.py:299
  28.9 5.8 %collective-permute-start.6 = (f32[4,32,256]{2,1,0:T(8,128)S(1)}, f32[4,32,256]{2,1,0:T(8,128)S(1)}, u32[]{:S(2)}, u32[]{:S(2)}) collective-permute-start(f32[4,32,256]{2,1,0:T(8,128)S(1)} %collective-permute-done.refs_3_), channel_id=1, source_target_pairs={{0,16},{16,0},{1,17},{17,1},{2,18},{18,2},{3,19},{19,3},{4,20},{20... | collective-permute-start | bytes 393224 | tf_op jit(solution)/shard_map/ppermute | solution.py:299
  32.5 2.3 %collective-permute-start.4 = (f32[4,32,256]{2,1,0:T(8,128)S(1)}, f32[4,32,256]{2,1,0:T(8,128)S(1)}, u32[]{:S(2)}, u32[]{:S(2)}) collective-permute-start(f32[4,32,256]{2,1,0:T(8,128)S(1)} %collective-permute-done.2.refs_1_), channel_id=1, source_target_pairs={{0,16},{16,0},{1,17},{17,1},{2,18},{18,2},{3,19},{19,3},{4,20},{20... | collective-permute-start | bytes 393224 | tf_op jit(solution)/shard_map/ppermute | solution.py:299
  33.7 1.3 %collective-permute-start.5 = (f32[4,32,256]{2,1,0:T(8,128)S(1)}, f32[4,32,256]{2,1,0:T(8,128)S(1)}, u32[]{:S(2)}, u32[]{:S(2)}) collective-permute-start(f32[4,32,256]{2,1,0:T(8,128)S(1)} %collective-permute-done.1.refs_2_), channel_id=1, source_target_pairs={{0,16},{16,0},{1,17},{17,1},{2,18},{18,2},{3,19},{19,3},{4,20},{20... | collective-permute-start | bytes 393224 | tf_op jit(solution)/shard_map/ppermute | solution.py:299
  69.3 37.0 %copy-start = (f32[2,256,256]{2,1,0:T(8,128)S(1)}, f32[2,256,256]{2,1,0:T(8,128)}, u32[]{:S(2)}) copy-start(f32[2,256,256]{2,1,0:T(8,128)} %terms.1) | copy-start | bytes 1572868
  69.3 6.9 %collective-permute-start.7 = (f32[2,64,256]{2,1,0:T(8,128)S(1)}, f32[2,64,256]{2,1,0:T(8,128)S(1)}, u32[]{:S(2)}, u32[]{:S(2)}) collective-permute-start(f32[2,64,256]{2,1,0:T(8,128)S(1)} %get-tuple-element.40), channel_id=1, source_target_pairs={{0,32},{32,64},{64,96},{96,0},{1,33},{33,65},{65,97},{97,1},{2,34}... | collective-permute-start | bytes 393224 | tf_op jit(solution)/shard_map/ppermute | solution.py:295
  69.4 10.3 %collective-permute-start.8 = (f32[2,64,256]{2,1,0:T(8,128)S(1)}, f32[2,64,256]{2,1,0:T(8,128)S(1)}, u32[]{:S(2)}, u32[]{:S(2)}) collective-permute-start(f32[2,64,256]{2,1,0:T(8,128)S(1)} %get-tuple-element.41), channel_id=1, source_target_pairs={{0,64},{32,96},{64,0},{96,32},{1,65},{33,97},{65,1},{97,33},{2,66}... | collective-permute-start | bytes 393224 | tf_op jit(solution)/shard_map/ppermute | solution.py:295
  70.9 8.9 %collective-permute-start.9 = (f32[2,64,256]{2,1,0:T(8,128)S(1)}, f32[2,64,256]{2,1,0:T(8,128)S(1)}, u32[]{:S(2)}, u32[]{:S(2)}) collective-permute-start(f32[2,64,256]{2,1,0:T(8,128)S(1)} %get-tuple-element.42), channel_id=1, source_target_pairs={{0,96},{32,0},{64,32},{96,64},{1,97},{33,1},{65,33},{97,65},{2,98}... | collective-permute-start | bytes 393224 | tf_op jit(solution)/shard_map/ppermute | solution.py:295
  72.7 7.9 %collective-permute-start.10 = (f32[2,64,256]{2,1,0:T(8,128)S(1)}, f32[2,64,256]{2,1,0:T(8,128)S(1)}, u32[]{:S(2)}, u32[]{:S(2)}) collective-permute-start(f32[2,64,256]{2,1,0:T(8,128)S(1)} %get-tuple-element.39.refs_0_), channel_id=1, source_target_pairs={{0,16},{16,0},{1,17},{17,1},{2,18},{18,2},{3,19},{19,3},{4,20},{20... | collective-permute-start | bytes 393224 | tf_op jit(solution)/shard_map/ppermute | solution.py:299
  76.3 4.5 %collective-permute-start.11 = (f32[2,64,256]{2,1,0:T(8,128)S(1)}, f32[2,64,256]{2,1,0:T(8,128)S(1)}, u32[]{:S(2)}, u32[]{:S(2)}) collective-permute-start(f32[2,64,256]{2,1,0:T(8,128)S(1)} %collective-permute-done.7.refs_1_), channel_id=1, source_target_pairs={{0,16},{16,0},{1,17},{17,1},{2,18},{18,2},{3,19},{19,3},{4,20},{20... | collective-permute-start | bytes 393224 | tf_op jit(solution)/shard_map/ppermute | solution.py:299
  79.7 1.3 %collective-permute-start.12 = (f32[2,64,256]{2,1,0:T(8,128)S(1)}, f32[2,64,256]{2,1,0:T(8,128)S(1)}, u32[]{:S(2)}, u32[]{:S(2)}) collective-permute-start(f32[2,64,256]{2,1,0:T(8,128)S(1)} %collective-permute-done.8.refs_2_), channel_id=1, source_target_pairs={{0,16},{16,0},{1,17},{17,1},{2,18},{18,2},{3,19},{19,3},{4,20},{20... | collective-permute-start | bytes 393224 | tf_op jit(solution)/shard_map/ppermute | solution.py:299
  79.8 1.8 %collective-permute-start.13 = (f32[2,64,256]{2,1,0:T(8,128)S(1)}, f32[2,64,256]{2,1,0:T(8,128)S(1)}, u32[]{:S(2)}, u32[]{:S(2)}) collective-permute-start(f32[2,64,256]{2,1,0:T(8,128)S(1)} %collective-permute-done.9.refs_3_), channel_id=1, source_target_pairs={{0,16},{16,0},{1,17},{17,1},{2,18},{18,2},{3,19},{19,3},{4,20},{20... | collective-permute-start | bytes 393224 | tf_op jit(solution)/shard_map/ppermute | solution.py:299
  82.2 5.0 %collective-permute-start.14 = (f32[64,256]{1,0:T(8,128)S(1)}, f32[64,256]{1,0:T(8,128)S(1)}, u32[]{:S(2)}, u32[]{:S(2)}) collective-permute-start(f32[64,256]{1,0:T(8,128)S(1)} %get-tuple-element.44), channel_id=1, source_target_pairs={{0,4},{4,8},{8,12},{12,0},{1,5},{5,9},{9,13},{13,1},{2,6},{6,10},{... | collective-permute-start | bytes 196616 | tf_op jit(solution)/shard_map/ppermute | solution.py:295
  82.6 5.0 %collective-permute-start.15 = (f32[64,256]{1,0:T(8,128)S(1)}, f32[64,256]{1,0:T(8,128)S(1)}, u32[]{:S(2)}, u32[]{:S(2)}) collective-permute-start(f32[64,256]{1,0:T(8,128)S(1)} %get-tuple-element.45), channel_id=1, source_target_pairs={{0,8},{4,12},{8,0},{12,4},{1,9},{5,13},{9,1},{13,5},{2,10},{6,14},... | collective-permute-start | bytes 196616 | tf_op jit(solution)/shard_map/ppermute | solution.py:295
  84.3 4.1 %collective-permute-start.16 = (f32[64,256]{1,0:T(8,128)S(1)}, f32[64,256]{1,0:T(8,128)S(1)}, u32[]{:S(2)}, u32[]{:S(2)}) collective-permute-start(f32[64,256]{1,0:T(8,128)S(1)} %get-tuple-element.46), channel_id=1, source_target_pairs={{0,12},{4,0},{8,4},{12,8},{1,13},{5,1},{9,5},{13,9},{2,14},{6,2},{... | collective-permute-start | bytes 196616 | tf_op jit(solution)/shard_map/ppermute | solution.py:295
  102.7 3.6 %collective-permute-start.17 = (f32[4,32,256]{2,1,0:T(8,128)S(1)}, f32[4,32,256]{2,1,0:T(8,128)S(1)}, u32[]{:S(2)}, u32[]{:S(2)}) collective-permute-start(f32[4,32,256]{2,1,0:T(8,128)S(1)} %shard_map.77.own), channel_id=1, source_target_pairs={{0,16},{16,0},{1,17},{17,1},{2,18},{18,2},{3,19},{19,3},{4,20},{20... | collective-permute-start | bytes 393224 | tf_op jit(solution)/shard_map/ppermute | solution.py:299

commit v10 on v9

--- a/solution.py
+++ b/solution.py
@@ -166,14 +166,18 @@
                     out[first, second, 4 * f + s] = total[at : at + 16, :]
 
 
-def half_kernel(inc, out):
-    for d in range(4):
+def half_kernel(inc, *outs):
+    core = lax.axis_index("core")
+    z, x = lax.axis_index("z"), lax.axis_index("x")
+    here = jnp.where(core == 0, z, x)
+    for step in range(4):
+        d = (here + step) & 3
         for k in range(8):
-            out[d, k] = (inc[0, d, k] + inc[1, d, k]) + (inc[2, d, k] + inc[3, d, k])
-
-
-def reduce_kernel(tab, mask, parts, mine, *refs):
-    outs, buf = refs[:4], refs[4]
+            outs[step][k] = (inc[0, d, k] + inc[1, d, k]) + (inc[2, d, k] + inc[3, d, k])
+
+
+def reduce_kernel(tab, mask, mine, *refs):
+    parts, outs, buf = refs[:4], refs[4:8], refs[8]
     core, here = lax.axis_index("core"), lax.axis_index("y")
     for step in range(4):
         for rel in range(2):
@@ -182,7 +186,7 @@
         rows = []
         for s in range(4):
             k = 4 * f + s
-            v = (parts[0, k] + parts[1, k]) + (parts[2, k] + parts[3, k])
+            v = (parts[0][k] + parts[1][k]) + (parts[2][k] + parts[3][k])
             rows.append(v)
             owner = tab[16 * f + s] >> 2
             step, rel = ((owner >> 1) - here) & 3, (owner & 1) ^ core
@@ -277,14 +281,24 @@
     return lax.all_to_all(v, axes, 0, 0, tiled=True)
 
 
-def grouped(v, stage):
+def grouped(v):
     groups = []
     for line in range(8):
         for o in range(4):
             along_x = [16 * line + 4 * o + i for i in range(4)]
             along_z = [16 * line + 4 * i + o for i in range(4)]
-            groups.append(along_x if line % 2 == stage else along_z)
+            groups.append(along_z if line % 2 else along_x)
     return lax.all_to_all(v, ALL, 0, 0, tiled=True, axis_index_groups=groups)
+
+
+def step_groups(v, step):
+    pairs = []
+    for line in range(8):
+        for z in range(4):
+            for x in range(4):
+                to = (4 * z + (x + step) % 4) if line % 2 else (4 * ((z + step) % 4) + x)
+                pairs.append((16 * line + 4 * z + x, 16 * line + to))
+    return lax.ppermute(v, ALL, pairs)
 
 
 def hbm(v):
@@ -343,16 +357,18 @@
         scratch=[pltpu.VMEM((2, 512, 256), F32)],
         limit=16,
     )(hi0, lo0, hi1, lo1, *own, *other)
-    parts = grouped(parts, 0)
-    parts = call(half_kernel, [VMEM], sds((4, 8, 16, 256)))(parts)
-    parts = grouped(parts, 1)
+    parts = grouped(parts)
+    outs = call(half_kernel, [VMEM], (sds((8, 16, 256)),) * 4)(parts)
+    parts = [outs[0]] + [None] * 3
+    for step in (1, 3, 2):
+        parts[step] = step_groups(outs[step], step)
     pair = sds((2, 64, 256))
     outs = call(
         reduce_kernel,
-        [SMEM, VMEM, VMEM, VMEM],
+        [SMEM] + [VMEM] * 6,
         (pair,) * 4,
         scratch=[pltpu.VMEM((4, 2, 64, 256), F32)],
-    )(tab, mask, parts, mine)
+    )(tab, mask, mine, *parts)
     own = [outs[0]] + [None] * 3
     for step in (1, 3, 2):
         own[step] = shift(outs[step], "y", step)

time: 108 us -> 106 us (0.981)
  blocking collectives: 45.4 us -> 35 us
  starting transfers between devices: 31 us -> 37.4 us
  waiting for transfers between devices: 15.9 us -> 18.3 us
    all_to_all x2 -> x1, blocking collectives: 31.3 us -> 20.3 us  [grouped(): return lax.all_to_all(v, ALL, 0, 0, tiled=True, axis_index_groups=groups)]
    ppermute x0 -> x3, starting transfers between devices: none -> 4.81 us  [step_groups(): return lax.ppermute(v, ALL, pairs)]
    ppermute x0 -> x3, waiting for transfers between devices: none -> 2.57 us  [step_groups(): return lax.ppermute(v, ALL, pairs)]
  transfers between devices with their start and end apart: 19 -> 22, of which waited for: 12 -> 15; matrix products, arithmetic and copies ran while one was open for 0% -> 0% of each run, Pallas kernels for 6% -> 6%
where the time goes in v10:
time: 106 us
  starting transfers between devices  37.4 us (35%)
  blocking collectives  35 us (33%)
  waiting for transfers between devices  18.3 us (17%)
  Pallas kernels  14.1 us (13%)
    all_to_all x1, blocking collectives, grouped(): return lax.all_to_all(v, ALL, 0, 0, tiled=True, axis_index_groups=groups)  20.3 us
    ppermute x9, starting transfers between devices, swap(): return lax.ppermute(v, 'core', [(0, 1), (1, 0)])  17.4 us
    all_to_all x1, blocking collectives, a2a(): return lax.all_to_all(v, axes, 0, 0, tiled=True)  14.7 us
    ppermute x9, starting transfers between devices, shift(): return lax.ppermute(v, axis, [(i, (i + step) % 4) for i in range(4)])  9.24 us
    all_to_all x1, waiting for transfers between devices, a2a(): return lax.all_to_all(v, axes, 0, 0, tiled=True)  9.19 us
    all_to_all x1, starting transfers between devices, a2a(): return lax.all_to_all(v, axes, 0, 0, tiled=True)  6.01 us
    ppermute x3, starting transfers between devices, step_groups(): return lax.ppermute(v, ALL, pairs)  4.81 us
    ppermute x9, waiting for transfers between devices, shift(): return lax.ppermute(v, axis, [(i, (i + step) % 4) for i in range(4)])  3.93 us
  transfers between devices with their start and end apart: 22, of which 15 were waited for; matrix products, arithmetic and copies ran while one was open for 0% of the time, Pallas kernels for 6%

profile of v10, /device:TPU:1, one launch (start us, length us, event | category | flops | bytes accessed | tf_op | source)
XLA Modules:
  0.0 105.6 jit_solution(17324736961629709018)
XLA Ops:
  0.6 0.0 copy-start.1
  0.6 0.0 copy-start.2
  0.7 3.1 %shard_map.69 = f32[8,96,256]{2,1,0:T(8,128)} custom-call(s32[2,32]{1,0:T(2,128)} %fb.7, f32[2,4,8,32,256]{4,3,2,1,0:T(8,128)} %bitcast.1), custom_call_target="tpu_custom_call" | custom-call | tf_op jit(solution)/shard_map/pallas_call | solution.py:317
  3.7 6.0 %all-to-all-start = ((f32[8,96,256]{2,1,0:T(8,128)}), f32[8,96,256]{2,1,0:T(8,128)S(1)}, u32[]{:S(2)}, u32[]{:S(2)}) async-start(f32[8,96,256]{2,1,0:T(8,128)} %shard_map.69), calls=%async_computation | async-start | bytes 1572864 | tf_op jit(solution)/shard_map/all_to_all | solution.py:281
  9.7 0.0 copy-done.1
  9.7 0.0 copy-done.2
  9.8 3.1 %shard_map.68 = (bf16[4,256,512]{2,1,0:T(8,128)(2,1)S(1)}, bf16[4,256,512]{2,1,0:T(8,128)(2,1)S(1)}, s32[32]{0:T(128)S(1)}, f32[2,256,256]{2,1,0:T(8,128)S(1)}) custom-call(s32[2,32]{1,0:T(2,128)S(1)} %copy-done.1, s32[2,4]{1,0:T(2,128)S(1)} %copy-done.2, f32[2048,1024]{1,0:T(8,128)} %inverse.3), custom_call_target="tpu_custom_call" | custom-call | flops 2097152 | bytes 6291456 | tf_op jit(solution)/shard_map/pallas_call | solution.py:332
  12.8 9.2 %all-to-all-done.inc = f32[8,96,256]{2,1,0:T(8,128)S(1)} async-done(((f32[8,96,256]{2,1,0:T(8,128)}), f32[8,96,256]{2,1,0:T(8,128)S(1)}, u32[]{:S(2)}, u32[]{:S(2)}) %all-to-all-start) | async-done | bytes 786464 | tf_op jit(solution)/shard_map/all_to_all | solution.py:281
  22.0 0.6 shard_map.70
  22.6 1.0 collective-permute-start.1
  23.6 1.2 %collective-permute-start = (f32[4,32,256]{2,1,0:T(8,128)S(1)}, f32[4,32,256]{2,1,0:T(8,128)S(1)}, u32[]{:S(2)}, u32[]{:S(2)}) collective-permute-start(f32[4,32,256]{2,1,0:T(8,128)S(1)} %get-tuple-element.36.after.refs_0_), channel_id=1, source_target_pairs={{0,64},{32,96},{64,0},{96,32},{1,65},{33,97},{65,1},{97,33},{2,66}... | collective-permute-start | bytes 393224 | tf_op jit(solution)/shard_map/ppermute | solution.py:309
  24.7 0.0 collective-permute-start.2
  24.7 1.4 %collective-permute-start.3 = (f32[4,32,256]{2,1,0:T(8,128)S(1)}, f32[4,32,256]{2,1,0:T(8,128)S(1)}, u32[]{:S(2)}, u32[]{:S(2)}) collective-permute-start(f32[4,32,256]{2,1,0:T(8,128)S(1)} %get-tuple-element.36.after.refs_0_), channel_id=1, source_target_pairs={{0,16},{16,0},{1,17},{17,1},{2,18},{18,2},{3,19},{19,3},{4,20},{20... | collective-permute-start | bytes 393224 | tf_op jit(solution)/shard_map/ppermute | solution.py:313
  26.2 2.2 %shard_map.71 = (bf16[4,256,512]{2,1,0:T(8,128)(2,1)S(1)}, bf16[4,256,512]{2,1,0:T(8,128)(2,1)S(1)}) custom-call(s32[2,32]{1,0:T(2,128)S(1)} %copy-done.1, s32[32]{0:T(128)S(1)} %get-tuple-element.31.tab, f32[2048,1024]{1,0:T(8,128)} %inverse.3, f32[4,32,256]{2,1,0:T(8,128)S(1)} %get-tuple-element.36.after.refs_0_), custom_call_target="tpu_custom_call" | custom-call | flops 2097152 | bytes 6291456 | tf_op jit(solution)/shard_map/pallas_call | solution.py:347
  28.4 0.0 collective-permute-done.1.refs_2_
  28.4 0.5 collective-permute-done.refs_3_
  28.9 3.5 %collective-permute-start.6 = (f32[4,32,256]{2,1,0:T(8,128)S(1)}, f32[4,32,256]{2,1,0:T(8,128)S(1)}, u32[]{:S(2)}, u32[]{:S(2)}) collective-permute-start(f32[4,32,256]{2,1,0:T(8,128)S(1)} %collective-permute-done.refs_3_), channel_id=1, source_target_pairs={{0,16},{16,0},{1,17},{17,1},{2,18},{18,2},{3,19},{19,3},{4,20},{20... | collective-permute-start | bytes 393224 | tf_op jit(solution)/shard_map/ppermute | solution.py:313
  32.4 0.1 collective-permute-done.2.refs_1_
  32.5 1.3 %collective-permute-start.4 = (f32[4,32,256]{2,1,0:T(8,128)S(1)}, f32[4,32,256]{2,1,0:T(8,128)S(1)}, u32[]{:S(2)}, u32[]{:S(2)}) collective-permute-start(f32[4,32,256]{2,1,0:T(8,128)S(1)} %collective-permute-done.2.refs_1_), channel_id=1, source_target_pairs={{0,16},{16,0},{1,17},{17,1},{2,18},{18,2},{3,19},{19,3},{4,20},{20... | collective-permute-start | bytes 393224 | tf_op jit(solution)/shard_map/ppermute | solution.py:313
  33.8 0.0 collective-permute-start.5
  33.8 0.0 collective-permute-done.3.refs_4_
  33.8 1.0 collective-permute-done.4.refs_5_
  34.8 0.0 collective-permute-done.6.refs_7_
  34.8 0.4 collective-permute-done.5.refs_6_
  35.1 1.9 %shard_map.72 = f32[4,4,8,16,256]{4,3,2,1,0:T(8,128)S(1)} custom-call(bf16[4,256,512]{2,1,0:T(8,128)(2,1)S(1)} %get-tuple-element.34.hi0, bf16[4,256,512]{2,1,0:T(8,128)(2,1)S(1)} %get-tuple-element.35.lo0, bf16[4,256,512]{2,1,0:T(8,128)(2,1)S(1)} %get-tuple-element.39.hi1, bf16[4,256,512]{2,1,0:T(8,128)(2,1)S(1)} %get-tuple-element.40.lo1, ...), custom_call_target="tpu_custom_call" | custom-call | tf_op jit(solution)/shard_map/pallas_call | solution.py:353
  37.0 20.3 %all_to_all.15.inc = f32[4,4,8,16,256]{4,3,2,1,0:T(8,128)S(1)} all-to-all(f32[4,4,8,16,256]{4,3,2,1,0:T(8,128)S(1)} %shard_map.72), channel_id=1, replica_groups={{0,1,2,3},{4,5,6,7},{8,9,10,11},{12,13,14,15},{16,20,24,28},{17,21,25,2..., dimensions={0} | all-to-all | bytes 4194304 | tf_op jit(solution)/shard_map/all_to_all | solution.py:291
  57.3 0.1 shard_map.73
  57.4 1.2 %collective-permute-start.7 = (f32[8,16,256]{2,1,0:T(8,128)S(1)}, f32[8,16,256]{2,1,0:T(8,128)S(1)}, u32[]{:S(2)}, u32[]{:S(2)}) collective-permute-start(f32[8,16,256]{2,1,0:T(8,128)S(1)} %get-tuple-element.44), channel_id=1, source_target_pairs={{0,4},{1,5},{2,6},{3,7},{4,8},{5,9},{6,10},{7,11},{8,12},{9,13},{1... | collective-permute-start | bytes 393224 | tf_op jit(solution)/shard_map/ppermute | solution.py:301
  58.6 2.3 %collective-permute-start.8 = (f32[8,16,256]{2,1,0:T(8,128)S(1)}, f32[8,16,256]{2,1,0:T(8,128)S(1)}, u32[]{:S(2)}, u32[]{:S(2)}) collective-permute-start(f32[8,16,256]{2,1,0:T(8,128)S(1)} %get-tuple-element.45), channel_id=1, source_target_pairs={{0,8},{1,9},{2,10},{3,11},{4,12},{5,13},{6,14},{7,15},{8,0},{9,1},... | collective-permute-start | bytes 393224 | tf_op jit(solution)/shard_map/ppermute | solution.py:301
  61.0 1.3 %collective-permute-start.9 = (f32[8,16,256]{2,1,0:T(8,128)S(1)}, f32[8,16,256]{2,1,0:T(8,128)S(1)}, u32[]{:S(2)}, u32[]{:S(2)}) collective-permute-start(f32[8,16,256]{2,1,0:T(8,128)S(1)} %get-tuple-element.46), channel_id=1, source_target_pairs={{0,12},{1,13},{2,14},{3,15},{4,0},{5,1},{6,2},{7,3},{8,4},{9,5},{1... | collective-permute-start | bytes 393224 | tf_op jit(solution)/shard_map/ppermute | solution.py:301
  62.2 0.3 collective-permute-done.7.refs_1_
  62.5 2.2 %collective-permute-done.8.refs_2_ = f32[8,16,256]{2,1,0:T(8,128)S(1)} collective-permute-done((f32[8,16,256]{2,1,0:T(8,128)S(1)}, f32[8,16,256]{2,1,0:T(8,128)S(1)}, u32[]{:S(2)}, u32[]{:S(2)}) %collective-permute-start.8) | collective-permute-done | bytes 131104 | tf_op jit(solution)/shard_map/ppermute | solution.py:301
  64.7 0.1 collective-permute-done.9.refs_3_
  64.8 1.0 shard_map.74
  65.8 0.0 copy-start
  65.8 0.1 collective-permute-start.10
  65.9 1.5 %collective-permute-start.11 = (f32[2,64,256]{2,1,0:T(8,128)S(1)}, f32[2,64,256]{2,1,0:T(8,128)S(1)}, u32[]{:S(2)}, u32[]{:S(2)}) collective-permute-start(f32[2,64,256]{2,1,0:T(8,128)S(1)} %get-tuple-element.49), channel_id=1, source_target_pairs={{0,64},{32,96},{64,0},{96,32},{1,65},{33,97},{65,1},{97,33},{2,66}... | collective-permute-start | bytes 393224 | tf_op jit(solution)/shard_map/ppermute | solution.py:309
  67.3 1.8 %collective-permute-start.12 = (f32[2,64,256]{2,1,0:T(8,128)S(1)}, f32[2,64,256]{2,1,0:T(8,128)S(1)}, u32[]{:S(2)}, u32[]{:S(2)}) collective-permute-start(f32[2,64,256]{2,1,0:T(8,128)S(1)} %get-tuple-element.50), channel_id=1, source_target_pairs={{0,96},{32,0},{64,32},{96,64},{1,97},{33,1},{65,33},{97,65},{2,98}... | collective-permute-start | bytes 393224 | tf_op jit(solution)/shard_map/ppermute | solution.py:309
  69.1 4.5 %collective-permute-start.13 = (f32[2,64,256]{2,1,0:T(8,128)S(1)}, f32[2,64,256]{2,1,0:T(8,128)S(1)}, u32[]{:S(2)}, u32[]{:S(2)}) collective-permute-start(f32[2,64,256]{2,1,0:T(8,128)S(1)} %get-tuple-element.47.refs_0_), channel_id=1, source_target_pairs={{0,16},{16,0},{1,17},{17,1},{2,18},{18,2},{3,19},{19,3},{4,20},{20... | collective-permute-start | bytes 393224 | tf_op jit(solution)/shard_map/ppermute | solution.py:313
  73.6 0.0 collective-permute-done.10.refs_1_
  73.6 3.5 %collective-permute-start.14 = (f32[2,64,256]{2,1,0:T(8,128)S(1)}, f32[2,64,256]{2,1,0:T(8,128)S(1)}, u32[]{:S(2)}, u32[]{:S(2)}) collective-permute-start(f32[2,64,256]{2,1,0:T(8,128)S(1)} %collective-permute-done.10.refs_1_), channel_id=1, source_target_pairs={{0,16},{16,0},{1,17},{17,1},{2,18},{18,2},{3,19},{19,3},{4,20},{20... | collective-permute-start | bytes 393224 | tf_op jit(solution)/shard_map/ppermute | solution.py:313
  77.1 0.0 collective-permute-done.11.refs_2_
  77.1 0.0 collective-permute-start.15
  77.1 0.0 collective-permute-done.12.refs_3_
  77.1 0.8 collective-permute-start.16
  78.0 0.0 collective-permute-done.13.refs_4_
  78.0 0.1 collective-permute-done.14.refs_5_
  78.1 0.4 collective-permute-done.15.refs_6_
  78.5 0.5 collective-permute-done.16.refs_7_
  79.0 0.6 shard_map.75
  79.6 0.7 collective-permute-start.17
  80.3 2.5 %collective-permute-start.18 = (f32[64,256]{1,0:T(8,128)S(1)}, f32[64,256]{1,0:T(8,128)S(1)}, u32[]{:S(2)}, u32[]{:S(2)}) collective-permute-start(f32[64,256]{1,0:T(8,128)S(1)} %get-tuple-element.53), channel_id=1, source_target_pairs={{0,8},{4,12},{8,0},{12,4},{1,9},{5,13},{9,1},{13,5},{2,10},{6,14},... | collective-permute-start | bytes 196616 | tf_op jit(solution)/shard_map/ppermute | solution.py:309
  82.8 0.6 collective-permute-start.19
  83.4 0.6 collective-permute-done.17.refs_1_
  84.0 1.8 %collective-permute-done.18.refs_2_ = f32[64,256]{1,0:T(8,128)S(1)} collective-permute-done((f32[64,256]{1,0:T(8,128)S(1)}, f32[64,256]{1,0:T(8,128)S(1)}, u32[]{:S(2)}, u32[]{:S(2)}) %collective-permute-start.18) | collective-permute-done | bytes 65568 | tf_op jit(solution)/shard_map/ppermute | solution.py:309
  85.8 0.9 collective-permute-done.19.refs_3_
  86.7 0.1 shard_map.76
  86.7 14.7 %all_to_all.16.inc = f32[16,32,256]{2,1,0:T(8,128)S(1)} all-to-all(f32[16,32,256]{2,1,0:T(8,128)S(1)} %shard_map.76), channel_id=1, replica_groups=mesh['y'=4,'core'=2,'z'=4,'x'=4] {'y','x'}, dimensions={0} | all-to-all | bytes 1048576 | tf_op jit(solution)/shard_map/all_to_all | solution.py:281
  101.4 2.3 %collective-permute-start.20 = (f32[4,32,256]{2,1,0:T(8,128)S(1)}, f32[4,32,256]{2,1,0:T(8,128)S(1)}, u32[]{:S(2)}, u32[]{:S(2)}) collective-permute-start(f32[4,32,256]{2,1,0:T(8,128)S(1)} %shard_map.77.own), channel_id=1, source_target_pairs={{0,16},{16,0},{1,17},{17,1},{2,18},{18,2},{3,19},{19,3},{4,20},{20... | collective-permute-start | bytes 393224 | tf_op jit(solution)/shard_map/ppermute | solution.py:313
  103.7 0.7 shard_map.78
  104.4 0.3 collective-permute-done.20.other
  104.7 0.0 copy-done
  104.7 0.9 shard_map.79
  (1 shorter events, 0.0 us)
Async XLA Ops:
  0.6 9.1 %copy-start.1 = (s32[2,32]{1,0:T(2,128)S(1)}, s32[2,32]{1,0:T(2,128)}, u32[]{:S(2)}) copy-start(s32[2,32]{1,0:T(2,128)} %fb.7) | copy-start | bytes 772
  0.6 9.1 %copy-start.2 = (s32[2,4]{1,0:T(2,128)S(1)}, s32[2,4]{1,0:T(2,128)}, u32[]{:S(2)}) copy-start(s32[2,4]{1,0:T(2,128)} %bounds.1) | copy-start | bytes 100
  3.7 18.3 %all-to-all-start = ((f32[8,96,256]{2,1,0:T(8,128)}), f32[8,96,256]{2,1,0:T(8,128)S(1)}, u32[]{:S(2)}, u32[]{:S(2)}) async-start(f32[8,96,256]{2,1,0:T(8,128)} %shard_map.69), calls=%async_computation | async-start | bytes 1572864 | tf_op jit(solution)/shard_map/all_to_all | solution.py:281
  22.6 5.8 %collective-permute-start.1 = (f32[4,32,256]{2,1,0:T(8,128)S(1)}, f32[4,32,256]{2,1,0:T(8,128)S(1)}, u32[]{:S(2)}, u32[]{:S(2)}) collective-permute-start(f32[4,32,256]{2,1,0:T(8,128)S(1)} %get-tuple-element.36.after.refs_0_), channel_id=1, source_target_pairs={{0,96},{32,0},{64,32},{96,64},{1,97},{33,1},{65,33},{97,65},{2,98}... | collective-permute-start | bytes 393224 | tf_op jit(solution)/shard_map/ppermute | solution.py:309
  23.6 5.4 %collective-permute-start = (f32[4,32,256]{2,1,0:T(8,128)S(1)}, f32[4,32,256]{2,1,0:T(8,128)S(1)}, u32[]{:S(2)}, u32[]{:S(2)}) collective-permute-start(f32[4,32,256]{2,1,0:T(8,128)S(1)} %get-tuple-element.36.after.refs_0_), channel_id=1, source_target_pairs={{0,64},{32,96},{64,0},{96,32},{1,65},{33,97},{65,1},{97,33},{2,66}... | collective-permute-start | bytes 393224 | tf_op jit(solution)/shard_map/ppermute | solution.py:309
  24.7 7.8 %collective-permute-start.2 = (f32[4,32,256]{2,1,0:T(8,128)S(1)}, f32[4,32,256]{2,1,0:T(8,128)S(1)}, u32[]{:S(2)}, u32[]{:S(2)}) collective-permute-start(f32[4,32,256]{2,1,0:T(8,128)S(1)} %get-tuple-element.36.after.refs_0_), channel_id=1, source_target_pairs={{0,32},{32,64},{64,96},{96,0},{1,33},{33,65},{65,97},{97,1},{2,34}... | collective-permute-start | bytes 393224 | tf_op jit(solution)/shard_map/ppermute | solution.py:309
  24.7 9.0 %collective-permute-start.3 = (f32[4,32,256]{2,1,0:T(8,128)S(1)}, f32[4,32,256]{2,1,0:T(8,128)S(1)}, u32[]{:S(2)}, u32[]{:S(2)}) collective-permute-start(f32[4,32,256]{2,1,0:T(8,128)S(1)} %get-tuple-element.36.after.refs_0_), channel_id=1, source_target_pairs={{0,16},{16,0},{1,17},{17,1},{2,18},{18,2},{3,19},{19,3},{4,20},{20... | collective-permute-start | bytes 393224 | tf_op jit(solution)/shard_map/ppermute | solution.py:313
  28.9 5.8 %collective-permute-start.6 = (f32[4,32,256]{2,1,0:T(8,128)S(1)}, f32[4,32,256]{2,1,0:T(8,128)S(1)}, u32[]{:S(2)}, u32[]{:S(2)}) collective-permute-start(f32[4,32,256]{2,1,0:T(8,128)S(1)} %collective-permute-done.refs_3_), channel_id=1, source_target_pairs={{0,16},{16,0},{1,17},{17,1},{2,18},{18,2},{3,19},{19,3},{4,20},{20... | collective-permute-start | bytes 393224 | tf_op jit(solution)/shard_map/ppermute | solution.py:313
  32.5 2.3 %collective-permute-start.4 = (f32[4,32,256]{2,1,0:T(8,128)S(1)}, f32[4,32,256]{2,1,0:T(8,128)S(1)}, u32[]{:S(2)}, u32[]{:S(2)}) collective-permute-start(f32[4,32,256]{2,1,0:T(8,128)S(1)} %collective-permute-done.2.refs_1_), channel_id=1, source_target_pairs={{0,16},{16,0},{1,17},{17,1},{2,18},{18,2},{3,19},{19,3},{4,20},{20... | collective-permute-start | bytes 393224 | tf_op jit(solution)/shard_map/ppermute | solution.py:313
  33.8 1.3 %collective-permute-start.5 = (f32[4,32,256]{2,1,0:T(8,128)S(1)}, f32[4,32,256]{2,1,0:T(8,128)S(1)}, u32[]{:S(2)}, u32[]{:S(2)}) collective-permute-start(f32[4,32,256]{2,1,0:T(8,128)S(1)} %collective-permute-done.1.refs_2_), channel_id=1, source_target_pairs={{0,16},{16,0},{1,17},{17,1},{2,18},{18,2},{3,19},{19,3},{4,20},{20... | collective-permute-start | bytes 393224 | tf_op jit(solution)/shard_map/ppermute | solution.py:313
  57.4 5.1 %collective-permute-start.7 = (f32[8,16,256]{2,1,0:T(8,128)S(1)}, f32[8,16,256]{2,1,0:T(8,128)S(1)}, u32[]{:S(2)}, u32[]{:S(2)}) collective-permute-start(f32[8,16,256]{2,1,0:T(8,128)S(1)} %get-tuple-element.44), channel_id=1, source_target_pairs={{0,4},{1,5},{2,6},{3,7},{4,8},{5,9},{6,10},{7,11},{8,12},{9,13},{1... | collective-permute-start | bytes 393224 | tf_op jit(solution)/shard_map/ppermute | solution.py:301
  58.6 6.1 %collective-permute-start.8 = (f32[8,16,256]{2,1,0:T(8,128)S(1)}, f32[8,16,256]{2,1,0:T(8,128)S(1)}, u32[]{:S(2)}, u32[]{:S(2)}) collective-permute-start(f32[8,16,256]{2,1,0:T(8,128)S(1)} %get-tuple-element.45), channel_id=1, source_target_pairs={{0,8},{1,9},{2,10},{3,11},{4,12},{5,13},{6,14},{7,15},{8,0},{9,1},... | collective-permute-start | bytes 393224 | tf_op jit(solution)/shard_map/ppermute | solution.py:301
  61.0 3.8 %collective-permute-start.9 = (f32[8,16,256]{2,1,0:T(8,128)S(1)}, f32[8,16,256]{2,1,0:T(8,128)S(1)}, u32[]{:S(2)}, u32[]{:S(2)}) collective-permute-start(f32[8,16,256]{2,1,0:T(8,128)S(1)} %get-tuple-element.46), channel_id=1, source_target_pairs={{0,12},{1,13},{2,14},{3,15},{4,0},{5,1},{6,2},{7,3},{8,4},{9,5},{1... | collective-permute-start | bytes 393224 | tf_op jit(solution)/shard_map/ppermute | solution.py:301
  65.8 39.0 %copy-start = (f32[2,256,256]{2,1,0:T(8,128)S(1)}, f32[2,256,256]{2,1,0:T(8,128)}, u32[]{:S(2)}) copy-start(f32[2,256,256]{2,1,0:T(8,128)} %terms.1) | copy-start | bytes 1572868
  65.8 7.9 %collective-permute-start.10 = (f32[2,64,256]{2,1,0:T(8,128)S(1)}, f32[2,64,256]{2,1,0:T(8,128)S(1)}, u32[]{:S(2)}, u32[]{:S(2)}) collective-permute-start(f32[2,64,256]{2,1,0:T(8,128)S(1)} %get-tuple-element.48), channel_id=1, source_target_pairs={{0,32},{32,64},{64,96},{96,0},{1,33},{33,65},{65,97},{97,1},{2,34}... | collective-permute-start | bytes 393224 | tf_op jit(solution)/shard_map/ppermute | solution.py:309
  65.9 11.3 %collective-permute-start.11 = (f32[2,64,256]{2,1,0:T(8,128)S(1)}, f32[2,64,256]{2,1,0:T(8,128)S(1)}, u32[]{:S(2)}, u32[]{:S(2)}) collective-permute-start(f32[2,64,256]{2,1,0:T(8,128)S(1)} %get-tuple-element.49), channel_id=1, source_target_pairs={{0,64},{32,96},{64,0},{96,32},{1,65},{33,97},{65,1},{97,33},{2,66}... | collective-permute-start | bytes 393224 | tf_op jit(solution)/shard_map/ppermute | solution.py:309
  67.3 9.8 %collective-permute-start.12 = (f32[2,64,256]{2,1,0:T(8,128)S(1)}, f32[2,64,256]{2,1,0:T(8,128)S(1)}, u32[]{:S(2)}, u32[]{:S(2)}) collective-permute-start(f32[2,64,256]{2,1,0:T(8,128)S(1)} %get-tuple-element.50), channel_id=1, source_target_pairs={{0,96},{32,0},{64,32},{96,64},{1,97},{33,1},{65,33},{97,65},{2,98}... | collective-permute-start | bytes 393224 | tf_op jit(solution)/shard_map/ppermute | solution.py:309
  69.1 8.9 %collective-permute-start.13 = (f32[2,64,256]{2,1,0:T(8,128)S(1)}, f32[2,64,256]{2,1,0:T(8,128)S(1)}, u32[]{:S(2)}, u32[]{:S(2)}) collective-permute-start(f32[2,64,256]{2,1,0:T(8,128)S(1)} %get-tuple-element.47.refs_0_), channel_id=1, source_target_pairs={{0,16},{16,0},{1,17},{17,1},{2,18},{18,2},{3,19},{19,3},{4,20},{20... | collective-permute-start | bytes 393224 | tf_op jit(solution)/shard_map/ppermute | solution.py:313
  73.6 4.5 %collective-permute-start.14 = (f32[2,64,256]{2,1,0:T(8,128)S(1)}, f32[2,64,256]{2,1,0:T(8,128)S(1)}, u32[]{:S(2)}, u32[]{:S(2)}) collective-permute-start(f32[2,64,256]{2,1,0:T(8,128)S(1)} %collective-permute-done.10.refs_1_), channel_id=1, source_target_pairs={{0,16},{16,0},{1,17},{17,1},{2,18},{18,2},{3,19},{19,3},{4,20},{20... | collective-permute-start | bytes 393224 | tf_op jit(solution)/shard_map/ppermute | solution.py:313
  77.1 1.3 %collective-permute-start.15 = (f32[2,64,256]{2,1,0:T(8,128)S(1)}, f32[2,64,256]{2,1,0:T(8,128)S(1)}, u32[]{:S(2)}, u32[]{:S(2)}) collective-permute-start(f32[2,64,256]{2,1,0:T(8,128)S(1)} %collective-permute-done.11.refs_2_), channel_id=1, source_target_pairs={{0,16},{16,0},{1,17},{17,1},{2,18},{18,2},{3,19},{19,3},{4,20},{20... | collective-permute-start | bytes 393224 | tf_op jit(solution)/shard_map/ppermute | solution.py:313
  77.1 1.8 %collective-permute-start.16 = (f32[2,64,256]{2,1,0:T(8,128)S(1)}, f32[2,64,256]{2,1,0:T(8,128)S(1)}, u32[]{:S(2)}, u32[]{:S(2)}) collective-permute-start(f32[2,64,256]{2,1,0:T(8,128)S(1)} %collective-permute-done.12.refs_3_), channel_id=1, source_target_pairs={{0,16},{16,0},{1,17},{17,1},{2,18},{18,2},{3,19},{19,3},{4,20},{20... | collective-permute-start | bytes 393224 | tf_op jit(solution)/shard_map/ppermute | solution.py:313
  79.6 4.4 %collective-permute-start.17 = (f32[64,256]{1,0:T(8,128)S(1)}, f32[64,256]{1,0:T(8,128)S(1)}, u32[]{:S(2)}, u32[]{:S(2)}) collective-permute-start(f32[64,256]{1,0:T(8,128)S(1)} %get-tuple-element.52), channel_id=1, source_target_pairs={{0,4},{4,8},{8,12},{12,0},{1,5},{5,9},{9,13},{13,1},{2,6},{6,10},{... | collective-permute-start | bytes 196616 | tf_op jit(solution)/shard_map/ppermute | solution.py:309
  80.3 5.5 %collective-permute-start.18 = (f32[64,256]{1,0:T(8,128)S(1)}, f32[64,256]{1,0:T(8,128)S(1)}, u32[]{:S(2)}, u32[]{:S(2)}) collective-permute-start(f32[64,256]{1,0:T(8,128)S(1)} %get-tuple-element.53), channel_id=1, source_target_pairs={{0,8},{4,12},{8,0},{12,4},{1,9},{5,13},{9,1},{13,5},{2,10},{6,14},... | collective-permute-start | bytes 196616 | tf_op jit(solution)/shard_map/ppermute | solution.py:309
  82.8 3.9 %collective-permute-start.19 = (f32[64,256]{1,0:T(8,128)S(1)}, f32[64,256]{1,0:T(8,128)S(1)}, u32[]{:S(2)}, u32[]{:S(2)}) collective-permute-start(f32[64,256]{1,0:T(8,128)S(1)} %get-tuple-element.54), channel_id=1, source_target_pairs={{0,12},{4,0},{8,4},{12,8},{1,13},{5,1},{9,5},{13,9},{2,14},{6,2},{... | collective-permute-start | bytes 196616 | tf_op jit(solution)/shard_map/ppermute | solution.py:309
  101.4 3.3 %collective-permute-start.20 = (f32[4,32,256]{2,1,0:T(8,128)S(1)}, f32[4,32,256]{2,1,0:T(8,128)S(1)}, u32[]{:S(2)}, u32[]{:S(2)}) collective-permute-start(f32[4,32,256]{2,1,0:T(8,128)S(1)} %shard_map.77.own), channel_id=1, source_target_pairs={{0,16},{16,0},{1,17},{17,1},{2,18},{18,2},{3,19},{19,3},{4,20},{20... | collective-permute-start | bytes 393224 | tf_op jit(solution)/shard_map/ppermute | solution.py:313

commit v11 on v10

--- a/solution.py
+++ b/solution.py
@@ -145,7 +145,7 @@
     own, other, (out, whole) = refs[:4], refs[4:8], refs[8:]
     here = lax.axis_index("y")
     core = lax.axis_index("core")
-    for step, mine, theirs in zip((0, 1, 3, 2), own, other):
+    for step, mine, theirs in zip((0, 2, 1, 3), own, other):
         y = (here - step) & 3
         for k in range(4):
             base = 256 * (k % 2) + 64 * y
@@ -342,7 +342,7 @@
         pick_kernel, [SMEM, VMEM], (sds((4, 32, 256)), sds((8, 16, 256)))
     )(tab, incoming)
     own = [slices]
-    for step in (1, 3, 2):
+    for step in (2, 1, 3):
         own.append(shift(slices, "y", step))
     hi1, lo1 = call(
         second_kernel, [SMEM, SMEM, ANY, ANY], tiles, scratch=buffers, limit=16, cost=cost
@@ -360,7 +360,7 @@
     parts = grouped(parts)
     outs = call(half_kernel, [VMEM], (sds((8, 16, 256)),) * 4)(parts)
     parts = [outs[0]] + [None] * 3
-    for step in (1, 3, 2):
+    for step in (2, 1, 3):
         parts[step] = step_groups(outs[step], step)
     pair = sds((2, 64, 256))
     outs = call(
@@ -370,7 +370,7 @@
         scratch=[pltpu.VMEM((4, 2, 64, 256), F32)],
     )(tab, mask, mine, *parts)
     own = [outs[0]] + [None] * 3
-    for step in (1, 3, 2):
+    for step in (2, 1, 3):
         own[step] = shift(outs[step], "y", step)
     other = [swap(v) for v in own]
     outs = call(
@@ -380,7 +380,7 @@
         scratch=[pltpu.VMEM((2, 4, 32, 256), F32)],
     )(fb, *own, *other)
     v = [outs[0]] + [None] * 3
-    for step in (1, 3, 2):
+    for step in (2, 1, 3):
         v[step] = shift(outs[step], "z", step)
     sums = call(
         spread_kernel,

time: 106 us -> 105 us (level)
  transfers between devices with their start and end apart: 22 -> 22, of which waited for: 15 -> 12; matrix products, arithmetic and copies ran while one was open for 0% -> 0% of each run, Pallas kernels for 6% -> 6%
where the time goes in v11:
time: 105 us
  starting transfers between devices  37.9 us (36%)
  blocking collectives  34.3 us (33%)
  waiting for transfers between devices  17.9 us (17%)
  Pallas kernels  14.1 us (13%)
    all_to_all x1, blocking collectives, grouped(): return lax.all_to_all(v, ALL, 0, 0, tiled=True, axis_index_groups=groups)  20.4 us
    ppermute x9, starting transfers between devices, swap(): return lax.ppermute(v, 'core', [(0, 1), (1, 0)])  17.3 us
    all_to_all x1, blocking collectives, a2a(): return lax.all_to_all(v, axes, 0, 0, tiled=True)  13.9 us
    ppermute x9, starting transfers between devices, shift(): return lax.ppermute(v, axis, [(i, (i + step) % 4) for i in range(4)])  9.98 us
    all_to_all x1, waiting for transfers between devices, a2a(): return lax.all_to_all(v, axes, 0, 0, tiled=True)  9.19 us
    all_to_all x1, starting transfers between devices, a2a(): return lax.all_to_all(v, axes, 0, 0, tiled=True)  5.98 us
    ppermute x3, starting transfers between devices, step_groups(): return lax.ppermute(v, ALL, pairs)  4.73 us
    ppermute x9, waiting for transfers between devices, shift(): return lax.ppermute(v, axis, [(i, (i + step) % 4) for i in range(4)])  3.32 us
  transfers between devices with their start and end apart: 22, of which 12 were waited for; matrix products, arithmetic and copies ran while one was open for 0% of the time, Pallas kernels for 6%

profile of v11, /device:TPU:1, one launch (start us, length us, event | category | flops | bytes accessed | tf_op | source)
XLA Modules:
  0.0 105.0 jit_solution(4215910718444874205)
XLA Ops:
  0.6 0.0 copy-start.1
  0.6 0.0 copy-start.2
  0.7 3.1 %shard_map.69 = f32[8,96,256]{2,1,0:T(8,128)} custom-call(s32[2,32]{1,0:T(2,128)} %fb.7, f32[2,4,8,32,256]{4,3,2,1,0:T(8,128)} %bitcast.1), custom_call_target="tpu_custom_call" | custom-call | tf_op jit(solution)/shard_map/pallas_call | solution.py:317
  3.8 6.0 %all-to-all-start = ((f32[8,96,256]{2,1,0:T(8,128)}), f32[8,96,256]{2,1,0:T(8,128)S(1)}, u32[]{:S(2)}, u32[]{:S(2)}) async-start(f32[8,96,256]{2,1,0:T(8,128)} %shard_map.69), calls=%async_computation | async-start | bytes 1572864 | tf_op jit(solution)/shard_map/all_to_all | solution.py:281
  9.7 0.0 copy-done.1
  9.7 0.0 copy-done.2
  9.7 3.1 %shard_map.68 = (bf16[4,256,512]{2,1,0:T(8,128)(2,1)S(1)}, bf16[4,256,512]{2,1,0:T(8,128)(2,1)S(1)}, s32[32]{0:T(128)S(1)}, f32[2,256,256]{2,1,0:T(8,128)S(1)}) custom-call(s32[2,32]{1,0:T(2,128)S(1)} %copy-done.1, s32[2,4]{1,0:T(2,128)S(1)} %copy-done.2, f32[2048,1024]{1,0:T(8,128)} %inverse.3), custom_call_target="tpu_custom_call" | custom-call | flops 2097152 | bytes 6291456 | tf_op jit(solution)/shard_map/pallas_call | solution.py:332
  12.8 9.2 %all-to-all-done.inc = f32[8,96,256]{2,1,0:T(8,128)S(1)} async-done(((f32[8,96,256]{2,1,0:T(8,128)}), f32[8,96,256]{2,1,0:T(8,128)S(1)}, u32[]{:S(2)}, u32[]{:S(2)}) %all-to-all-start) | async-done | bytes 786464 | tf_op jit(solution)/shard_map/all_to_all | solution.py:281
  22.0 0.6 shard_map.70
  22.6 0.4 collective-permute-start.1
  23.0 2.4 %collective-permute-start = (f32[4,32,256]{2,1,0:T(8,128)S(1)}, f32[4,32,256]{2,1,0:T(8,128)S(1)}, u32[]{:S(2)}, u32[]{:S(2)}) collective-permute-start(f32[4,32,256]{2,1,0:T(8,128)S(1)} %get-tuple-element.36.after.refs_0_), channel_id=1, source_target_pairs={{0,96},{32,0},{64,32},{96,64},{1,97},{33,1},{65,33},{97,65},{2,98}... | collective-permute-start | bytes 393224 | tf_op jit(solution)/shard_map/ppermute | solution.py:309
  25.3 0.0 collective-permute-start.2
  25.3 1.4 %collective-permute-start.3 = (f32[4,32,256]{2,1,0:T(8,128)S(1)}, f32[4,32,256]{2,1,0:T(8,128)S(1)}, u32[]{:S(2)}, u32[]{:S(2)}) collective-permute-start(f32[4,32,256]{2,1,0:T(8,128)S(1)} %get-tuple-element.36.after.refs_0_), channel_id=1, source_target_pairs={{0,16},{16,0},{1,17},{17,1},{2,18},{18,2},{3,19},{19,3},{4,20},{20... | collective-permute-start | bytes 393224 | tf_op jit(solution)/shard_map/ppermute | solution.py:313
  26.8 2.2 %shard_map.71 = (bf16[4,256,512]{2,1,0:T(8,128)(2,1)S(1)}, bf16[4,256,512]{2,1,0:T(8,128)(2,1)S(1)}) custom-call(s32[2,32]{1,0:T(2,128)S(1)} %copy-done.1, s32[32]{0:T(128)S(1)} %get-tuple-element.31.tab, f32[2048,1024]{1,0:T(8,128)} %inverse.3, f32[4,32,256]{2,1,0:T(8,128)S(1)} %get-tuple-element.36.after.refs_0_), custom_call_target="tpu_custom_call" | custom-call | flops 2097152 | bytes 6291456 | tf_op jit(solution)/shard_map/pallas_call | solution.py:347
  29.0 0.0 collective-permute-done.1.refs_2_
  29.0 0.0 collective-permute-done.refs_3_
  29.0 2.9 %collective-permute-start.6 = (f32[4,32,256]{2,1,0:T(8,128)S(1)}, f32[4,32,256]{2,1,0:T(8,128)S(1)}, u32[]{:S(2)}, u32[]{:S(2)}) collective-permute-start(f32[4,32,256]{2,1,0:T(8,128)S(1)} %collective-permute-done.refs_3_), channel_id=1, source_target_pairs={{0,16},{16,0},{1,17},{17,1},{2,18},{18,2},{3,19},{19,3},{4,20},{20... | collective-permute-start | bytes 393224 | tf_op jit(solution)/shard_map/ppermute | solution.py:313
  31.9 0.0 collective-permute-done.2.refs_1_
  31.9 1.3 %collective-permute-start.4 = (f32[4,32,256]{2,1,0:T(8,128)S(1)}, f32[4,32,256]{2,1,0:T(8,128)S(1)}, u32[]{:S(2)}, u32[]{:S(2)}) collective-permute-start(f32[4,32,256]{2,1,0:T(8,128)S(1)} %collective-permute-done.2.refs_1_), channel_id=1, source_target_pairs={{0,16},{16,0},{1,17},{17,1},{2,18},{18,2},{3,19},{19,3},{4,20},{20... | collective-permute-start | bytes 393224 | tf_op jit(solution)/shard_map/ppermute | solution.py:313
  33.2 0.0 collective-permute-start.5
  33.3 0.0 collective-permute-done.3.refs_4_
  33.3 1.0 collective-permute-done.4.refs_5_
  34.2 0.0 collective-permute-done.6.refs_7_
  34.2 0.4 collective-permute-done.5.refs_6_
  34.6 1.9 %shard_map.72 = f32[4,4,8,16,256]{4,3,2,1,0:T(8,128)S(1)} custom-call(bf16[4,256,512]{2,1,0:T(8,128)(2,1)S(1)} %get-tuple-element.34.hi0, bf16[4,256,512]{2,1,0:T(8,128)(2,1)S(1)} %get-tuple-element.35.lo0, bf16[4,256,512]{2,1,0:T(8,128)(2,1)S(1)} %get-tuple-element.39.hi1, bf16[4,256,512]{2,1,0:T(8,128)(2,1)S(1)} %get-tuple-element.40.lo1, ...), custom_call_target="tpu_custom_call" | custom-call | tf_op jit(solution)/shard_map/pallas_call | solution.py:353
  36.5 20.4 %all_to_all.15.inc = f32[4,4,8,16,256]{4,3,2,1,0:T(8,128)S(1)} all-to-all(f32[4,4,8,16,256]{4,3,2,1,0:T(8,128)S(1)} %shard_map.72), channel_id=1, replica_groups={{0,1,2,3},{4,5,6,7},{8,9,10,11},{12,13,14,15},{16,20,24,28},{17,21,25,2..., dimensions={0} | all-to-all | bytes 4194304 | tf_op jit(solution)/shard_map/all_to_all | solution.py:291
  56.8 0.1 shard_map.73
  56.9 1.2 %collective-permute-start.7 = (f32[8,16,256]{2,1,0:T(8,128)S(1)}, f32[8,16,256]{2,1,0:T(8,128)S(1)}, u32[]{:S(2)}, u32[]{:S(2)}) collective-permute-start(f32[8,16,256]{2,1,0:T(8,128)S(1)} %get-tuple-element.44), channel_id=1, source_target_pairs={{0,4},{1,5},{2,6},{3,7},{4,8},{5,9},{6,10},{7,11},{8,12},{9,13},{1... | collective-permute-start | bytes 393224 | tf_op jit(solution)/shard_map/ppermute | solution.py:301
  58.1 2.5 %collective-permute-start.8 = (f32[8,16,256]{2,1,0:T(8,128)S(1)}, f32[8,16,256]{2,1,0:T(8,128)S(1)}, u32[]{:S(2)}, u32[]{:S(2)}) collective-permute-start(f32[8,16,256]{2,1,0:T(8,128)S(1)} %get-tuple-element.45), channel_id=1, source_target_pairs={{0,8},{1,9},{2,10},{3,11},{4,12},{5,13},{6,14},{7,15},{8,0},{9,1},... | collective-permute-start | bytes 393224 | tf_op jit(solution)/shard_map/ppermute | solution.py:301
  60.6 1.1 %collective-permute-start.9 = (f32[8,16,256]{2,1,0:T(8,128)S(1)}, f32[8,16,256]{2,1,0:T(8,128)S(1)}, u32[]{:S(2)}, u32[]{:S(2)}) collective-permute-start(f32[8,16,256]{2,1,0:T(8,128)S(1)} %get-tuple-element.46), channel_id=1, source_target_pairs={{0,12},{1,13},{2,14},{3,15},{4,0},{5,1},{6,2},{7,3},{8,4},{9,5},{1... | collective-permute-start | bytes 393224 | tf_op jit(solution)/shard_map/ppermute | solution.py:301
  61.7 0.4 collective-permute-done.7.refs_1_
  62.0 2.3 %collective-permute-done.8.refs_2_ = f32[8,16,256]{2,1,0:T(8,128)S(1)} collective-permute-done((f32[8,16,256]{2,1,0:T(8,128)S(1)}, f32[8,16,256]{2,1,0:T(8,128)S(1)}, u32[]{:S(2)}, u32[]{:S(2)}) %collective-permute-start.8) | collective-permute-done | bytes 131104 | tf_op jit(solution)/shard_map/ppermute | solution.py:301
  64.3 0.1 collective-permute-done.9.refs_3_
  64.4 1.0 shard_map.74
  65.4 0.0 copy-start
  65.4 0.1 collective-permute-start.10
  65.5 3.4 %collective-permute-start.11 = (f32[2,64,256]{2,1,0:T(8,128)S(1)}, f32[2,64,256]{2,1,0:T(8,128)S(1)}, u32[]{:S(2)}, u32[]{:S(2)}) collective-permute-start(f32[2,64,256]{2,1,0:T(8,128)S(1)} %get-tuple-element.49), channel_id=1, source_target_pairs={{0,64},{32,96},{64,0},{96,32},{1,65},{33,97},{65,1},{97,33},{2,66}... | collective-permute-start | bytes 393224 | tf_op jit(solution)/shard_map/ppermute | solution.py:309
  68.9 0.0 collective-permute-start.12
  68.9 4.2 %collective-permute-start.13 = (f32[2,64,256]{2,1,0:T(8,128)S(1)}, f32[2,64,256]{2,1,0:T(8,128)S(1)}, u32[]{:S(2)}, u32[]{:S(2)}) collective-permute-start(f32[2,64,256]{2,1,0:T(8,128)S(1)} %get-tuple-element.47.refs_0_), channel_id=1, source_target_pairs={{0,16},{16,0},{1,17},{17,1},{2,18},{18,2},{3,19},{19,3},{4,20},{20... | collective-permute-start | bytes 393224 | tf_op jit(solution)/shard_map/ppermute | solution.py:313
  73.1 0.0 collective-permute-done.10.refs_1_
  73.1 2.1 %collective-permute-start.14 = (f32[2,64,256]{2,1,0:T(8,128)S(1)}, f32[2,64,256]{2,1,0:T(8,128)S(1)}, u32[]{:S(2)}, u32[]{:S(2)}) collective-permute-start(f32[2,64,256]{2,1,0:T(8,128)S(1)} %collective-permute-done.10.refs_1_), channel_id=1, source_target_pairs={{0,16},{16,0},{1,17},{17,1},{2,18},{18,2},{3,19},{19,3},{4,20},{20... | collective-permute-start | bytes 393224 | tf_op jit(solution)/shard_map/ppermute | solution.py:313
  75.2 0.0 collective-permute-done.11.refs_2_
  75.2 2.3 %collective-permute-start.15 = (f32[2,64,256]{2,1,0:T(8,128)S(1)}, f32[2,64,256]{2,1,0:T(8,128)S(1)}, u32[]{:S(2)}, u32[]{:S(2)}) collective-permute-start(f32[2,64,256]{2,1,0:T(8,128)S(1)} %collective-permute-done.11.refs_2_), channel_id=1, source_target_pairs={{0,16},{16,0},{1,17},{17,1},{2,18},{18,2},{3,19},{19,3},{4,20},{20... | collective-permute-start | bytes 393224 | tf_op jit(solution)/shard_map/ppermute | solution.py:313
  77.4 0.0 collective-permute-done.12.refs_3_
  77.4 0.6 collective-permute-start.16
  78.1 0.0 collective-permute-done.13.refs_4_
  78.1 0.0 collective-permute-done.14.refs_5_
  78.1 0.4 collective-permute-done.15.refs_6_
  78.4 0.6 collective-permute-done.16.refs_7_
  79.1 0.6 shard_map.75
  79.7 0.7 collective-permute-start.17
  80.3 2.5 %collective-permute-start.18 = (f32[64,256]{1,0:T(8,128)S(1)}, f32[64,256]{1,0:T(8,128)S(1)}, u32[]{:S(2)}, u32[]{:S(2)}) collective-permute-start(f32[64,256]{1,0:T(8,128)S(1)} %get-tuple-element.53), channel_id=1, source_target_pairs={{0,8},{4,12},{8,0},{12,4},{1,9},{5,13},{9,1},{13,5},{2,10},{6,14},... | collective-permute-start | bytes 196616 | tf_op jit(solution)/shard_map/ppermute | solution.py:309
  82.9 0.6 collective-permute-start.19
  83.4 0.6 collective-permute-done.17.refs_1_
  84.1 1.8 %collective-permute-done.18.refs_2_ = f32[64,256]{1,0:T(8,128)S(1)} collective-permute-done((f32[64,256]{1,0:T(8,128)S(1)}, f32[64,256]{1,0:T(8,128)S(1)}, u32[]{:S(2)}, u32[]{:S(2)}) %collective-permute-start.18) | collective-permute-done | bytes 65568 | tf_op jit(solution)/shard_map/ppermute | solution.py:309
  85.8 0.9 collective-permute-done.19.refs_3_
  86.7 0.1 shard_map.76
  86.8 13.9 %all_to_all.16.inc = f32[16,32,256]{2,1,0:T(8,128)S(1)} all-to-all(f32[16,32,256]{2,1,0:T(8,128)S(1)} %shard_map.76), channel_id=1, replica_groups=mesh['y'=4,'core'=2,'z'=4,'x'=4] {'y','x'}, dimensions={0} | all-to-all | bytes 1048576 | tf_op jit(solution)/shard_map/all_to_all | solution.py:281
  100.7 2.4 %collective-permute-start.20 = (f32[4,32,256]{2,1,0:T(8,128)S(1)}, f32[4,32,256]{2,1,0:T(8,128)S(1)}, u32[]{:S(2)}, u32[]{:S(2)}) collective-permute-start(f32[4,32,256]{2,1,0:T(8,128)S(1)} %shard_map.77.own), channel_id=1, source_target_pairs={{0,16},{16,0},{1,17},{17,1},{2,18},{18,2},{3,19},{19,3},{4,20},{20... | collective-permute-start | bytes 393224 | tf_op jit(solution)/shard_map/ppermute | solution.py:313
  103.1 0.7 shard_map.78
  103.8 0.3 collective-permute-done.20.other
  104.1 0.0 copy-done
  104.1 0.9 shard_map.79
  (1 shorter events, 0.0 us)
Async XLA Ops:
  0.6 9.1 %copy-start.1 = (s32[2,32]{1,0:T(2,128)S(1)}, s32[2,32]{1,0:T(2,128)}, u32[]{:S(2)}) copy-start(s32[2,32]{1,0:T(2,128)} %fb.7) | copy-start | bytes 772
  0.6 9.1 %copy-start.2 = (s32[2,4]{1,0:T(2,128)S(1)}, s32[2,4]{1,0:T(2,128)}, u32[]{:S(2)}) copy-start(s32[2,4]{1,0:T(2,128)} %bounds.1) | copy-start | bytes 100
  3.8 18.3 %all-to-all-start = ((f32[8,96,256]{2,1,0:T(8,128)}), f32[8,96,256]{2,1,0:T(8,128)S(1)}, u32[]{:S(2)}, u32[]{:S(2)}) async-start(f32[8,96,256]{2,1,0:T(8,128)} %shard_map.69), calls=%async_computation | async-start | bytes 1572864 | tf_op jit(solution)/shard_map/all_to_all | solution.py:281
  22.6 6.4 %collective-permute-start.1 = (f32[4,32,256]{2,1,0:T(8,128)S(1)}, f32[4,32,256]{2,1,0:T(8,128)S(1)}, u32[]{:S(2)}, u32[]{:S(2)}) collective-permute-start(f32[4,32,256]{2,1,0:T(8,128)S(1)} %get-tuple-element.36.after.refs_0_), channel_id=1, source_target_pairs={{0,32},{32,64},{64,96},{96,0},{1,33},{33,65},{65,97},{97,1},{2,34}... | collective-permute-start | bytes 393224 | tf_op jit(solution)/shard_map/ppermute | solution.py:309
  23.0 6.0 %collective-permute-start = (f32[4,32,256]{2,1,0:T(8,128)S(1)}, f32[4,32,256]{2,1,0:T(8,128)S(1)}, u32[]{:S(2)}, u32[]{:S(2)}) collective-permute-start(f32[4,32,256]{2,1,0:T(8,128)S(1)} %get-tuple-element.36.after.refs_0_), channel_id=1, source_target_pairs={{0,96},{32,0},{64,32},{96,64},{1,97},{33,1},{65,33},{97,65},{2,98}... | collective-permute-start | bytes 393224 | tf_op jit(solution)/shard_map/ppermute | solution.py:309
  25.3 6.6 %collective-permute-start.2 = (f32[4,32,256]{2,1,0:T(8,128)S(1)}, f32[4,32,256]{2,1,0:T(8,128)S(1)}, u32[]{:S(2)}, u32[]{:S(2)}) collective-permute-start(f32[4,32,256]{2,1,0:T(8,128)S(1)} %get-tuple-element.36.after.refs_0_), channel_id=1, source_target_pairs={{0,64},{32,96},{64,0},{96,32},{1,65},{33,97},{65,1},{97,33},{2,66}... | collective-permute-start | bytes 393224 | tf_op jit(solution)/shard_map/ppermute | solution.py:309
  25.3 7.9 %collective-permute-start.3 = (f32[4,32,256]{2,1,0:T(8,128)S(1)}, f32[4,32,256]{2,1,0:T(8,128)S(1)}, u32[]{:S(2)}, u32[]{:S(2)}) collective-permute-start(f32[4,32,256]{2,1,0:T(8,128)S(1)} %get-tuple-element.36.after.refs_0_), channel_id=1, source_target_pairs={{0,16},{16,0},{1,17},{17,1},{2,18},{18,2},{3,19},{19,3},{4,20},{20... | collective-permute-start | bytes 393224 | tf_op jit(solution)/shard_map/ppermute | solution.py:313
  29.0 5.2 %collective-permute-start.6 = (f32[4,32,256]{2,1,0:T(8,128)S(1)}, f32[4,32,256]{2,1,0:T(8,128)S(1)}, u32[]{:S(2)}, u32[]{:S(2)}) collective-permute-start(f32[4,32,256]{2,1,0:T(8,128)S(1)} %collective-permute-done.refs_3_), channel_id=1, source_target_pairs={{0,16},{16,0},{1,17},{17,1},{2,18},{18,2},{3,19},{19,3},{4,20},{20... | collective-permute-start | bytes 393224 | tf_op jit(solution)/shard_map/ppermute | solution.py:313
  31.9 2.3 %collective-permute-start.4 = (f32[4,32,256]{2,1,0:T(8,128)S(1)}, f32[4,32,256]{2,1,0:T(8,128)S(1)}, u32[]{:S(2)}, u32[]{:S(2)}) collective-permute-start(f32[4,32,256]{2,1,0:T(8,128)S(1)} %collective-permute-done.2.refs_1_), channel_id=1, source_target_pairs={{0,16},{16,0},{1,17},{17,1},{2,18},{18,2},{3,19},{19,3},{4,20},{20... | collective-permute-start | bytes 393224 | tf_op jit(solution)/shard_map/ppermute | solution.py:313
  33.2 1.3 %collective-permute-start.5 = (f32[4,32,256]{2,1,0:T(8,128)S(1)}, f32[4,32,256]{2,1,0:T(8,128)S(1)}, u32[]{:S(2)}, u32[]{:S(2)}) collective-permute-start(f32[4,32,256]{2,1,0:T(8,128)S(1)} %collective-permute-done.1.refs_2_), channel_id=1, source_target_pairs={{0,16},{16,0},{1,17},{17,1},{2,18},{18,2},{3,19},{19,3},{4,20},{20... | collective-permute-start | bytes 393224 | tf_op jit(solution)/shard_map/ppermute | solution.py:313
  56.9 5.1 %collective-permute-start.7 = (f32[8,16,256]{2,1,0:T(8,128)S(1)}, f32[8,16,256]{2,1,0:T(8,128)S(1)}, u32[]{:S(2)}, u32[]{:S(2)}) collective-permute-start(f32[8,16,256]{2,1,0:T(8,128)S(1)} %get-tuple-element.44), channel_id=1, source_target_pairs={{0,4},{1,5},{2,6},{3,7},{4,8},{5,9},{6,10},{7,11},{8,12},{9,13},{1... | collective-permute-start | bytes 393224 | tf_op jit(solution)/shard_map/ppermute | solution.py:301
  58.1 6.2 %collective-permute-start.8 = (f32[8,16,256]{2,1,0:T(8,128)S(1)}, f32[8,16,256]{2,1,0:T(8,128)S(1)}, u32[]{:S(2)}, u32[]{:S(2)}) collective-permute-start(f32[8,16,256]{2,1,0:T(8,128)S(1)} %get-tuple-element.45), channel_id=1, source_target_pairs={{0,8},{1,9},{2,10},{3,11},{4,12},{5,13},{6,14},{7,15},{8,0},{9,1},... | collective-permute-start | bytes 393224 | tf_op jit(solution)/shard_map/ppermute | solution.py:301
  60.6 3.8 %collective-permute-start.9 = (f32[8,16,256]{2,1,0:T(8,128)S(1)}, f32[8,16,256]{2,1,0:T(8,128)S(1)}, u32[]{:S(2)}, u32[]{:S(2)}) collective-permute-start(f32[8,16,256]{2,1,0:T(8,128)S(1)} %get-tuple-element.46), channel_id=1, source_target_pairs={{0,12},{1,13},{2,14},{3,15},{4,0},{5,1},{6,2},{7,3},{8,4},{9,5},{1... | collective-permute-start | bytes 393224 | tf_op jit(solution)/shard_map/ppermute | solution.py:301
  65.4 38.7 %copy-start = (f32[2,256,256]{2,1,0:T(8,128)S(1)}, f32[2,256,256]{2,1,0:T(8,128)}, u32[]{:S(2)}) copy-start(f32[2,256,256]{2,1,0:T(8,128)} %terms.1) | copy-start | bytes 1572868
  65.4 7.7 %collective-permute-start.10 = (f32[2,64,256]{2,1,0:T(8,128)S(1)}, f32[2,64,256]{2,1,0:T(8,128)S(1)}, u32[]{:S(2)}, u32[]{:S(2)}) collective-permute-start(f32[2,64,256]{2,1,0:T(8,128)S(1)} %get-tuple-element.48), channel_id=1, source_target_pairs={{0,32},{32,64},{64,96},{96,0},{1,33},{33,65},{65,97},{97,1},{2,34}... | collective-permute-start | bytes 393224 | tf_op jit(solution)/shard_map/ppermute | solution.py:309
  65.5 9.7 %collective-permute-start.11 = (f32[2,64,256]{2,1,0:T(8,128)S(1)}, f32[2,64,256]{2,1,0:T(8,128)S(1)}, u32[]{:S(2)}, u32[]{:S(2)}) collective-permute-start(f32[2,64,256]{2,1,0:T(8,128)S(1)} %get-tuple-element.49), channel_id=1, source_target_pairs={{0,64},{32,96},{64,0},{96,32},{1,65},{33,97},{65,1},{97,33},{2,66}... | collective-permute-start | bytes 393224 | tf_op jit(solution)/shard_map/ppermute | solution.py:309
  68.9 8.6 %collective-permute-start.12 = (f32[2,64,256]{2,1,0:T(8,128)S(1)}, f32[2,64,256]{2,1,0:T(8,128)S(1)}, u32[]{:S(2)}, u32[]{:S(2)}) collective-permute-start(f32[2,64,256]{2,1,0:T(8,128)S(1)} %get-tuple-element.50), channel_id=1, source_target_pairs={{0,96},{32,0},{64,32},{96,64},{1,97},{33,1},{65,33},{97,65},{2,98}... | collective-permute-start | bytes 393224 | tf_op jit(solution)/shard_map/ppermute | solution.py:309
  68.9 9.2 %collective-permute-start.13 = (f32[2,64,256]{2,1,0:T(8,128)S(1)}, f32[2,64,256]{2,1,0:T(8,128)S(1)}, u32[]{:S(2)}, u32[]{:S(2)}) collective-permute-start(f32[2,64,256]{2,1,0:T(8,128)S(1)} %get-tuple-element.47.refs_0_), channel_id=1, source_target_pairs={{0,16},{16,0},{1,17},{17,1},{2,18},{18,2},{3,19},{19,3},{4,20},{20... | collective-permute-start | bytes 393224 | tf_op jit(solution)/shard_map/ppermute | solution.py:313
  73.1 5.0 %collective-permute-start.14 = (f32[2,64,256]{2,1,0:T(8,128)S(1)}, f32[2,64,256]{2,1,0:T(8,128)S(1)}, u32[]{:S(2)}, u32[]{:S(2)}) collective-permute-start(f32[2,64,256]{2,1,0:T(8,128)S(1)} %collective-permute-done.10.refs_1_), channel_id=1, source_target_pairs={{0,16},{16,0},{1,17},{17,1},{2,18},{18,2},{3,19},{19,3},{4,20},{20... | collective-permute-start | bytes 393224 | tf_op jit(solution)/shard_map/ppermute | solution.py:313
  75.2 3.2 %collective-permute-start.15 = (f32[2,64,256]{2,1,0:T(8,128)S(1)}, f32[2,64,256]{2,1,0:T(8,128)S(1)}, u32[]{:S(2)}, u32[]{:S(2)}) collective-permute-start(f32[2,64,256]{2,1,0:T(8,128)S(1)} %collective-permute-done.11.refs_2_), channel_id=1, source_target_pairs={{0,16},{16,0},{1,17},{17,1},{2,18},{18,2},{3,19},{19,3},{4,20},{20... | collective-permute-start | bytes 393224 | tf_op jit(solution)/shard_map/ppermute | solution.py:313
  77.4 1.6 %collective-permute-start.16 = (f32[2,64,256]{2,1,0:T(8,128)S(1)}, f32[2,64,256]{2,1,0:T(8,128)S(1)}, u32[]{:S(2)}, u32[]{:S(2)}) collective-permute-start(f32[2,64,256]{2,1,0:T(8,128)S(1)} %collective-permute-done.12.refs_3_), channel_id=1, source_target_pairs={{0,16},{16,0},{1,17},{17,1},{2,18},{18,2},{3,19},{19,3},{4,20},{20... | collective-permute-start | bytes 393224 | tf_op jit(solution)/shard_map/ppermute | solution.py:313
  79.7 4.4 %collective-permute-start.17 = (f32[64,256]{1,0:T(8,128)S(1)}, f32[64,256]{1,0:T(8,128)S(1)}, u32[]{:S(2)}, u32[]{:S(2)}) collective-permute-start(f32[64,256]{1,0:T(8,128)S(1)} %get-tuple-element.52), channel_id=1, source_target_pairs={{0,4},{4,8},{8,12},{12,0},{1,5},{5,9},{9,13},{13,1},{2,6},{6,10},{... | collective-permute-start | bytes 196616 | tf_op jit(solution)/shard_map/ppermute | solution.py:309
  80.3 5.5 %collective-permute-start.18 = (f32[64,256]{1,0:T(8,128)S(1)}, f32[64,256]{1,0:T(8,128)S(1)}, u32[]{:S(2)}, u32[]{:S(2)}) collective-permute-start(f32[64,256]{1,0:T(8,128)S(1)} %get-tuple-element.53), channel_id=1, source_target_pairs={{0,8},{4,12},{8,0},{12,4},{1,9},{5,13},{9,1},{13,5},{2,10},{6,14},... | collective-permute-start | bytes 196616 | tf_op jit(solution)/shard_map/ppermute | solution.py:309
  82.9 3.9 %collective-permute-start.19 = (f32[64,256]{1,0:T(8,128)S(1)}, f32[64,256]{1,0:T(8,128)S(1)}, u32[]{:S(2)}, u32[]{:S(2)}) collective-permute-start(f32[64,256]{1,0:T(8,128)S(1)} %get-tuple-element.54), channel_id=1, source_target_pairs={{0,12},{4,0},{8,4},{12,8},{1,13},{5,1},{9,5},{13,9},{2,14},{6,2},{... | collective-permute-start | bytes 196616 | tf_op jit(solution)/shard_map/ppermute | solution.py:309
  100.7 3.4 %collective-permute-start.20 = (f32[4,32,256]{2,1,0:T(8,128)S(1)}, f32[4,32,256]{2,1,0:T(8,128)S(1)}, u32[]{:S(2)}, u32[]{:S(2)}) collective-permute-start(f32[4,32,256]{2,1,0:T(8,128)S(1)} %shard_map.77.own), channel_id=1, source_target_pairs={{0,16},{16,0},{1,17},{17,1},{2,18},{18,2},{3,19},{19,3},{4,20},{20... | collective-permute-start | bytes 393224 | tf_op jit(solution)/shard_map/ppermute | solution.py:313
